TPU v7x, 512 devices: a whole 4x8x8 slice. The times are simulated.
512 devices in a mesh: frm: 32 (over y, z_lo), hgt: 4 (over x), wid: 4 (over z_hi, core).
Axes of the slice: x: 4, y: 8, z: 8 (z_hi: 2, z_lo: 4; z = z_hi * 4 + z_lo), core: 2. Of those that a mesh axis runs over, the one named last changes fastest.
Arguments:
- video: bfloat16 [1280, 1536, 512], P('frm', 'hgt', 'wid'), may hold values from -30 to 30
- height_factor: bfloat16 [1536, 256], P('hgt'), may hold values from -0.15625 to 0.15625
- width_factor: bfloat16 [512, 256], P('wid'), may hold values from -0.25 to 0.25
- start_basis: float32 [1280, 64], P('frm'), may hold values from -6 to 6
Outputs:
- gram: float32 [1280, 1280], P('frm', ('hgt', 'wid'))
- frame_factor: float32 [1280, 64], P('frm')
All inputs are finite; a program needn't handle non-finite values.
Results may differ from a plain program's by a relative error of at most 0.02.
Values may be sent and summed in bfloat16 or wider, within the bound.
No kernel may reach another device: no remote copies, remote signals or barrier semaphores. Data moves between devices by JAX's collectives and lax.ppermute only.
A program may use at most 64 MiB of HBM per device.

v0:
```python
import math

import jax
import jax.numpy as jnp
from jax import lax
from jax.experimental import pallas as pl
from jax.experimental.pallas import tpu as pltpu
from jax.sharding import Mesh, PartitionSpec as P

ITERS = 3
Z_HI = 2
CORES = 2
Z_LO = 4
N_X = 4
LANES = 128
PLANE = ("zh", "y", "zl")
DEEP = ("zh", "zl")
PIVOTS = 4
VMEM = pl.BlockSpec(memory_space=pltpu.VMEM)
SMEM = pl.BlockSpec(memory_space=pltpu.SMEM)
PARAMS = pltpu.CompilerParams(vmem_limit_bytes=40 << 20)
F32 = jnp.float32
HIGHEST = lax.Precision.HIGHEST


def shape(*dims, dtype=F32):
    return jax.ShapeDtypeStruct(dims, dtype)


def gram_kernel(scale, at, blocks, kept, sent, core, acc):
    _, total, depth = blocks.shape
    strip = kept.shape[1]
    for j in range(N_X):
        for x in range(N_X):
            for zh in range(Z_HI):
                for c in range(CORES):
                    source = ((x * Z_HI + zh) * CORES + c) * strip
                    place = ((zh * N_X + x) * CORES + c) * strip
                    core[place : place + strip, j * depth : (j + 1) * depth] = blocks[
                        j, source : source + strip, :
                    ]
    rows = []
    for zh in range(Z_HI):
        start = zh * (total // Z_HI) + at[0] * (CORES * strip)
        rows.append(core[pl.ds(pl.multiple_of(start, 32), CORES * strip), :])
    rows = jnp.concatenate(rows, axis=0)
    mine = at[1]
    wide = 2 * LANES
    for pair in range(total // wide):
        acc[...] = scale * lax.dot_general(
            rows,
            core[pair * wide : (pair + 1) * wide, :],
            (((1,), (1,)), ((), ())),
            preferred_element_type=F32,
        )
        for side in range(2):
            tile = 2 * pair + side
            lanes = slice(side * LANES, (side + 1) * LANES)
            for zh in range(Z_HI):
                base = zh * CORES * strip
                keep_at = pl.multiple_of(base + mine * strip, 8)
                send_at = pl.multiple_of(base + (1 - mine) * strip, 8)
                kept[tile * Z_HI + zh] = acc[pl.ds(keep_at, strip), lanes]
                sent[tile * Z_HI + zh] = acc[pl.ds(send_at, strip), lanes]


def cut_kernel(a, b, out_a, out_b):
    start = 0
    for out in (out_a, out_b):
        pieces, rows, _ = out.shape
        for j in range(pieces):
            out[j] = a[start : start + rows, :] + b[start : start + rows, :]
            start += rows


def sum_kernel(in_a, in_b, out_a, out_b):
    for parts, out in ((in_a, out_a), (in_b, out_b)):
        total = parts[0]
        for j in range(1, parts.shape[0]):
            total = total + parts[j]
        for j in range(out.shape[0]):
            out[j] = total


def put_product(gram, basis, out):
    half = basis.shape[0]
    rank = basis.shape[1] // Z_HI
    low = jnp.dot(gram[:, :half], basis, precision=HIGHEST, preferred_element_type=F32)
    high = jnp.dot(gram[:, half:], basis, precision=HIGHEST, preferred_element_type=F32)
    product = low[:, :rank] + high[:, rank:]
    strip = product.shape[0] // Z_HI
    packed = jnp.concatenate([product[:strip], product[strip:]], axis=1)
    for j in range(out.shape[0]):
        out[j] = packed


def first_kernel(in_a, in_b, basis, gram, out):
    mine, total = gram.shape
    cut = in_a.shape[0]
    for t in range(total // LANES):
        lanes = slice(t * LANES, (t + 1) * LANES)
        low, high = t * mine, (t + 1) * mine
        if low < cut:
            end = min(high, cut)
            gram[: end - low, lanes] = in_a[low:end, :]
        if high > cut:
            begin = max(low, cut)
            gram[begin - low :, lanes] = in_b[begin - cut : high - cut, :]
    put_product(gram[...], basis[...], out)


def inverse_factor(small):
    n = small.shape[0]
    group = 8
    row_id = lax.broadcasted_iota(jnp.int32, (n, n), 0)
    col_id = lax.broadcasted_iota(jnp.int32, (n, n), 1)
    whole = jnp.concatenate([small, (row_id == col_id).astype(F32)], axis=1)
    blocks = [whole[g * group : (g + 1) * group] for g in range(n // group)]
    sub = lax.broadcasted_iota(jnp.int32, (group, 1), 0)
    done = []
    for k in range(0, n, PIVOTS):
        g, i = divmod(k, group)
        live = blocks[g:]
        cols = [
            [jnp.broadcast_to(b[:, k + m : k + m + 1], b.shape) for b in live] for m in range(PIVOTS)
        ]
        rows = [blocks[g][i + m : i + m + 1, :] for m in range(PIVOTS)]
        corner = [[cols[m][0][i + r : i + r + 1, :] for m in range(PIVOTS)] for r in range(PIVOTS)]
        for m in range(PIVOTS):
            inverse = 1.0 / corner[m][m]
            cols[m] = [c * inverse for c in cols[m]]
            for r in range(m + 1, PIVOTS):
                factor = corner[r][m] * inverse
                rows[r] = rows[r] - factor * rows[m]
                for q in range(m + 1, PIVOTS):
                    corner[r][q] = corner[r][q] - factor * corner[m][q]
                cols[r] = [c - w * corner[m][r] for c, w in zip(cols[r], cols[m])]
            done.append(rows[m] * lax.rsqrt(corner[m][m]))
        for at, block in enumerate(live):
            new = block
            for m in range(PIVOTS):
                new = new - cols[m][at] * rows[m]
            if at == 0:
                new = jnp.where(sub >= i + PIVOTS, new, block)
            blocks[g + at] = new
    return jnp.concatenate(done, axis=0)[:, n:]


def factor_of(packed):
    both = lax.dot_general(
        packed, packed, (((0,), (0,)), ((), ())), precision=HIGHEST, preferred_element_type=F32
    )
    rank = both.shape[0] // Z_HI
    inverse = inverse_factor(both[:rank, :rank] + both[rank:, rank:])
    zero = jnp.zeros_like(inverse)
    return jnp.concatenate(
        [jnp.concatenate([inverse, zero], axis=1), jnp.concatenate([zero, inverse], axis=1)], axis=0
    )


def apply_factor(rows, inverse):
    return lax.dot_general(
        rows, inverse, (((1,), (1,)), ((), ())), precision=HIGHEST, preferred_element_type=F32
    )


def step_kernel(packed, gram, out):
    product = packed[...]
    basis = apply_factor(product, factor_of(product))
    put_product(gram[...], basis, out)


def last_kernel(at, packed, out):
    frames, rank = out.shape
    inverse = factor_of(packed[...])
    rows = packed[pl.ds(pl.multiple_of(at[3], 8), frames), :]
    rows = apply_factor(rows, inverse) * math.sqrt(Z_HI * packed.shape[0])
    out[...] = jnp.where(at[2] == 0, rows[:, :rank], rows[:, rank:])


def call(kernel, outs, ins, args, scratch=()):
    return pl.pallas_call(
        kernel,
        out_shape=outs,
        in_specs=ins,
        out_specs=jax.tree.map(lambda _: VMEM, outs),
        scratch_shapes=list(scratch),
        compiler_params=PARAMS,
    )(*args)


def spread(x, axes):
    copies = jnp.broadcast_to(x[None], (lax.axis_size(axes),) + x.shape)
    return lax.all_to_all(copies, axes, 0, 0, tiled=True)


def swap(x, axis):
    return lax.ppermute(x, axis, [(0, 1), (1, 0)])


def local(video, height_factor, width_factor, start_basis):
    rank_h = height_factor.shape[1]
    rank_w = width_factor.shape[1]
    rank_f = start_basis.shape[1]
    frames_dev, _, cols = video.shape
    frm = lax.axis_index(("y", "zl"))
    frm_count = lax.axis_size(("y", "zl"))
    total = frames_dev * frm_count
    x_at, zh_at, core_at = lax.axis_index("x"), lax.axis_index("zh"), lax.axis_index("c")
    first = core_at == 0
    strip = total // (N_X * Z_HI * CORES)
    frame = frm * frames_dev
    frame_zh = frame // (CORES * strip) % Z_HI
    frame_row = (frame // (Z_HI * CORES * strip) * CORES + frame // strip % CORES) * strip + frame % strip
    at = jnp.stack([x_at, core_at, frame_zh, frame_row]).astype(jnp.int32)

    mid = jnp.einsum(
        "fhw,hr->rfw", video, height_factor, preferred_element_type=F32
    ).astype(jnp.bfloat16)
    mid, width, start = lax.optimization_barrier((mid, width_factor, start_basis))
    mid = lax.psum_scatter(mid, "x", scatter_dimension=0, tiled=True)
    width_other = swap(width, "zh")
    basis = spread(start, ("y", "zl")).reshape(N_X, Z_HI, CORES, strip, rank_f)
    basis = basis.transpose(0, 2, 3, 1, 4).reshape(total // Z_HI, Z_HI * rank_f)
    mid, width_other, basis = lax.optimization_barrier((mid, width_other, basis))

    mid = lax.all_to_all(mid, PLANE, 0, 0, tiled=True).reshape(Z_HI, total, cols)
    low_width = jnp.where(zh_at == 0, width, width_other)
    high_width = jnp.where(zh_at == 0, width_other, width)
    part = jnp.dot(mid[0], low_width, preferred_element_type=F32) + jnp.dot(
        mid[1], high_width, preferred_element_type=F32
    )
    half = rank_w // CORES
    low, high = part[:, :half], part[:, half:]
    came = swap(jnp.where(first, high, low).astype(jnp.bfloat16), "c")
    own = jnp.where(first, low, high).astype(jnp.bfloat16)
    core = (own.astype(F32) + came.astype(F32)).astype(jnp.bfloat16)

    blocks = spread(core, "x")
    mine = Z_HI * strip
    tiles = total // LANES
    kept, sent = call(
        lambda *refs: gram_kernel(1.0 / (rank_h * rank_w), *refs),
        [shape(tiles * Z_HI, strip, LANES)] * 2,
        [SMEM, VMEM],
        (at, blocks),
        [
            pltpu.VMEM((total, N_X * half), jnp.bfloat16),
            pltpu.VMEM((total // N_X, 2 * LANES), F32),
        ],
    )
    came = swap(sent, "c")

    flat = tiles * mine
    ring = lax.axis_size("y")
    rows_a = -(-flat // (2 * 8 * ring)) * 8
    rows_b = flat // ring - rows_a
    part_a, part_b = shape(ring, rows_a, LANES), shape(ring, rows_b, LANES)
    sides = call(
        cut_kernel,
        [part_a, part_b],
        [VMEM] * 2,
        (kept.reshape(flat, LANES), came.reshape(flat, LANES)),
    )
    axes = (DEEP, "y")
    sides = [lax.all_to_all(x, axes[i], 0, 0, tiled=True) for i, x in enumerate(sides)]
    sides = call(sum_kernel, [part_a, part_b], [VMEM] * 2, sides)
    sides = [lax.all_to_all(x, axes[1 - i], 0, 0, tiled=True) for i, x in enumerate(sides)]
    sides = call(sum_kernel, [part_a, part_b], [VMEM] * 2, sides)
    sides = [lax.all_to_all(x, axes[i], 0, 0, tiled=True) for i, x in enumerate(sides)]

    packed_shape = shape(N_X * CORES, strip, Z_HI * rank_f)
    gram, packed = call(
        first_kernel,
        [shape(mine, total), packed_shape],
        [VMEM] * 3,
        [x.reshape(-1, LANES) for x in sides] + [basis],
    )
    for step in range(ITERS):
        packed = lax.all_to_all(packed, ("x", "c"), 0, 0, tiled=True)
        packed = packed.reshape(total // Z_HI, Z_HI * rank_f)
        if step < ITERS - 1:
            packed = call(step_kernel, packed_shape, [VMEM] * 2, (packed, gram))
    factor = call(last_kernel, shape(frames_dev, rank_f), [SMEM, VMEM], (at, packed))
    strip_rows = lax.dynamic_slice_in_dim(gram, zh_at * strip, strip, 0)
    column = frame_zh * (total // Z_HI) + frame_row
    gram_out = lax.dynamic_slice_in_dim(strip_rows.T, column, frames_dev, 0)
    return (gram_out, factor)


def solution(mesh):
    frm, hgt, _ = mesh.devices.shape
    fine = Mesh(
        mesh.devices.reshape(frm // Z_LO, Z_LO, hgt, Z_HI, CORES), ("y", "zl", "x", "zh", "c")
    )
    frm, hgt, wid = ("y", "zl"), "x", ("zh", "c")
    return jax.shard_map(
        local,
        mesh=fine,
        in_specs=(P(frm, hgt, wid), P(hgt, None), P(wid, None), P(frm, None)),
        out_specs=(P(frm, ("x", "zh", "c")), P(frm, None)),
        check_vma=False,
    )
```

profile of v0, /device:TPU:1, one launch (start us, length us, event | category | flops | bytes accessed | tf_op | source)
XLA Modules:
  0.0 284.7 jit_solution(11715032645383099489)
XLA Ops:
  8.1 5.2 %convolution_convert_fusion = bf16[256,40,128]{2,0,1:T(8,128)(2,1)} fusion(bf16[40,384,128]{2,1,0:T(8,128)(2,1)} %param.4, bf16[384,256]{1,0:T(8,128)(2,1)S(1)} %copy-done), kind=kOutput, calls=%fused_computation.1 | convolution fusion | flops 1007943680 | bytes 6750208 | tf_op jit(solution)/shard_map/fhw,hr->rfw/dot_general | solution.py:217
  14.0 1.1 reshape.48
  15.2 13.5 %all-to-all-start = ((f32[32,1,2560]{2,1,0:T(1,128)}), f32[32,1,2560]{2,1,0:T(1,128)S(1)}, u32[]{:S(2)}, u32[]{:S(2)}) async-start(f32[32,1,2560]{2,1,0:T(1,128)} %reshape.48), calls=%async_computation.1 | async-start | bytes 655360 | tf_op jit(solution)/shard_map/all_to_all | solution.py:194
  28.6 7.9 %collective-permute-start = (bf16[128,256]{1,0:T(8,128)(2,1)S(1)}, bf16[128,256]{1,0:T(8,128)(2,1)S(1)}, u32[]{:S(2)}, u32[]{:S(2)}) collective-permute-start(bf16[128,256]{1,0:T(8,128)(2,1)S(1)} %copy-done.1), channel_id=1, source_target_pairs={{0,2},{2,0},{1,3},{3,1},{4,6},{6,4},{5,7},{7,5},{8,10},{10,8},{9,1... | collective-permute-start | bytes 196616 | tf_op jit(solution)/shard_map/ppermute | solution.py:198
  36.6 5.4 %all-to-all-done = f32[32,1,2560]{2,1,0:T(1,128)S(1)} async-done(((f32[32,1,2560]{2,1,0:T(1,128)}), f32[32,1,2560]{2,1,0:T(1,128)S(1)}, u32[]{:S(2)}, u32[]{:S(2)}) %all-to-all-start) | async-done | bytes 327712 | tf_op jit(solution)/shard_map/all_to_all | solution.py:194
  42.5 1.4 reduce
  45.1 13.2 %reduce-scatter.2.cloned.1.call-done = bf16[64,40,128]{2,0,1:T(8,128)(2,1)} async-done(((bf16[256,40,128]{2,0,1:T(8,128)(2,1)}), bf16[64,40,128]{2,0,1:T(8,128)(2,1)}) %reduce-scatter.2.cloned.1.call-update) | async-done | bytes 655376 | tf_op jit(solution)/shard_map/reduce_scatter | solution.py:221
  58.3 2.4 copy.16
  60.6 13.0 %all-to-all-start.1 = ((bf16[64,40,128]{2,1,0:T(8,128)(2,1)}), bf16[64,40,128]{2,1,0:T(8,128)(2,1)S(1)}, u32[]{:S(2)}, u32[]{:S(2)}) async-start(bf16[64,40,128]{2,1,0:T(8,128)(2,1)} %copy.16), calls=%async_computation.2 | async-start | bytes 1310720 | tf_op jit(solution)/shard_map/all_to_all | solution.py:227
  73.6 19.9 %all-to-all-done.1 = bf16[64,40,128]{2,1,0:T(8,128)(2,1)S(1)} async-done(((bf16[64,40,128]{2,1,0:T(8,128)(2,1)}), bf16[64,40,128]{2,1,0:T(8,128)(2,1)S(1)}, u32[]{:S(2)}, u32[]{:S(2)}) %all-to-all-start.1) | async-done | bytes 655392 | tf_op jit(solution)/shard_map/all_to_all | solution.py:227
  94.3 4.7 %collective-permute-start.1 = (bf16[1280,128]{1,0:T(8,128)(2,1)S(1)}, bf16[1280,128]{1,0:T(8,128)(2,1)S(1)}, u32[]{:S(2)}, u32[]{:S(2)}) collective-permute-start(bf16[1280,128]{1,0:T(8,128)(2,1)S(1)} %select_convert_fusion), channel_id=1, source_target_pairs={{0,1},{1,0},{2,3},{3,2},{4,5},{5,4},{6,7},{7,6},{8,9},{9,8},{10,11... | collective-permute-start | bytes 983048 | tf_op jit(solution)/shard_map/ppermute | solution.py:198
  99.0 1.2 collective-permute-done.1
  100.3 1.3 broadcast_in_dim.5
  101.6 3.5 %all-to-all-start.2 = ((bf16[4,1280,128]{2,1,0:T(8,128)(2,1)}), bf16[4,1280,128]{2,1,0:T(8,128)(2,1)S(1)}, u32[]{:S(2)}, u32[]{:S(2)}) async-start(bf16[4,1280,128]{2,1,0:T(8,128)(2,1)} %broadcast_in_dim.5), calls=%async_computation.3 | async-start | bytes 2621440 | tf_op jit(solution)/shard_map/all_to_all | solution.py:194
  105.3 17.4 %all-to-all-done.2.refs_1_ = bf16[4,1280,128]{2,1,0:T(8,128)(2,1)S(1)} async-done(((bf16[4,1280,128]{2,1,0:T(8,128)(2,1)}), bf16[4,1280,128]{2,1,0:T(8,128)(2,1)S(1)}, u32[]{:S(2)}, u32[]{:S(2)}) %all-to-all-start.2) | async-done | bytes 1310752 | tf_op jit(solution)/shard_map/all_to_all | solution.py:194
  122.7 1.5 shard_map.59
  124.2 3.1 %collective-permute-start.2 = (f32[20,80,128]{2,1,0:T(8,128)S(1)}, f32[20,80,128]{2,1,0:T(8,128)S(1)}, u32[]{:S(2)}, u32[]{:S(2)}) collective-permute-start(f32[20,80,128]{2,1,0:T(8,128)S(1)} %get-tuple-element.24), channel_id=1, source_target_pairs={{0,1},{1,0},{2,3},{3,2},{4,5},{5,4},{6,7},{7,6},{8,9},{9,8},{10,11... | collective-permute-start | bytes 2457608 | tf_op jit(solution)/shard_map/ppermute | solution.py:198
  127.3 1.9 collective-permute-done.2
  129.4 18.1 %all_to_all.60.in_b = f32[8,96,128]{2,1,0:T(8,128)S(1)} all-to-all(f32[8,96,128]{2,1,0:T(8,128)S(1)} %get-tuple-element.26), channel_id=1, replica_groups=mesh['y'=8,'zl'=4,'x'=4,'zh'=2,'c'=2] {'y'}, dimensions={0} | all-to-all | bytes 786432 | tf_op jit(solution)/shard_map/all_to_all | solution.py:266
  147.5 18.0 %all_to_all.61.in_a = f32[8,104,128]{2,1,0:T(8,128)S(1)} all-to-all(f32[8,104,128]{2,1,0:T(8,128)S(1)} %get-tuple-element.25), channel_id=1, replica_groups=mesh['y'=8,'zl'=4,'x'=4,'zh'=2,'c'=2] {'zh','zl'}, dimensions={0} | all-to-all | bytes 851968 | tf_op jit(solution)/shard_map/all_to_all | solution.py:266
  165.5 14.4 %all_to_all.62.in_b = f32[8,96,128]{2,1,0:T(8,128)S(1)} all-to-all(f32[8,96,128]{2,1,0:T(8,128)S(1)} %get-tuple-element.28), channel_id=1, replica_groups=mesh['y'=8,'zl'=4,'x'=4,'zh'=2,'c'=2] {'zh','zl'}, dimensions={0} | all-to-all | bytes 786432 | tf_op jit(solution)/shard_map/all_to_all | solution.py:268
  180.0 13.7 %all_to_all.63.in_a = f32[8,104,128]{2,1,0:T(8,128)S(1)} all-to-all(f32[8,104,128]{2,1,0:T(8,128)S(1)} %get-tuple-element.27), channel_id=1, replica_groups=mesh['y'=8,'zl'=4,'x'=4,'zh'=2,'c'=2] {'y'}, dimensions={0} | all-to-all | bytes 851968 | tf_op jit(solution)/shard_map/all_to_all | solution.py:268
  194.5 14.0 %all_to_all.64 = f32[8,96,128]{2,1,0:T(8,128)S(1)} all-to-all(f32[8,96,128]{2,1,0:T(8,128)S(1)} %get-tuple-element.30), channel_id=1, replica_groups=mesh['y'=8,'zl'=4,'x'=4,'zh'=2,'c'=2] {'y'}, dimensions={0} | all-to-all | bytes 786432 | tf_op jit(solution)/shard_map/all_to_all | solution.py:270
  208.5 6.4 %all-to-all-start.7 = ((f32[8,104,128]{2,1,0:T(8,128)}), f32[8,104,128]{2,1,0:T(8,128)S(1)}, u32[]{:S(2)}, u32[]{:S(2)}) async-start(f32[8,104,128]{2,1,0:T(8,128)} %get-tuple-element.29), calls=%async_computation.8 | async-start | bytes 851968 | tf_op jit(solution)/shard_map/all_to_all | solution.py:270
  215.0 11.0 %all-to-all-done.7 = f32[8,104,128]{2,1,0:T(8,128)S(1)} async-done(((f32[8,104,128]{2,1,0:T(8,128)}), f32[8,104,128]{2,1,0:T(8,128)S(1)}, u32[]{:S(2)}, u32[]{:S(2)}) %all-to-all-start.7) | async-done | bytes 426016 | tf_op jit(solution)/shard_map/all_to_all | solution.py:270
  227.0 15.3 %all_to_all.65 = f32[8,80,128]{2,1,0:T(8,128)S(1)} all-to-all(f32[8,80,128]{2,1,0:T(8,128)S(1)} %get-tuple-element.33), channel_id=1, replica_groups=mesh['y'=8,'zl'=4,'x'=4,'zh'=2,'c'=2] {'x','c'}, dimensions={0} | all-to-all | bytes 655360 | tf_op jit(solution)/shard_map/all_to_all | solution.py:280
  242.3 4.4 %shard_map.64 = f32[8,80,128]{2,1,0:T(8,128)S(1)} custom-call(f32[640,128]{1,0:T(8,128)S(1)} %bitcast.29, f32[160,1280]{1,0:T(8,128)S(1)} %get-tuple-element.32.gram), custom_call_target="tpu_custom_call" | custom-call | tf_op jit(solution)/shard_map/pallas_call | solution.py:182
  246.7 10.6 %all_to_all.66 = f32[8,80,128]{2,1,0:T(8,128)S(1)} all-to-all(f32[8,80,128]{2,1,0:T(8,128)S(1)} %shard_map.64), channel_id=1, replica_groups=mesh['y'=8,'zl'=4,'x'=4,'zh'=2,'c'=2] {'x','c'}, dimensions={0} | all-to-all | bytes 655360 | tf_op jit(solution)/shard_map/all_to_all | solution.py:280
  257.3 5.1 %shard_map.65 = f32[8,80,128]{2,1,0:T(8,128)} custom-call(f32[640,128]{1,0:T(8,128)S(1)} %bitcast.30, f32[160,1280]{1,0:T(8,128)S(1)} %get-tuple-element.32.gram), custom_call_target="tpu_custom_call" | custom-call | tf_op jit(solution)/shard_map/pallas_call | solution.py:182
  262.4 4.1 %all-to-all-start.11 = ((f32[8,80,128]{2,1,0:T(8,128)}), f32[8,80,128]{2,1,0:T(8,128)S(1)}, u32[]{:S(2)}, u32[]{:S(2)}) async-start(f32[8,80,128]{2,1,0:T(8,128)} %shard_map.65), calls=%async_computation.12 | async-start | bytes 655360 | tf_op jit(solution)/shard_map/all_to_all | solution.py:280
  267.2 6.4 %all-to-all-done.11 = f32[8,80,128]{2,1,0:T(8,128)S(1)} async-done(((f32[8,80,128]{2,1,0:T(8,128)}), f32[8,80,128]{2,1,0:T(8,128)S(1)}, u32[]{:S(2)}, u32[]{:S(2)}) %all-to-all-start.11) | async-done | bytes 327712 | tf_op jit(solution)/shard_map/all_to_all | solution.py:280
  273.6 4.2 %shard_map.66 = f32[40,64]{1,0:T(8,128)} custom-call(s32[4]{0:T(128)S(1)} %pad_add_fusion.refs_0_.at, f32[640,128]{1,0:T(8,128)S(1)} %bitcast.28), custom_call_target="tpu_custom_call" | custom-call | tf_op jit(solution)/shard_map/pallas_call | solution.py:182
  (27 shorter events, 7.2 us)
Async XLA Ops:
  7.2 0.9 copy-start
  7.2 51.1 %reduce-scatter.2.cloned.1.call-start = ((), (), s32[]{:S(2)}) async-start(), calls=%async_computation.13 | async-start | bytes 3276800 | tf_op jit(solution)/shard_map/reduce_scatter | solution.py:221
  13.3 0.7 copy-start.2
  13.3 15.4 %copy-start.1 = (bf16[128,256]{1,0:T(8,128)(2,1)S(1)}, bf16[128,256]{1,0:T(8,128)(2,1)}, u32[]{:S(2)}) copy-start(bf16[128,256]{1,0:T(8,128)(2,1)} %param.6) | copy-start | bytes 196612
  15.2 26.8 %all-to-all-start = ((f32[32,1,2560]{2,1,0:T(1,128)}), f32[32,1,2560]{2,1,0:T(1,128)S(1)}, u32[]{:S(2)}, u32[]{:S(2)}) async-start(f32[32,1,2560]{2,1,0:T(1,128)} %reshape.48), calls=%async_computation.1 | async-start | bytes 655360 | tf_op jit(solution)/shard_map/all_to_all | solution.py:194
  28.6 16.4 %collective-permute-start = (bf16[128,256]{1,0:T(8,128)(2,1)S(1)}, bf16[128,256]{1,0:T(8,128)(2,1)S(1)}, u32[]{:S(2)}, u32[]{:S(2)}) collective-permute-start(bf16[128,256]{1,0:T(8,128)(2,1)S(1)} %copy-done.1), channel_id=1, source_target_pairs={{0,2},{2,0},{1,3},{3,1},{4,6},{6,4},{5,7},{7,5},{8,10},{10,8},{9,1... | collective-permute-start | bytes 196616 | tf_op jit(solution)/shard_map/ppermute | solution.py:198
  60.6 32.9 %all-to-all-start.1 = ((bf16[64,40,128]{2,1,0:T(8,128)(2,1)}), bf16[64,40,128]{2,1,0:T(8,128)(2,1)S(1)}, u32[]{:S(2)}, u32[]{:S(2)}) async-start(bf16[64,40,128]{2,1,0:T(8,128)(2,1)} %copy.16), calls=%async_computation.2 | async-start | bytes 1310720 | tf_op jit(solution)/shard_map/all_to_all | solution.py:227
  94.3 5.9 %collective-permute-start.1 = (bf16[1280,128]{1,0:T(8,128)(2,1)S(1)}, bf16[1280,128]{1,0:T(8,128)(2,1)S(1)}, u32[]{:S(2)}, u32[]{:S(2)}) collective-permute-start(bf16[1280,128]{1,0:T(8,128)(2,1)S(1)} %select_convert_fusion), channel_id=1, source_target_pairs={{0,1},{1,0},{2,3},{3,2},{4,5},{5,4},{6,7},{7,6},{8,9},{9,8},{10,11... | collective-permute-start | bytes 983048 | tf_op jit(solution)/shard_map/ppermute | solution.py:198
  101.6 21.2 %all-to-all-start.2 = ((bf16[4,1280,128]{2,1,0:T(8,128)(2,1)}), bf16[4,1280,128]{2,1,0:T(8,128)(2,1)S(1)}, u32[]{:S(2)}, u32[]{:S(2)}) async-start(bf16[4,1280,128]{2,1,0:T(8,128)(2,1)} %broadcast_in_dim.5), calls=%async_computation.3 | async-start | bytes 2621440 | tf_op jit(solution)/shard_map/all_to_all | solution.py:194
  124.2 5.1 %collective-permute-start.2 = (f32[20,80,128]{2,1,0:T(8,128)S(1)}, f32[20,80,128]{2,1,0:T(8,128)S(1)}, u32[]{:S(2)}, u32[]{:S(2)}) collective-permute-start(f32[20,80,128]{2,1,0:T(8,128)S(1)} %get-tuple-element.24), channel_id=1, source_target_pairs={{0,1},{1,0},{2,3},{3,2},{4,5},{5,4},{6,7},{7,6},{8,9},{9,8},{10,11... | collective-permute-start | bytes 2457608 | tf_op jit(solution)/shard_map/ppermute | solution.py:198
  208.5 17.5 %all-to-all-start.7 = ((f32[8,104,128]{2,1,0:T(8,128)}), f32[8,104,128]{2,1,0:T(8,128)S(1)}, u32[]{:S(2)}, u32[]{:S(2)}) async-start(f32[8,104,128]{2,1,0:T(8,128)} %get-tuple-element.29), calls=%async_computation.8 | async-start | bytes 851968 | tf_op jit(solution)/shard_map/all_to_all | solution.py:270
  262.4 11.2 %all-to-all-start.11 = ((f32[8,80,128]{2,1,0:T(8,128)}), f32[8,80,128]{2,1,0:T(8,128)S(1)}, u32[]{:S(2)}, u32[]{:S(2)}) async-start(f32[8,80,128]{2,1,0:T(8,128)} %shard_map.65), calls=%async_computation.12 | async-start | bytes 655360 | tf_op jit(solution)/shard_map/all_to_all | solution.py:280
Sparse Core Ops, SparseCore 0:
  13.4 44.8 reduce-scatter.1
where the time goes:
time: 286 us; the launch traced here: 285 us
  blocking collectives  104 us (36%)
  waiting for transfers between devices  76.5 us (27%)
  starting transfers between devices  56.2 us (20%)
  Pallas kernels  17.1 us (6%)
  between operations  14.3 us (5%)
  local copies, waits for them, and re-layouts  9.02 us (3%)
  matrix products  5.79 us (2%)
    all_to_all x3, blocking collectives, local(): lax.all_to_all(x, axes[i], 0, 0, tiled=True)  50.1 us
    all_to_all x2, blocking collectives, local(): lax.all_to_all(x, axes[1 - i], 0, 0, tiled=True)  28.1 us
    all_to_all x2, blocking collectives, local(): packed = lax.all_to_all(packed, ('x', 'c'), 0, 0, tiled=True)  25.9 us
    all_to_all x2, waiting for transfers between devices, spread(): return lax.all_to_all(copies, axes, 0, 0, tiled=True)  22.8 us
    all_to_all x1, waiting for transfers between devices, local(): lax.all_to_all(mid, PLANE, 0, 0, tiled=True).reshape(Z_HI, total, cols)  19.9 us
    pallas_call x8, Pallas kernels, call(): pl.pallas_call(kernel, out_shape=outs, in_specs=ins, out_specs=jax.tree.m...  17.1 us
    all_to_all x2, starting transfers between devices, spread(): return lax.all_to_all(copies, axes, 0, 0, tiled=True)  17 us
    ppermute x3, starting transfers between devices, swap(): return lax.ppermute(x, axis, [(0, 1), (1, 0)])  15.7 us
  transfers between devices with their start and end apart: 9, of which 8 were waited for; matrix products, arithmetic and copies ran while one was open for 2% of the time, Pallas kernels for 0%

commit v1 on v0

--- a/solution.py
+++ b/solution.py
@@ -14,7 +14,6 @@
 N_X = 4
 LANES = 128
 PLANE = ("zh", "y", "zl")
-DEEP = ("zh", "zl")
 PIVOTS = 4
 VMEM = pl.BlockSpec(memory_space=pltpu.VMEM)
 SMEM = pl.BlockSpec(memory_space=pltpu.SMEM)
@@ -64,22 +63,21 @@
                 sent[tile * Z_HI + zh] = acc[pl.ds(send_at, strip), lanes]
 
 
-def cut_kernel(a, b, out_a, out_b):
-    start = 0
-    for out in (out_a, out_b):
-        pieces, rows, _ = out.shape
-        for j in range(pieces):
-            out[j] = a[start : start + rows, :] + b[start : start + rows, :]
-            start += rows
-
-
-def sum_kernel(in_a, in_b, out_a, out_b):
-    for parts, out in ((in_a, out_a), (in_b, out_b)):
-        total = parts[0]
-        for j in range(1, parts.shape[0]):
-            total = total + parts[j]
-        for j in range(out.shape[0]):
-            out[j] = total
+def pack_kernel(a, b, out):
+    pieces, rows, _ = out.shape
+    for j in range(pieces):
+        out[j] = a[j * rows : (j + 1) * rows, :] + b[j * rows : (j + 1) * rows, :]
+
+
+def sum_kernel(parts, start, out):
+    count, rows, _ = parts.shape
+    total = parts[0]
+    for j in range(1, count):
+        total = total + parts[j]
+    share = start.shape[0]
+    for j in range(count):
+        out[j, 0:rows, :] = total
+        out[j, rows : rows + share, :] = start[...]
 
 
 def put_product(gram, basis, out):
@@ -94,18 +92,26 @@
         out[j] = packed
 
 
-def first_kernel(in_a, in_b, basis, gram, out):
+def first_kernel(rows, pieces, gram, out, flat, basis):
+    count, _, _ = pieces.shape
+    for j in range(count):
+        flat[j * rows : (j + 1) * rows, :] = pieces[j, 0:rows, :]
     mine, total = gram.shape
-    cut = in_a.shape[0]
     for t in range(total // LANES):
-        lanes = slice(t * LANES, (t + 1) * LANES)
-        low, high = t * mine, (t + 1) * mine
-        if low < cut:
-            end = min(high, cut)
-            gram[: end - low, lanes] = in_a[low:end, :]
-        if high > cut:
-            begin = max(low, cut)
-            gram[begin - low :, lanes] = in_b[begin - cut : high - cut, :]
+        gram[:, t * LANES : (t + 1) * LANES] = flat[t * mine : (t + 1) * mine, :]
+    rank = basis.shape[1] // Z_HI
+    strip = 4 * basis.shape[0] // (count // Z_HI)
+    share = strip // (2 * 2 * Z_HI)
+    for j in range(count):
+        zh, frm = divmod(j, count // Z_HI)
+        place, odd = divmod(frm, 2)
+        x, side, c = place // (Z_HI * CORES), place // CORES % Z_HI, place % CORES
+        start = (x * CORES + c) * strip + (2 * odd + zh) * (strip // 4)
+        block = pieces[j, rows : rows + share, :]
+        for part in range(2):
+            basis[start + part * share : start + (part + 1) * share, side * rank : (side + 1) * rank] = (
+                block[:, part * rank : (part + 1) * rank]
+            )
     put_product(gram[...], basis[...], out)
 
 
@@ -194,6 +200,27 @@
     return lax.all_to_all(copies, axes, 0, 0, tiled=True)
 
 
+def shift(x, by):
+    return lax.ppermute(x, "x", [(i, (i + by) % N_X) for i in range(N_X)])
+
+
+def ring_sum(mid, x_at):
+    frames, rank, cols = mid.shape
+    block, half = rank // N_X, frames // 2
+    ends = []
+    for way, first in ((1, 0), (-1, half)):
+        total = None
+        for step in range(1, N_X + 1):
+            at = lax.rem(x_at - way * step + 2 * N_X, N_X) * block
+            own = lax.dynamic_slice(mid, (first, at, 0), (half, block, cols))
+            if total is not None:
+                total = shift(total, way)
+                own = (total.astype(F32) + own.astype(F32)).astype(mid.dtype)
+            total = own
+        ends.append(total)
+    return jnp.concatenate(ends, axis=0)
+
+
 def swap(x, axis):
     return lax.ppermute(x, axis, [(0, 1), (1, 0)])
 
@@ -204,8 +231,7 @@
     rank_f = start_basis.shape[1]
     frames_dev, _, cols = video.shape
     frm = lax.axis_index(("y", "zl"))
-    frm_count = lax.axis_size(("y", "zl"))
-    total = frames_dev * frm_count
+    total = frames_dev * lax.axis_size(("y", "zl"))
     x_at, zh_at, core_at = lax.axis_index("x"), lax.axis_index("zh"), lax.axis_index("c")
     first = core_at == 0
     strip = total // (N_X * Z_HI * CORES)
@@ -215,15 +241,14 @@
     at = jnp.stack([x_at, core_at, frame_zh, frame_row]).astype(jnp.int32)
 
     mid = jnp.einsum(
-        "fhw,hr->rfw", video, height_factor, preferred_element_type=F32
+        "fhw,hr->frw", video, height_factor, preferred_element_type=F32
     ).astype(jnp.bfloat16)
-    mid, width, start = lax.optimization_barrier((mid, width_factor, start_basis))
-    mid = lax.psum_scatter(mid, "x", scatter_dimension=0, tiled=True)
+    mid, width = lax.optimization_barrier((mid, width_factor))
     width_other = swap(width, "zh")
-    basis = spread(start, ("y", "zl")).reshape(N_X, Z_HI, CORES, strip, rank_f)
-    basis = basis.transpose(0, 2, 3, 1, 4).reshape(total // Z_HI, Z_HI * rank_f)
-    mid, width_other, basis = lax.optimization_barrier((mid, width_other, basis))
-
+    mid = ring_sum(mid, x_at)
+    mid, width_other = lax.optimization_barrier((mid, width_other))
+
+    mid = mid.transpose(1, 0, 2)
     mid = lax.all_to_all(mid, PLANE, 0, 0, tiled=True).reshape(Z_HI, total, cols)
     low_width = jnp.where(zh_at == 0, width, width_other)
     high_width = jnp.where(zh_at == 0, width_other, width)
@@ -252,29 +277,29 @@
     came = swap(sent, "c")
 
     flat = tiles * mine
-    ring = lax.axis_size("y")
-    rows_a = -(-flat // (2 * 8 * ring)) * 8
-    rows_b = flat // ring - rows_a
-    part_a, part_b = shape(ring, rows_a, LANES), shape(ring, rows_b, LANES)
-    sides = call(
-        cut_kernel,
-        [part_a, part_b],
+    count = lax.axis_size(PLANE)
+    rows = flat // count
+    pieces = call(
+        pack_kernel,
+        shape(count, rows, LANES),
         [VMEM] * 2,
         (kept.reshape(flat, LANES), came.reshape(flat, LANES)),
     )
-    axes = (DEEP, "y")
-    sides = [lax.all_to_all(x, axes[i], 0, 0, tiled=True) for i, x in enumerate(sides)]
-    sides = call(sum_kernel, [part_a, part_b], [VMEM] * 2, sides)
-    sides = [lax.all_to_all(x, axes[1 - i], 0, 0, tiled=True) for i, x in enumerate(sides)]
-    sides = call(sum_kernel, [part_a, part_b], [VMEM] * 2, sides)
-    sides = [lax.all_to_all(x, axes[i], 0, 0, tiled=True) for i, x in enumerate(sides)]
+    pieces = lax.all_to_all(pieces, PLANE, 0, 0, tiled=True)
+    share = frames_dev // (2 * Z_HI)
+    start = lax.dynamic_slice_in_dim(start_basis, zh_at * 2 * share, 2 * share, 0)
+    start = jnp.concatenate([start[:share], start[share:]], axis=1)
+    padded = -(-(rows + share) // 8) * 8
+    pieces = call(sum_kernel, shape(count, padded, LANES), [VMEM] * 2, (pieces, start))
+    pieces = lax.all_to_all(pieces, PLANE, 0, 0, tiled=True)
 
     packed_shape = shape(N_X * CORES, strip, Z_HI * rank_f)
     gram, packed = call(
-        first_kernel,
+        lambda *refs: first_kernel(rows, *refs),
         [shape(mine, total), packed_shape],
-        [VMEM] * 3,
-        [x.reshape(-1, LANES) for x in sides] + [basis],
+        [VMEM],
+        (pieces,),
+        [pltpu.VMEM((flat, LANES), F32), pltpu.VMEM((total // Z_HI, Z_HI * rank_f), F32)],
     )
     for step in range(ITERS):
         packed = lax.all_to_all(packed, ("x", "c"), 0, 0, tiled=True)

time: 286 us -> 255 us (0.89)
  blocking collectives: 104 us -> 65.1 us
  starting transfers between devices: 56.2 us -> 71.3 us
  between operations: 14.3 us -> 1.06 us
  waiting for transfers between devices: 76.5 us -> 81.4 us
  local copies, waits for them, and re-layouts: 9.02 us -> 5.06 us
  other arithmetic: 1.67 us -> 5.48 us
    all_to_all x5 -> x1, blocking collectives: 78.2 us -> 42.3 us  [local(): pieces = lax.all_to_all(pieces, PLANE, 0, 0, tiled=True)]
    ppermute x0 -> x6, starting transfers between devices: none -> 21 us  [shift(): return lax.ppermute(x, 'x', [(i, (i + by) % N_X) for i in range(N_X)])]
    all_to_all x1, waiting for transfers between devices: 11 us -> 27.2 us  [local(): pieces = lax.all_to_all(pieces, PLANE, 0, 0, tiled=True)]
    all_to_all x2 -> x1, starting transfers between devices: 17 us -> 3.54 us  [spread(): return lax.all_to_all(copies, axes, 0, 0, tiled=True)]
    reduce_scatter x1 -> x0, waiting for transfers between devices: 13.2 us -> none  [local(): mid = lax.psum_scatter(mid, 'x', scatter_dimension=0, tiled=True)]
    ppermute x0 -> x6, waiting for transfers between devices: none -> 10.7 us  [shift(): return lax.ppermute(x, 'x', [(i, (i + by) % N_X) for i in range(N_X)])]
    ppermute x3, starting transfers between devices: 15.7 us -> 24.2 us  [swap(): return lax.ppermute(x, axis, [(0, 1), (1, 0)])]
    all_to_all x2 -> x1, waiting for transfers between devices: 22.8 us -> 17.4 us  [spread(): return lax.all_to_all(copies, axes, 0, 0, tiled=True)]
  transfers between devices with their start and end apart: 9 -> 13, of which waited for: 8 -> 11; matrix products, arithmetic and copies ran while one was open for 2% -> 1% of each run, Pallas kernels for 0% -> 0%
where the time goes in v1:
time: 255 us; the launch traced here: 252 us
  waiting for transfers between devices  81.4 us (32%)
  starting transfers between devices  71.3 us (28%)
  blocking collectives  65.1 us (26%)
  Pallas kernels  17.6 us (7%)
  other arithmetic  5.48 us (2%)
  matrix products  5.15 us (2%)
  local copies, waits for them, and re-layouts  5.06 us (2%)
    all_to_all x1, blocking collectives, local(): pieces = lax.all_to_all(pieces, PLANE, 0, 0, tiled=True)  42.3 us
    all_to_all x1, waiting for transfers between devices, local(): pieces = lax.all_to_all(pieces, PLANE, 0, 0, tiled=True)  27.2 us
    ppermute x3, starting transfers between devices, swap(): return lax.ppermute(x, axis, [(0, 1), (1, 0)])  24.2 us
    all_to_all x2, blocking collectives, local(): packed = lax.all_to_all(packed, ('x', 'c'), 0, 0, tiled=True)  22.8 us
    ppermute x6, starting transfers between devices, shift(): return lax.ppermute(x, 'x', [(i, (i + by) % N_X) for i in range(N_X)])  21 us
    pallas_call x7, Pallas kernels, call(): pl.pallas_call(kernel, out_shape=outs, in_specs=ins, out_specs=jax.tree.m...  17.6 us
    all_to_all x1, waiting for transfers between devices, spread(): return lax.all_to_all(copies, axes, 0, 0, tiled=True)  17.4 us
    all_to_all x1, waiting for transfers between devices, local(): lax.all_to_all(mid, PLANE, 0, 0, tiled=True).reshape(Z_HI, total, cols)  16.1 us
  transfers between devices with their start and end apart: 13, of which 11 were waited for; matrix products, arithmetic and copies ran while one was open for 1% of the time, Pallas kernels for 0%

profile of v1, /device:TPU:1, one launch (start us, length us, event | category | flops | bytes accessed | tf_op | source)
XLA Modules:
  0.0 252.2 jit_solution(14820766112929492015)
XLA Ops:
  1.6 3.7 %convert_bitcast_fusion = bf16[40,256,128]{2,1,0:T(8,128)(2,1)S(1)} fusion(bf16[40,384,128]{2,1,0:T(8,128)(2,1)} %param.4, bf16[384,256]{1,0:T(8,128)(2,1)S(1)} %copy-done), kind=kOutput, calls=%fused_computation.1 | convolution fusion | flops 1007943680 | bytes 6750208 | tf_op jit(solution)/shard_map/fhw,hr->frw/dot_general | solution.py:243
  6.0 3.9 %collective-permute-start = (bf16[20,64,128]{2,1,0:T(8,128)(2,1)}, bf16[20,64,128]{2,1,0:T(8,128)(2,1)S(1)}, u32[]{:S(2)}, u32[]{:S(2)}) collective-permute-start(bf16[20,64,128]{2,1,0:T(8,128)(2,1)} %get-tuple-element.30), channel_id=1, source_target_pairs={{0,4},{4,8},{8,12},{12,0},{1,5},{5,9},{9,13},{13,1},{2,6},{6,10},{... | collective-permute-start | bytes 983048 | tf_op jit(solution)/shard_map/ppermute | solution.py:204
  10.0 3.2 %collective-permute-start.3 = (bf16[20,64,128]{2,1,0:T(8,128)(2,1)S(1)}, bf16[20,64,128]{2,1,0:T(8,128)(2,1)}, u32[]{:S(2)}, u32[]{:S(2)}) collective-permute-start(bf16[20,64,128]{2,1,0:T(8,128)(2,1)S(1)} %get-tuple-element.31), channel_id=1, source_target_pairs={{0,12},{4,0},{8,4},{12,8},{1,13},{5,1},{9,5},{13,9},{2,14},{6,2},{... | collective-permute-start | bytes 983048 | tf_op jit(solution)/shard_map/ppermute | solution.py:204
  13.2 2.7 %collective-permute-done = bf16[20,64,128]{2,1,0:T(8,128)(2,1)S(1)} collective-permute-done((bf16[20,64,128]{2,1,0:T(8,128)(2,1)}, bf16[20,64,128]{2,1,0:T(8,128)(2,1)S(1)}, u32[]{:S(2)}, u32[]{:S(2)}) %collective-permute-start) | collective-permute-done | bytes 327712 | tf_op jit(solution)/shard_map/ppermute | solution.py:204
  15.9 2.0 collective-permute-done.3
  17.9 1.9 add_convert_fusion.6
  19.8 5.4 %collective-permute-start.1 = (bf16[20,64,128]{2,1,0:T(8,128)(2,1)}, bf16[20,64,128]{2,1,0:T(8,128)(2,1)S(1)}, u32[]{:S(2)}, u32[]{:S(2)}) collective-permute-start(bf16[20,64,128]{2,1,0:T(8,128)(2,1)} %get-tuple-element.28), channel_id=1, source_target_pairs={{0,4},{4,8},{8,12},{12,0},{1,5},{5,9},{9,13},{13,1},{2,6},{6,10},{... | collective-permute-start | bytes 983048 | tf_op jit(solution)/shard_map/ppermute | solution.py:204
  25.3 1.9 collective-permute-start.4
  27.2 2.5 %collective-permute-done.1 = bf16[20,64,128]{2,1,0:T(8,128)(2,1)S(1)} collective-permute-done((bf16[20,64,128]{2,1,0:T(8,128)(2,1)}, bf16[20,64,128]{2,1,0:T(8,128)(2,1)S(1)}, u32[]{:S(2)}, u32[]{:S(2)}) %collective-permute-start.1) | collective-permute-done | bytes 327712 | tf_op jit(solution)/shard_map/ppermute | solution.py:204
  29.8 3.5 %collective-permute-done.4 = bf16[20,64,128]{2,1,0:T(8,128)(2,1)} collective-permute-done((bf16[20,64,128]{2,1,0:T(8,128)(2,1)S(1)}, bf16[20,64,128]{2,1,0:T(8,128)(2,1)}, u32[]{:S(2)}, u32[]{:S(2)}) %collective-permute-start.4) | collective-permute-done | bytes 327712 | tf_op jit(solution)/shard_map/ppermute | solution.py:204
  33.2 1.9 add_convert_fusion.5
  35.2 2.1 collective-permute-start.2
  37.3 4.4 %collective-permute-start.5 = (bf16[20,64,128]{2,1,0:T(8,128)(2,1)S(1)}, bf16[20,64,128]{2,1,0:T(8,128)(2,1)}, u32[]{:S(2)}, u32[]{:S(2)}) collective-permute-start(bf16[20,64,128]{2,1,0:T(8,128)(2,1)S(1)} %get-tuple-element.27), channel_id=1, source_target_pairs={{0,12},{4,0},{8,4},{12,8},{1,13},{5,1},{9,5},{13,9},{2,14},{6,2},{... | collective-permute-start | bytes 983048 | tf_op jit(solution)/shard_map/ppermute | solution.py:204
  41.7 11.8 %collective-permute-start.6 = (bf16[128,256]{1,0:T(8,128)(2,1)S(1)}, bf16[128,256]{1,0:T(8,128)(2,1)}, u32[]{:S(2)}, u32[]{:S(2)}) collective-permute-start(bf16[128,256]{1,0:T(8,128)(2,1)S(1)} %copy-done.1), channel_id=1, source_target_pairs={{0,2},{2,0},{1,3},{3,1},{4,6},{6,4},{5,7},{7,5},{8,10},{10,8},{9,1... | collective-permute-start | bytes 196616 | tf_op jit(solution)/shard_map/ppermute | solution.py:225
  56.6 13.5 %all-to-all-start = ((bf16[64,40,128]{2,1,0:T(8,128)(2,1)}), bf16[64,40,128]{2,1,0:T(8,128)(2,1)S(1)}, u32[]{:S(2)}, u32[]{:S(2)}) async-start(bf16[64,40,128]{2,1,0:T(8,128)(2,1)} %copy.13), calls=%async_computation | async-start | bytes 1310720 | tf_op jit(solution)/shard_map/all_to_all | solution.py:252
  70.1 16.1 %all-to-all-done = bf16[64,40,128]{2,1,0:T(8,128)(2,1)S(1)} async-done(((bf16[64,40,128]{2,1,0:T(8,128)(2,1)}), bf16[64,40,128]{2,1,0:T(8,128)(2,1)S(1)}, u32[]{:S(2)}, u32[]{:S(2)}) %all-to-all-start) | async-done | bytes 655392 | tf_op jit(solution)/shard_map/all_to_all | solution.py:252
  87.8 9.3 %collective-permute-start.7 = (bf16[1280,128]{1,0:T(8,128)(2,1)S(1)}, bf16[1280,128]{1,0:T(8,128)(2,1)S(1)}, u32[]{:S(2)}, u32[]{:S(2)}) collective-permute-start(bf16[1280,128]{1,0:T(8,128)(2,1)S(1)} %select_convert_fusion), channel_id=1, source_target_pairs={{0,1},{1,0},{2,3},{3,2},{4,5},{5,4},{6,7},{7,6},{8,9},{9,8},{10,11... | collective-permute-start | bytes 983048 | tf_op jit(solution)/shard_map/ppermute | solution.py:225
  99.7 3.5 %all-to-all-start.1 = ((bf16[4,1280,128]{2,1,0:T(8,128)(2,1)}), bf16[4,1280,128]{2,1,0:T(8,128)(2,1)S(1)}, u32[]{:S(2)}, u32[]{:S(2)}) async-start(bf16[4,1280,128]{2,1,0:T(8,128)(2,1)} %broadcast_in_dim.2), calls=%async_computation.1 | async-start | bytes 2621440 | tf_op jit(solution)/shard_map/all_to_all | solution.py:200
  103.4 17.4 %all-to-all-done.1.refs_1_ = bf16[4,1280,128]{2,1,0:T(8,128)(2,1)S(1)} async-done(((bf16[4,1280,128]{2,1,0:T(8,128)(2,1)}), bf16[4,1280,128]{2,1,0:T(8,128)(2,1)S(1)}, u32[]{:S(2)}, u32[]{:S(2)}) %all-to-all-start.1) | async-done | bytes 1310752 | tf_op jit(solution)/shard_map/all_to_all | solution.py:200
  120.9 1.5 shard_map.59
  122.4 3.1 %collective-permute-start.8 = (f32[20,80,128]{2,1,0:T(8,128)S(1)}, f32[20,80,128]{2,1,0:T(8,128)S(1)}, u32[]{:S(2)}, u32[]{:S(2)}) collective-permute-start(f32[20,80,128]{2,1,0:T(8,128)S(1)} %get-tuple-element.15), channel_id=1, source_target_pairs={{0,1},{1,0},{2,3},{3,2},{4,5},{5,4},{6,7},{7,6},{8,9},{9,8},{10,11... | collective-permute-start | bytes 2457608 | tf_op jit(solution)/shard_map/ppermute | solution.py:225
  125.5 1.9 collective-permute-done.8
  128.5 5.0 %all-to-all-start.2 = ((f32[64,25,128]{2,1,0:T(8,128)}), f32[64,25,128]{2,1,0:T(8,128)S(1)}, u32[]{:S(2)}, u32[]{:S(2)}) async-start(f32[64,25,128]{2,1,0:T(8,128)} %shard_map.60), calls=%async_computation.2 | async-start | bytes 2097152 | tf_op jit(solution)/shard_map/all_to_all | solution.py:288
  133.6 27.2 %all-to-all-done.2.parts = f32[64,25,128]{2,1,0:T(8,128)S(1)} async-done(((f32[64,25,128]{2,1,0:T(8,128)}), f32[64,25,128]{2,1,0:T(8,128)S(1)}, u32[]{:S(2)}, u32[]{:S(2)}) %all-to-all-start.2) | async-done | bytes 819232 | tf_op jit(solution)/shard_map/all_to_all | solution.py:288
  160.9 42.3 %all_to_all.35.refs_0_ = f32[64,40,128]{2,1,0:T(8,128)S(1)} all-to-all(f32[64,40,128]{2,1,0:T(8,128)S(1)} %shard_map.61), channel_id=1, replica_groups=mesh['y'=8,'zl'=4,'x'=4,'zh'=2,'c'=2] {'zh','y','zl'}, dimensions={0} | all-to-all | bytes 2621440 | tf_op jit(solution)/shard_map/all_to_all | solution.py:294
  204.4 12.2 %all_to_all.36 = f32[8,80,128]{2,1,0:T(8,128)S(1)} all-to-all(f32[8,80,128]{2,1,0:T(8,128)S(1)} %get-tuple-element.17), channel_id=1, replica_groups=mesh['y'=8,'zl'=4,'x'=4,'zh'=2,'c'=2] {'x','c'}, dimensions={0} | all-to-all | bytes 655360 | tf_op jit(solution)/shard_map/all_to_all | solution.py:305
  216.6 4.4 %shard_map.63 = f32[8,80,128]{2,1,0:T(8,128)S(1)} custom-call(f32[640,128]{1,0:T(8,128)S(1)} %bitcast.23, f32[160,1280]{1,0:T(8,128)S(1)} %get-tuple-element.16.gram), custom_call_target="tpu_custom_call" | custom-call | tf_op jit(solution)/shard_map/pallas_call | solution.py:188
  221.0 10.6 %all_to_all.37 = f32[8,80,128]{2,1,0:T(8,128)S(1)} all-to-all(f32[8,80,128]{2,1,0:T(8,128)S(1)} %shard_map.63), channel_id=1, replica_groups=mesh['y'=8,'zl'=4,'x'=4,'zh'=2,'c'=2] {'x','c'}, dimensions={0} | all-to-all | bytes 655360 | tf_op jit(solution)/shard_map/all_to_all | solution.py:305
  231.6 5.1 %shard_map.64 = f32[8,80,128]{2,1,0:T(8,128)} custom-call(f32[640,128]{1,0:T(8,128)S(1)} %bitcast.24, f32[160,1280]{1,0:T(8,128)S(1)} %get-tuple-element.16.gram), custom_call_target="tpu_custom_call" | custom-call | tf_op jit(solution)/shard_map/pallas_call | solution.py:188
  236.7 4.1 %all-to-all-start.6 = ((f32[8,80,128]{2,1,0:T(8,128)}), f32[8,80,128]{2,1,0:T(8,128)S(1)}, u32[]{:S(2)}, u32[]{:S(2)}) async-start(f32[8,80,128]{2,1,0:T(8,128)} %shard_map.64), calls=%async_computation.6 | async-start | bytes 655360 | tf_op jit(solution)/shard_map/all_to_all | solution.py:305
  241.6 6.4 %all-to-all-done.6 = f32[8,80,128]{2,1,0:T(8,128)S(1)} async-done(((f32[8,80,128]{2,1,0:T(8,128)}), f32[8,80,128]{2,1,0:T(8,128)S(1)}, u32[]{:S(2)}, u32[]{:S(2)}) %all-to-all-start.6) | async-done | bytes 327712 | tf_op jit(solution)/shard_map/all_to_all | solution.py:305
  247.9 4.2 %shard_map.65 = f32[40,64]{1,0:T(8,128)} custom-call(s32[4]{0:T(128)S(1)} %pad_add_fusion.refs_0_.at, f32[640,128]{1,0:T(8,128)S(1)} %bitcast.22), custom_call_target="tpu_custom_call" | custom-call | tf_op jit(solution)/shard_map/pallas_call | solution.py:188
  (28 shorter events, 12.3 us)
Async XLA Ops:
  0.6 0.9 copy-start
  5.2 36.4 %copy-start.1 = (bf16[128,256]{1,0:T(8,128)(2,1)S(1)}, bf16[128,256]{1,0:T(8,128)(2,1)}, u32[]{:S(2)}) copy-start(bf16[128,256]{1,0:T(8,128)(2,1)} %param.6) | copy-start | bytes 196612
  6.0 9.9 %collective-permute-start = (bf16[20,64,128]{2,1,0:T(8,128)(2,1)}, bf16[20,64,128]{2,1,0:T(8,128)(2,1)S(1)}, u32[]{:S(2)}, u32[]{:S(2)}) collective-permute-start(bf16[20,64,128]{2,1,0:T(8,128)(2,1)} %get-tuple-element.30), channel_id=1, source_target_pairs={{0,4},{4,8},{8,12},{12,0},{1,5},{5,9},{9,13},{13,1},{2,6},{6,10},{... | collective-permute-start | bytes 983048 | tf_op jit(solution)/shard_map/ppermute | solution.py:204
  10.0 7.9 %collective-permute-start.3 = (bf16[20,64,128]{2,1,0:T(8,128)(2,1)S(1)}, bf16[20,64,128]{2,1,0:T(8,128)(2,1)}, u32[]{:S(2)}, u32[]{:S(2)}) collective-permute-start(bf16[20,64,128]{2,1,0:T(8,128)(2,1)S(1)} %get-tuple-element.31), channel_id=1, source_target_pairs={{0,12},{4,0},{8,4},{12,8},{1,13},{5,1},{9,5},{13,9},{2,14},{6,2},{... | collective-permute-start | bytes 983048 | tf_op jit(solution)/shard_map/ppermute | solution.py:204
  19.8 9.9 %collective-permute-start.1 = (bf16[20,64,128]{2,1,0:T(8,128)(2,1)}, bf16[20,64,128]{2,1,0:T(8,128)(2,1)S(1)}, u32[]{:S(2)}, u32[]{:S(2)}) collective-permute-start(bf16[20,64,128]{2,1,0:T(8,128)(2,1)} %get-tuple-element.28), channel_id=1, source_target_pairs={{0,4},{4,8},{8,12},{12,0},{1,5},{5,9},{9,13},{13,1},{2,6},{6,10},{... | collective-permute-start | bytes 983048 | tf_op jit(solution)/shard_map/ppermute | solution.py:204
  25.3 7.9 %collective-permute-start.4 = (bf16[20,64,128]{2,1,0:T(8,128)(2,1)S(1)}, bf16[20,64,128]{2,1,0:T(8,128)(2,1)}, u32[]{:S(2)}, u32[]{:S(2)}) collective-permute-start(bf16[20,64,128]{2,1,0:T(8,128)(2,1)S(1)} %get-tuple-element.29), channel_id=1, source_target_pairs={{0,12},{4,0},{8,4},{12,8},{1,13},{5,1},{9,5},{13,9},{2,14},{6,2},{... | collective-permute-start | bytes 983048 | tf_op jit(solution)/shard_map/ppermute | solution.py:204
  35.2 18.3 %collective-permute-start.2 = (bf16[20,64,128]{2,1,0:T(8,128)(2,1)}, bf16[20,64,128]{2,1,0:T(8,128)(2,1)S(1)}, u32[]{:S(2)}, u32[]{:S(2)}) collective-permute-start(bf16[20,64,128]{2,1,0:T(8,128)(2,1)} %get-tuple-element.26), channel_id=1, source_target_pairs={{0,4},{4,8},{8,12},{12,0},{1,5},{5,9},{9,13},{13,1},{2,6},{6,10},{... | collective-permute-start | bytes 983048 | tf_op jit(solution)/shard_map/ppermute | solution.py:204
  37.3 16.2 %collective-permute-start.5 = (bf16[20,64,128]{2,1,0:T(8,128)(2,1)S(1)}, bf16[20,64,128]{2,1,0:T(8,128)(2,1)}, u32[]{:S(2)}, u32[]{:S(2)}) collective-permute-start(bf16[20,64,128]{2,1,0:T(8,128)(2,1)S(1)} %get-tuple-element.27), channel_id=1, source_target_pairs={{0,12},{4,0},{8,4},{12,8},{1,13},{5,1},{9,5},{13,9},{2,14},{6,2},{... | collective-permute-start | bytes 983048 | tf_op jit(solution)/shard_map/ppermute | solution.py:204
  41.7 13.6 %collective-permute-start.6 = (bf16[128,256]{1,0:T(8,128)(2,1)S(1)}, bf16[128,256]{1,0:T(8,128)(2,1)}, u32[]{:S(2)}, u32[]{:S(2)}) collective-permute-start(bf16[128,256]{1,0:T(8,128)(2,1)S(1)} %copy-done.1), channel_id=1, source_target_pairs={{0,2},{2,0},{1,3},{3,1},{4,6},{6,4},{5,7},{7,5},{8,10},{10,8},{9,1... | collective-permute-start | bytes 196616 | tf_op jit(solution)/shard_map/ppermute | solution.py:225
  56.6 29.6 %all-to-all-start = ((bf16[64,40,128]{2,1,0:T(8,128)(2,1)}), bf16[64,40,128]{2,1,0:T(8,128)(2,1)S(1)}, u32[]{:S(2)}, u32[]{:S(2)}) async-start(bf16[64,40,128]{2,1,0:T(8,128)(2,1)} %copy.13), calls=%async_computation | async-start | bytes 1310720 | tf_op jit(solution)/shard_map/all_to_all | solution.py:252
  87.8 10.5 %collective-permute-start.7 = (bf16[1280,128]{1,0:T(8,128)(2,1)S(1)}, bf16[1280,128]{1,0:T(8,128)(2,1)S(1)}, u32[]{:S(2)}, u32[]{:S(2)}) collective-permute-start(bf16[1280,128]{1,0:T(8,128)(2,1)S(1)} %select_convert_fusion), channel_id=1, source_target_pairs={{0,1},{1,0},{2,3},{3,2},{4,5},{5,4},{6,7},{7,6},{8,9},{9,8},{10,11... | collective-permute-start | bytes 983048 | tf_op jit(solution)/shard_map/ppermute | solution.py:225
  99.7 21.2 %all-to-all-start.1 = ((bf16[4,1280,128]{2,1,0:T(8,128)(2,1)}), bf16[4,1280,128]{2,1,0:T(8,128)(2,1)S(1)}, u32[]{:S(2)}, u32[]{:S(2)}) async-start(bf16[4,1280,128]{2,1,0:T(8,128)(2,1)} %broadcast_in_dim.2), calls=%async_computation.1 | async-start | bytes 2621440 | tf_op jit(solution)/shard_map/all_to_all | solution.py:200
  122.4 11.2 %copy-start.2 = (f32[40,64]{1,0:T(8,128)S(1)}, f32[40,64]{1,0:T(8,128)}, u32[]{:S(2)}) copy-start(f32[40,64]{1,0:T(8,128)} %param.7) | copy-start | bytes 30724
  122.4 5.0 %collective-permute-start.8 = (f32[20,80,128]{2,1,0:T(8,128)S(1)}, f32[20,80,128]{2,1,0:T(8,128)S(1)}, u32[]{:S(2)}, u32[]{:S(2)}) collective-permute-start(f32[20,80,128]{2,1,0:T(8,128)S(1)} %get-tuple-element.15), channel_id=1, source_target_pairs={{0,1},{1,0},{2,3},{3,2},{4,5},{5,4},{6,7},{7,6},{8,9},{9,8},{10,11... | collective-permute-start | bytes 2457608 | tf_op jit(solution)/shard_map/ppermute | solution.py:225
  128.5 32.3 %all-to-all-start.2 = ((f32[64,25,128]{2,1,0:T(8,128)}), f32[64,25,128]{2,1,0:T(8,128)S(1)}, u32[]{:S(2)}, u32[]{:S(2)}) async-start(f32[64,25,128]{2,1,0:T(8,128)} %shard_map.60), calls=%async_computation.2 | async-start | bytes 2097152 | tf_op jit(solution)/shard_map/all_to_all | solution.py:288
  236.7 11.2 %all-to-all-start.6 = ((f32[8,80,128]{2,1,0:T(8,128)}), f32[8,80,128]{2,1,0:T(8,128)S(1)}, u32[]{:S(2)}, u32[]{:S(2)}) async-start(f32[8,80,128]{2,1,0:T(8,128)} %shard_map.64), calls=%async_computation.6 | async-start | bytes 655360 | tf_op jit(solution)/shard_map/all_to_all | solution.py:305

commit v2 on v0

--- a/solution.py
+++ b/solution.py
@@ -13,8 +13,8 @@
 Z_LO = 4
 N_X = 4
 LANES = 128
+FRM = ("y", "zl")
 PLANE = ("zh", "y", "zl")
-DEEP = ("zh", "zl")
 PIVOTS = 4
 VMEM = pl.BlockSpec(memory_space=pltpu.VMEM)
 SMEM = pl.BlockSpec(memory_space=pltpu.SMEM)
@@ -25,6 +25,47 @@
 
 def shape(*dims, dtype=F32):
     return jax.ShapeDtypeStruct(dims, dtype)
+
+
+def pick_kernel(at, mid, out_a, out_b):
+    for way, first, out in ((1, 0, out_a), (-1, mid.shape[0] // 2, out_b)):
+        ring_block(at, mid, 1, way, first, out, None)
+
+
+def ring_block(at, mid, step, way, first, out, came):
+    half, block, _ = out.shape
+    start = pl.multiple_of(lax.rem(at[0] - way * step + 2 * N_X, N_X) * block, 64)
+    for f in range(half):
+        own = mid[first + f, pl.ds(start, block), :]
+        if came is not None:
+            own = (own.astype(F32) + came[f].astype(F32)).astype(out.dtype)
+        out[f] = own
+
+
+def core_kernel(at, mid, width, width_other, own, sent):
+    half = own.shape[1]
+    zh = at[4]
+    part = jnp.dot(mid[zh], width[...], preferred_element_type=F32) + jnp.dot(
+        mid[1 - zh], width_other[...], preferred_element_type=F32
+    )
+    low, high = part[:, :half].astype(own.dtype), part[:, half:].astype(own.dtype)
+    first = at[1] == 0
+
+    @pl.when(first)
+    def _():
+        own[...] = low
+        sent[...] = high
+
+    @pl.when(jnp.logical_not(first))
+    def _():
+        own[...] = high
+        sent[...] = low
+
+
+def copies_kernel(a, b, out):
+    total = (a[...].astype(F32) + b[...].astype(F32)).astype(out.dtype)
+    for j in range(out.shape[0]):
+        out[j] = total
 
 
 def gram_kernel(scale, at, blocks, kept, sent, core, acc):
@@ -64,22 +105,13 @@
                 sent[tile * Z_HI + zh] = acc[pl.ds(send_at, strip), lanes]
 
 
-def cut_kernel(a, b, out_a, out_b):
-    start = 0
-    for out in (out_a, out_b):
-        pieces, rows, _ = out.shape
-        for j in range(pieces):
-            out[j] = a[start : start + rows, :] + b[start : start + rows, :]
-            start += rows
-
-
-def sum_kernel(in_a, in_b, out_a, out_b):
-    for parts, out in ((in_a, out_a), (in_b, out_b)):
-        total = parts[0]
-        for j in range(1, parts.shape[0]):
-            total = total + parts[j]
-        for j in range(out.shape[0]):
-            out[j] = total
+def sum_kernel(rows, parts, out):
+    count = parts.shape[0] // rows
+    total = parts[0:rows, :]
+    for j in range(1, count):
+        total = total + parts[j * rows : (j + 1) * rows, :]
+    for j in range(count):
+        out[j * rows : (j + 1) * rows, :] = total
 
 
 def put_product(gram, basis, out):
@@ -94,18 +126,21 @@
         out[j] = packed
 
 
-def first_kernel(in_a, in_b, basis, gram, out):
+def first_kernel(flat, shards, gram, out, basis):
     mine, total = gram.shape
-    cut = in_a.shape[0]
     for t in range(total // LANES):
-        lanes = slice(t * LANES, (t + 1) * LANES)
-        low, high = t * mine, (t + 1) * mine
-        if low < cut:
-            end = min(high, cut)
-            gram[: end - low, lanes] = in_a[low:end, :]
-        if high > cut:
-            begin = max(low, cut)
-            gram[begin - low :, lanes] = in_b[begin - cut : high - cut, :]
+        gram[:, t * LANES : (t + 1) * LANES] = flat[t * mine : (t + 1) * mine, :]
+    rank = basis.shape[1] // Z_HI
+    strip = total // (N_X * Z_HI * CORES)
+    half = strip // 4
+    for frm in range(total // (2 * half)):
+        place, odd = divmod(frm, 2)
+        x, side, c = place // (Z_HI * CORES), place // CORES % Z_HI, place % CORES
+        for part in range(2):
+            start = (x * CORES + c) * strip + (2 * odd + part) * half
+            basis[start : start + half, side * rank : (side + 1) * rank] = shards[
+                frm * half : (frm + 1) * half, part * rank : (part + 1) * rank
+            ]
     put_product(gram[...], basis[...], out)
 
 
@@ -189,13 +224,33 @@
     )(*args)
 
 
-def spread(x, axes):
-    copies = jnp.broadcast_to(x[None], (lax.axis_size(axes),) + x.shape)
-    return lax.all_to_all(copies, axes, 0, 0, tiled=True)
+def trade(x, axes):
+    count = lax.axis_size(axes)
+    rows = lax.all_to_all(x.reshape(count, 1, -1), axes, 0, 0, tiled=True)
+    return rows.reshape(x.shape)
+
+
+def shift(x, by):
+    return lax.ppermute(x, "x", [(i, (i + by) % N_X) for i in range(N_X)])
 
 
 def swap(x, axis):
     return lax.ppermute(x, axis, [(0, 1), (1, 0)])
+
+
+def ring_sum(mid, at):
+    frames, rank, cols = mid.shape
+    piece = shape(frames // 2, rank // N_X, cols, dtype=mid.dtype)
+    ends = list(call(pick_kernel, [piece, piece], [SMEM, VMEM], (at, mid)))
+    ways = ((1, 0), (-1, frames // 2))
+    for step in range(2, N_X + 1):
+        for i, (way, first) in enumerate(ways):
+
+            def kernel(at, came, mid, out, way=way, first=first, step=step):
+                ring_block(at, mid, step, way, first, out, came)
+
+            ends[i] = call(kernel, piece, [SMEM, VMEM, VMEM], (at, shift(ends[i], way), mid))
+    return jnp.concatenate(ends, axis=0)
 
 
 def local(video, height_factor, width_factor, start_basis):
@@ -203,40 +258,41 @@
     rank_w = width_factor.shape[1]
     rank_f = start_basis.shape[1]
     frames_dev, _, cols = video.shape
-    frm = lax.axis_index(("y", "zl"))
-    frm_count = lax.axis_size(("y", "zl"))
-    total = frames_dev * frm_count
+    frm = lax.axis_index(FRM)
+    total = frames_dev * lax.axis_size(FRM)
     x_at, zh_at, core_at = lax.axis_index("x"), lax.axis_index("zh"), lax.axis_index("c")
-    first = core_at == 0
     strip = total // (N_X * Z_HI * CORES)
     frame = frm * frames_dev
     frame_zh = frame // (CORES * strip) % Z_HI
     frame_row = (frame // (Z_HI * CORES * strip) * CORES + frame // strip % CORES) * strip + frame % strip
-    at = jnp.stack([x_at, core_at, frame_zh, frame_row]).astype(jnp.int32)
+    at = jnp.stack([x_at, core_at, frame_zh, frame_row, zh_at]).astype(jnp.int32)
 
     mid = jnp.einsum(
-        "fhw,hr->rfw", video, height_factor, preferred_element_type=F32
+        "fhw,hr->frw", video, height_factor, preferred_element_type=F32
     ).astype(jnp.bfloat16)
-    mid, width, start = lax.optimization_barrier((mid, width_factor, start_basis))
-    mid = lax.psum_scatter(mid, "x", scatter_dimension=0, tiled=True)
+    mid = ring_sum(mid, at).transpose(1, 0, 2)
+
+    mid, width = lax.optimization_barrier((mid, width_factor))
     width_other = swap(width, "zh")
-    basis = spread(start, ("y", "zl")).reshape(N_X, Z_HI, CORES, strip, rank_f)
-    basis = basis.transpose(0, 2, 3, 1, 4).reshape(total // Z_HI, Z_HI * rank_f)
-    mid, width_other, basis = lax.optimization_barrier((mid, width_other, basis))
-
     mid = lax.all_to_all(mid, PLANE, 0, 0, tiled=True).reshape(Z_HI, total, cols)
-    low_width = jnp.where(zh_at == 0, width, width_other)
-    high_width = jnp.where(zh_at == 0, width_other, width)
-    part = jnp.dot(mid[0], low_width, preferred_element_type=F32) + jnp.dot(
-        mid[1], high_width, preferred_element_type=F32
-    )
     half = rank_w // CORES
-    low, high = part[:, :half], part[:, half:]
-    came = swap(jnp.where(first, high, low).astype(jnp.bfloat16), "c")
-    own = jnp.where(first, low, high).astype(jnp.bfloat16)
-    core = (own.astype(F32) + came.astype(F32)).astype(jnp.bfloat16)
-
-    blocks = spread(core, "x")
+    own, sent = call(
+        core_kernel,
+        [shape(total, half, dtype=mid.dtype)] * 2,
+        [SMEM] + [VMEM] * 3,
+        (at, mid, width, width_other),
+    )
+
+    copies = call(
+        copies_kernel, shape(N_X, total, half, dtype=mid.dtype), [VMEM] * 2, (own, swap(sent, "c"))
+    )
+    part = frames_dev // 2
+    start = jnp.concatenate([start_basis[:part], start_basis[part:]], axis=1).reshape(1, -1)
+    start = jnp.broadcast_to(start[None], (lax.axis_size(FRM),) + start.shape)
+    copies, start = lax.optimization_barrier((copies, start))
+    blocks = lax.all_to_all(copies, "x", 0, 0, tiled=True)
+    shards = lax.all_to_all(start, FRM, 0, 0, tiled=True).reshape(-1, LANES)
+    blocks, shards = lax.optimization_barrier((blocks, shards))
     mine = Z_HI * strip
     tiles = total // LANES
     kept, sent = call(
@@ -251,30 +307,19 @@
     )
     came = swap(sent, "c")
 
-    flat = tiles * mine
-    ring = lax.axis_size("y")
-    rows_a = -(-flat // (2 * 8 * ring)) * 8
-    rows_b = flat // ring - rows_a
-    part_a, part_b = shape(ring, rows_a, LANES), shape(ring, rows_b, LANES)
-    sides = call(
-        cut_kernel,
-        [part_a, part_b],
-        [VMEM] * 2,
-        (kept.reshape(flat, LANES), came.reshape(flat, LANES)),
-    )
-    axes = (DEEP, "y")
-    sides = [lax.all_to_all(x, axes[i], 0, 0, tiled=True) for i, x in enumerate(sides)]
-    sides = call(sum_kernel, [part_a, part_b], [VMEM] * 2, sides)
-    sides = [lax.all_to_all(x, axes[1 - i], 0, 0, tiled=True) for i, x in enumerate(sides)]
-    sides = call(sum_kernel, [part_a, part_b], [VMEM] * 2, sides)
-    sides = [lax.all_to_all(x, axes[i], 0, 0, tiled=True) for i, x in enumerate(sides)]
+    flat = shape(tiles * mine, LANES)
+    pieces = trade(kept.reshape(flat.shape) + came.reshape(flat.shape), PLANE)
+    rows = flat.shape[0] // lax.axis_size(PLANE)
+    pieces = call(lambda *refs: sum_kernel(rows, *refs), flat, [VMEM], (pieces,))
+    pieces = trade(pieces, PLANE)
 
     packed_shape = shape(N_X * CORES, strip, Z_HI * rank_f)
     gram, packed = call(
         first_kernel,
         [shape(mine, total), packed_shape],
-        [VMEM] * 3,
-        [x.reshape(-1, LANES) for x in sides] + [basis],
+        [VMEM] * 2,
+        (pieces, shards),
+        [pltpu.VMEM((total // Z_HI, Z_HI * rank_f), F32)],
     )
     for step in range(ITERS):
         packed = lax.all_to_all(packed, ("x", "c"), 0, 0, tiled=True)

time: 286 us -> 248 us (0.87)
  waiting for transfers between devices: 76.5 us -> 27.6 us
  blocking collectives: 104 us -> 123 us
  between operations: 14.3 us -> 1 us
  starting transfers between devices: 56.2 us -> 66.3 us
  local copies, waits for them, and re-layouts: 9.02 us -> 3.14 us
  Pallas kernels: 17.1 us -> 21.9 us
    all_to_all x3 -> x0, waiting for transfers between devices: 33.8 us -> none  [the longest x2 22.8 us: spread(): return lax.all_to_all(copies, axes, 0, 0, tiled=True)]
    all_to_all x3 -> x0, starting transfers between devices: 23.4 us -> none  [the longest x2 17 us: spread(): return lax.all_to_all(copies, axes, 0, 0, tiled=True)]
    ppermute x0 -> x6, starting transfers between devices: none -> 21.6 us  [shift(): return lax.ppermute(x, 'x', [(i, (i + by) % N_X) for i in range(N_X)])]
    all_to_all x5 -> x4, blocking collectives: 78.2 us -> 98.6 us  [the longest x2 59.5 us: trade(): rows = lax.all_to_all(x.reshape(count, 1, -1), axes, 0, 0, tiled=True)]
    all_to_all x1, waiting for transfers between devices: 19.9 us -> 0.42 us  [local(): lax.all_to_all(mid, PLANE, 0, 0, tiled=True).reshape(Z_HI, total, cols)]
    reduce_scatter x1 -> x0, waiting for transfers between devices: 13.2 us -> none  [local(): mid = lax.psum_scatter(mid, 'x', scatter_dimension=0, tiled=True)]
    ppermute x3, waiting for transfers between devices: 3.17 us -> 12.2 us  [swap(): return lax.ppermute(x, axis, [(0, 1), (1, 0)])]
    ppermute x0 -> x6, waiting for transfers between devices: none -> 8.6 us  [shift(): return lax.ppermute(x, 'x', [(i, (i + by) % N_X) for i in range(N_X)])]
  transfers between devices with their start and end apart: 9 -> 11, of which waited for: 8 -> 9; matrix products, arithmetic and copies ran while one was open for 2% -> 0% of each run, Pallas kernels for 0% -> 1%
where the time goes in v2:
time: 248 us; the launch traced here: 246 us
  blocking collectives  123 us (50%)
  starting transfers between devices  66.3 us (27%)
  waiting for transfers between devices  27.6 us (11%)
  Pallas kernels  21.9 us (9%)
  matrix products  3.66 us (1%)
  local copies, waits for them, and re-layouts  3.14 us (1%)
    all_to_all x2, blocking collectives, trade(): rows = lax.all_to_all(x.reshape(count, 1, -1), axes, 0, 0, tiled=True)  59.5 us
    all_to_all x2, blocking collectives, local(): packed = lax.all_to_all(packed, ('x', 'c'), 0, 0, tiled=True)  24 us
    pallas_call x15, Pallas kernels, call(): pl.pallas_call(kernel, out_shape=outs, in_specs=ins, out_specs=jax.tree.m...  21.9 us
    ppermute x3, starting transfers between devices, swap(): return lax.ppermute(x, axis, [(0, 1), (1, 0)])  21.8 us
    ppermute x6, starting transfers between devices, shift(): return lax.ppermute(x, 'x', [(i, (i + by) % N_X) for i in range(N_X)])  21.6 us
    all_to_all x1, blocking collectives, local(): shards = lax.all_to_all(start, FRM, 0, 0, tiled=True).reshape(-1, LANES)  19.8 us
    all_to_all x1, blocking collectives, local(): blocks = lax.all_to_all(copies, 'x', 0, 0, tiled=True)  19.3 us
    all_to_all x1, starting transfers between devices, local(): lax.all_to_all(mid, PLANE, 0, 0, tiled=True).reshape(Z_HI, total, cols)  18.8 us
  transfers between devices with their start and end apart: 11, of which 9 were waited for; matrix products, arithmetic and copies ran while one was open for 0% of the time, Pallas kernels for 1%

profile of v2, /device:TPU:1, one launch (start us, length us, event | category | flops | bytes accessed | tf_op | source)
XLA Modules:
  0.0 246.4 jit_solution(2992904234424837518)
XLA Ops:
  1.6 3.7 %convert_bitcast_fusion.mid = bf16[40,256,128]{2,1,0:T(8,128)(2,1)S(1)} fusion(bf16[40,384,128]{2,1,0:T(8,128)(2,1)} %param.4, bf16[384,256]{1,0:T(8,128)(2,1)S(1)} %copy-done), kind=kOutput, calls=%fused_computation | convolution fusion | flops 1007943680 | bytes 6750208 | tf_op jit(solution)/shard_map/fhw,hr->frw/dot_general | solution.py:270
  5.9 3.9 %collective-permute-start = (bf16[20,64,128]{2,1,0:T(8,128)(2,1)S(1)}, bf16[20,64,128]{2,1,0:T(8,128)(2,1)S(1)}, u32[]{:S(2)}, u32[]{:S(2)}) collective-permute-start(bf16[20,64,128]{2,1,0:T(8,128)(2,1)S(1)} %get-tuple-element.16), channel_id=1, source_target_pairs={{0,4},{4,8},{8,12},{12,0},{1,5},{5,9},{9,13},{13,1},{2,6},{6,10},{... | collective-permute-start | bytes 983048 | tf_op jit(solution)/shard_map/ppermute | solution.py:234
  9.9 3.2 %collective-permute-start.3 = (bf16[20,64,128]{2,1,0:T(8,128)(2,1)S(1)}, bf16[20,64,128]{2,1,0:T(8,128)(2,1)S(1)}, u32[]{:S(2)}, u32[]{:S(2)}) collective-permute-start(bf16[20,64,128]{2,1,0:T(8,128)(2,1)S(1)} %get-tuple-element.17), channel_id=1, source_target_pairs={{0,12},{4,0},{8,4},{12,8},{1,13},{5,1},{9,5},{13,9},{2,14},{6,2},{... | collective-permute-start | bytes 983048 | tf_op jit(solution)/shard_map/ppermute | solution.py:234
  13.1 2.5 %collective-permute-done.came = bf16[20,64,128]{2,1,0:T(8,128)(2,1)S(1)} collective-permute-done((bf16[20,64,128]{2,1,0:T(8,128)(2,1)S(1)}, bf16[20,64,128]{2,1,0:T(8,128)(2,1)S(1)}, u32[]{:S(2)}, u32[]{:S(2)}) %collective-permute-start) | collective-permute-done | bytes 327712 | tf_op jit(solution)/shard_map/ppermute | solution.py:234
  16.2 3.8 %collective-permute-start.1 = (bf16[20,64,128]{2,1,0:T(8,128)(2,1)S(1)}, bf16[20,64,128]{2,1,0:T(8,128)(2,1)S(1)}, u32[]{:S(2)}, u32[]{:S(2)}) collective-permute-start(bf16[20,64,128]{2,1,0:T(8,128)(2,1)S(1)} %shard_map.60), channel_id=1, source_target_pairs={{0,4},{4,8},{8,12},{12,0},{1,5},{5,9},{9,13},{13,1},{2,6},{6,10},{... | collective-permute-start | bytes 983048 | tf_op jit(solution)/shard_map/ppermute | solution.py:234
  20.6 4.2 %collective-permute-start.4 = (bf16[20,64,128]{2,1,0:T(8,128)(2,1)S(1)}, bf16[20,64,128]{2,1,0:T(8,128)(2,1)S(1)}, u32[]{:S(2)}, u32[]{:S(2)}) collective-permute-start(bf16[20,64,128]{2,1,0:T(8,128)(2,1)S(1)} %shard_map.63), channel_id=1, source_target_pairs={{0,12},{4,0},{8,4},{12,8},{1,13},{5,1},{9,5},{13,9},{2,14},{6,2},{... | collective-permute-start | bytes 983048 | tf_op jit(solution)/shard_map/ppermute | solution.py:234
  24.8 1.9 collective-permute-done.1.came
  27.3 2.8 %collective-permute-start.2 = (bf16[20,64,128]{2,1,0:T(8,128)(2,1)S(1)}, bf16[20,64,128]{2,1,0:T(8,128)(2,1)S(1)}, u32[]{:S(2)}, u32[]{:S(2)}) collective-permute-start(bf16[20,64,128]{2,1,0:T(8,128)(2,1)S(1)} %shard_map.61), channel_id=1, source_target_pairs={{0,4},{4,8},{8,12},{12,0},{1,5},{5,9},{9,13},{13,1},{2,6},{6,10},{... | collective-permute-start | bytes 983048 | tf_op jit(solution)/shard_map/ppermute | solution.py:234
  30.8 3.7 %collective-permute-start.5 = (bf16[20,64,128]{2,1,0:T(8,128)(2,1)S(1)}, bf16[20,64,128]{2,1,0:T(8,128)(2,1)S(1)}, u32[]{:S(2)}, u32[]{:S(2)}) collective-permute-start(bf16[20,64,128]{2,1,0:T(8,128)(2,1)S(1)} %shard_map.64), channel_id=1, source_target_pairs={{0,12},{4,0},{8,4},{12,8},{1,13},{5,1},{9,5},{13,9},{2,14},{6,2},{... | collective-permute-start | bytes 983048 | tf_op jit(solution)/shard_map/ppermute | solution.py:234
  34.5 2.1 collective-permute-done.2.came
  37.3 2.1 collective-permute-done.5.came
  40.0 1.3 copy.10
  41.3 18.8 %all-to-all-start = ((bf16[64,40,128]{2,1,0:T(8,128)(2,1)}), bf16[64,40,128]{2,1,0:T(8,128)(2,1)S(1)}, u32[]{:S(2)}, u32[]{:S(2)}) async-start(bf16[64,40,128]{2,1,0:T(8,128)(2,1)} %copy.10), calls=%async_computation | async-start | bytes 1310720 | tf_op jit(solution)/shard_map/all_to_all | solution.py:277
  60.1 6.9 %collective-permute-start.6 = (bf16[128,256]{1,0:T(8,128)(2,1)S(1)}, bf16[128,256]{1,0:T(8,128)(2,1)S(1)}, u32[]{:S(2)}, u32[]{:S(2)}) collective-permute-start(bf16[128,256]{1,0:T(8,128)(2,1)S(1)} %copy-done.1), channel_id=1, source_target_pairs={{0,2},{2,0},{1,3},{3,1},{4,6},{6,4},{5,7},{7,5},{8,10},{10,8},{9,1... | collective-permute-start | bytes 196616 | tf_op jit(solution)/shard_map/ppermute | solution.py:238
  67.1 9.1 %collective-permute-done.6.width_other = bf16[128,256]{1,0:T(8,128)(2,1)S(1)} collective-permute-done((bf16[128,256]{1,0:T(8,128)(2,1)S(1)}, bf16[128,256]{1,0:T(8,128)(2,1)S(1)}, u32[]{:S(2)}, u32[]{:S(2)}) %collective-permute-start.6) | collective-permute-done | bytes 65568 | tf_op jit(solution)/shard_map/ppermute | solution.py:238
  77.7 8.9 %collective-permute-start.7 = (bf16[1280,128]{1,0:T(8,128)(2,1)S(1)}, bf16[1280,128]{1,0:T(8,128)(2,1)S(1)}, u32[]{:S(2)}, u32[]{:S(2)}) collective-permute-start(bf16[1280,128]{1,0:T(8,128)(2,1)S(1)} %get-tuple-element.21), channel_id=1, source_target_pairs={{0,1},{1,0},{2,3},{3,2},{4,5},{5,4},{6,7},{7,6},{8,9},{9,8},{10,11... | collective-permute-start | bytes 983048 | tf_op jit(solution)/shard_map/ppermute | solution.py:238
  86.7 1.1 collective-permute-done.7.b
  88.1 19.8 %all_to_all.40 = f32[32,1,2560]{2,1,0:T(1,128)S(1)} all-to-all(f32[32,1,2560]{2,1,0:T(1,128)S(1)} %broadcast_in_dim.8), channel_id=1, replica_groups=mesh['y'=8,'zl'=4,'x'=4,'zh'=2,'c'=2] {'y','zl'}, dimensions={0} | all-to-all | bytes 655360 | tf_op jit(solution)/shard_map/all_to_all | solution.py:294
  108.0 19.3 %all_to_all.41.refs_1_ = bf16[4,1280,128]{2,1,0:T(8,128)(2,1)S(1)} all-to-all(bf16[4,1280,128]{2,1,0:T(8,128)(2,1)S(1)} %shard_map.67), channel_id=1, replica_groups=mesh['y'=8,'zl'=4,'x'=4,'zh'=2,'c'=2] {'x'}, dimensions={0} | all-to-all | bytes 2621440 | tf_op jit(solution)/shard_map/all_to_all | solution.py:293
  127.3 1.5 shard_map.68
  128.7 6.0 %collective-permute-start.8 = (f32[20,80,128]{2,1,0:T(8,128)S(1)}, f32[20,80,128]{2,1,0:T(8,128)S(1)}, u32[]{:S(2)}, u32[]{:S(2)}) collective-permute-start(f32[20,80,128]{2,1,0:T(8,128)S(1)} %get-tuple-element.26), channel_id=1, source_target_pairs={{0,1},{1,0},{2,3},{3,2},{4,5},{5,4},{6,7},{7,6},{8,9},{9,8},{10,11... | collective-permute-start | bytes 2457608 | tf_op jit(solution)/shard_map/ppermute | solution.py:238
  134.7 1.9 collective-permute-done.8
  136.7 28.6 %all_to_all.42 = f32[64,1,3200]{2,1,0:T(1,128)S(1)} all-to-all(f32[64,1,3200]{2,1,0:T(1,128)S(1)} %bitcast.34), channel_id=1, replica_groups=mesh['y'=8,'zl'=4,'x'=4,'zh'=2,'c'=2] {'zh','y','zl'}, dimensions={0} | all-to-all | bytes 1638400 | tf_op jit(solution)/shard_map/all_to_all | solution.py:229
  165.5 30.9 %all_to_all.43 = f32[64,1,3200]{2,1,0:T(1,128)S(1)} all-to-all(f32[64,1,3200]{2,1,0:T(1,128)S(1)} %bitcast.28), channel_id=1, replica_groups=mesh['y'=8,'zl'=4,'x'=4,'zh'=2,'c'=2] {'zh','y','zl'}, dimensions={0} | all-to-all | bytes 1638400 | tf_op jit(solution)/shard_map/all_to_all | solution.py:229
  196.4 1.1 shard_map.70
  197.5 13.3 %all_to_all.44 = f32[8,80,128]{2,1,0:T(8,128)S(1)} all-to-all(f32[8,80,128]{2,1,0:T(8,128)S(1)} %get-tuple-element.29), channel_id=1, replica_groups=mesh['y'=8,'zl'=4,'x'=4,'zh'=2,'c'=2] {'x','c'}, dimensions={0} | all-to-all | bytes 655360 | tf_op jit(solution)/shard_map/all_to_all | solution.py:325
  210.8 4.4 %shard_map.71 = f32[8,80,128]{2,1,0:T(8,128)S(1)} custom-call(f32[640,128]{1,0:T(8,128)S(1)} %bitcast.32, f32[160,1280]{1,0:T(8,128)S(1)} %get-tuple-element.28.gram), custom_call_target="tpu_custom_call" | custom-call | tf_op jit(solution)/shard_map/pallas_call | solution.py:217
  215.2 10.6 %all_to_all.45 = f32[8,80,128]{2,1,0:T(8,128)S(1)} all-to-all(f32[8,80,128]{2,1,0:T(8,128)S(1)} %shard_map.71), channel_id=1, replica_groups=mesh['y'=8,'zl'=4,'x'=4,'zh'=2,'c'=2] {'x','c'}, dimensions={0} | all-to-all | bytes 655360 | tf_op jit(solution)/shard_map/all_to_all | solution.py:325
  225.8 5.1 %shard_map.72 = f32[8,80,128]{2,1,0:T(8,128)} custom-call(f32[640,128]{1,0:T(8,128)S(1)} %bitcast.33, f32[160,1280]{1,0:T(8,128)S(1)} %get-tuple-element.28.gram), custom_call_target="tpu_custom_call" | custom-call | tf_op jit(solution)/shard_map/pallas_call | solution.py:217
  231.0 4.1 %all-to-all-start.7 = ((f32[8,80,128]{2,1,0:T(8,128)}), f32[8,80,128]{2,1,0:T(8,128)S(1)}, u32[]{:S(2)}, u32[]{:S(2)}) async-start(f32[8,80,128]{2,1,0:T(8,128)} %shard_map.72), calls=%async_computation.7 | async-start | bytes 655360 | tf_op jit(solution)/shard_map/all_to_all | solution.py:325
  235.8 6.4 %all-to-all-done.7 = f32[8,80,128]{2,1,0:T(8,128)S(1)} async-done(((f32[8,80,128]{2,1,0:T(8,128)}), f32[8,80,128]{2,1,0:T(8,128)S(1)}, u32[]{:S(2)}, u32[]{:S(2)}) %all-to-all-start.7) | async-done | bytes 327712 | tf_op jit(solution)/shard_map/all_to_all | solution.py:325
  242.2 4.2 %shard_map.73 = f32[40,64]{1,0:T(8,128)} custom-call(s32[5]{0:T(128)S(1)} %stack.23.at.refs_0_, f32[640,128]{1,0:T(8,128)S(1)} %bitcast.30), custom_call_target="tpu_custom_call" | custom-call | tf_op jit(solution)/shard_map/pallas_call | solution.py:217
  (27 shorter events, 8.2 us)
Async XLA Ops:
  0.6 0.9 copy-start
  5.9 9.7 %collective-permute-start = (bf16[20,64,128]{2,1,0:T(8,128)(2,1)S(1)}, bf16[20,64,128]{2,1,0:T(8,128)(2,1)S(1)}, u32[]{:S(2)}, u32[]{:S(2)}) collective-permute-start(bf16[20,64,128]{2,1,0:T(8,128)(2,1)S(1)} %get-tuple-element.16), channel_id=1, source_target_pairs={{0,4},{4,8},{8,12},{12,0},{1,5},{5,9},{9,13},{13,1},{2,6},{6,10},{... | collective-permute-start | bytes 983048 | tf_op jit(solution)/shard_map/ppermute | solution.py:234
  9.9 10.1 %collective-permute-start.3 = (bf16[20,64,128]{2,1,0:T(8,128)(2,1)S(1)}, bf16[20,64,128]{2,1,0:T(8,128)(2,1)S(1)}, u32[]{:S(2)}, u32[]{:S(2)}) collective-permute-start(bf16[20,64,128]{2,1,0:T(8,128)(2,1)S(1)} %get-tuple-element.17), channel_id=1, source_target_pairs={{0,12},{4,0},{8,4},{12,8},{1,13},{5,1},{9,5},{13,9},{2,14},{6,2},{... | collective-permute-start | bytes 983048 | tf_op jit(solution)/shard_map/ppermute | solution.py:234
  16.2 10.5 %collective-permute-start.1 = (bf16[20,64,128]{2,1,0:T(8,128)(2,1)S(1)}, bf16[20,64,128]{2,1,0:T(8,128)(2,1)S(1)}, u32[]{:S(2)}, u32[]{:S(2)}) collective-permute-start(bf16[20,64,128]{2,1,0:T(8,128)(2,1)S(1)} %shard_map.60), channel_id=1, source_target_pairs={{0,4},{4,8},{8,12},{12,0},{1,5},{5,9},{9,13},{13,1},{2,6},{6,10},{... | collective-permute-start | bytes 983048 | tf_op jit(solution)/shard_map/ppermute | solution.py:234
  20.6 9.5 %collective-permute-start.4 = (bf16[20,64,128]{2,1,0:T(8,128)(2,1)S(1)}, bf16[20,64,128]{2,1,0:T(8,128)(2,1)S(1)}, u32[]{:S(2)}, u32[]{:S(2)}) collective-permute-start(bf16[20,64,128]{2,1,0:T(8,128)(2,1)S(1)} %shard_map.63), channel_id=1, source_target_pairs={{0,12},{4,0},{8,4},{12,8},{1,13},{5,1},{9,5},{13,9},{2,14},{6,2},{... | collective-permute-start | bytes 983048 | tf_op jit(solution)/shard_map/ppermute | solution.py:234
  27.3 9.3 %collective-permute-start.2 = (bf16[20,64,128]{2,1,0:T(8,128)(2,1)S(1)}, bf16[20,64,128]{2,1,0:T(8,128)(2,1)S(1)}, u32[]{:S(2)}, u32[]{:S(2)}) collective-permute-start(bf16[20,64,128]{2,1,0:T(8,128)(2,1)S(1)} %shard_map.61), channel_id=1, source_target_pairs={{0,4},{4,8},{8,12},{12,0},{1,5},{5,9},{9,13},{13,1},{2,6},{6,10},{... | collective-permute-start | bytes 983048 | tf_op jit(solution)/shard_map/ppermute | solution.py:234
  30.8 8.6 %collective-permute-start.5 = (bf16[20,64,128]{2,1,0:T(8,128)(2,1)S(1)}, bf16[20,64,128]{2,1,0:T(8,128)(2,1)S(1)}, u32[]{:S(2)}, u32[]{:S(2)}) collective-permute-start(bf16[20,64,128]{2,1,0:T(8,128)(2,1)S(1)} %shard_map.64), channel_id=1, source_target_pairs={{0,12},{4,0},{8,4},{12,8},{1,13},{5,1},{9,5},{13,9},{2,14},{6,2},{... | collective-permute-start | bytes 983048 | tf_op jit(solution)/shard_map/ppermute | solution.py:234
  37.2 22.9 %copy-start.1 = (bf16[128,256]{1,0:T(8,128)(2,1)S(1)}, bf16[128,256]{1,0:T(8,128)(2,1)}, u32[]{:S(2)}) copy-start(bf16[128,256]{1,0:T(8,128)(2,1)} %width) | copy-start | bytes 196612
  37.2 49.4 %copy-start.2 = (f32[40,64]{1,0:T(8,128)S(1)}, f32[40,64]{1,0:T(8,128)}, u32[]{:S(2)}) copy-start(f32[40,64]{1,0:T(8,128)} %param.7) | copy-start | bytes 30724
  41.3 35.3 %all-to-all-start = ((bf16[64,40,128]{2,1,0:T(8,128)(2,1)}), bf16[64,40,128]{2,1,0:T(8,128)(2,1)S(1)}, u32[]{:S(2)}, u32[]{:S(2)}) async-start(bf16[64,40,128]{2,1,0:T(8,128)(2,1)} %copy.10), calls=%async_computation | async-start | bytes 1310720 | tf_op jit(solution)/shard_map/all_to_all | solution.py:277
  60.1 16.1 %collective-permute-start.6 = (bf16[128,256]{1,0:T(8,128)(2,1)S(1)}, bf16[128,256]{1,0:T(8,128)(2,1)S(1)}, u32[]{:S(2)}, u32[]{:S(2)}) collective-permute-start(bf16[128,256]{1,0:T(8,128)(2,1)S(1)} %copy-done.1), channel_id=1, source_target_pairs={{0,2},{2,0},{1,3},{3,1},{4,6},{6,4},{5,7},{7,5},{8,10},{10,8},{9,1... | collective-permute-start | bytes 196616 | tf_op jit(solution)/shard_map/ppermute | solution.py:238
  77.7 10.2 %collective-permute-start.7 = (bf16[1280,128]{1,0:T(8,128)(2,1)S(1)}, bf16[1280,128]{1,0:T(8,128)(2,1)S(1)}, u32[]{:S(2)}, u32[]{:S(2)}) collective-permute-start(bf16[1280,128]{1,0:T(8,128)(2,1)S(1)} %get-tuple-element.21), channel_id=1, source_target_pairs={{0,1},{1,0},{2,3},{3,2},{4,5},{5,4},{6,7},{7,6},{8,9},{9,8},{10,11... | collective-permute-start | bytes 983048 | tf_op jit(solution)/shard_map/ppermute | solution.py:238
  128.7 7.9 %collective-permute-start.8 = (f32[20,80,128]{2,1,0:T(8,128)S(1)}, f32[20,80,128]{2,1,0:T(8,128)S(1)}, u32[]{:S(2)}, u32[]{:S(2)}) collective-permute-start(f32[20,80,128]{2,1,0:T(8,128)S(1)} %get-tuple-element.26), channel_id=1, source_target_pairs={{0,1},{1,0},{2,3},{3,2},{4,5},{5,4},{6,7},{7,6},{8,9},{9,8},{10,11... | collective-permute-start | bytes 2457608 | tf_op jit(solution)/shard_map/ppermute | solution.py:238
  231.0 11.2 %all-to-all-start.7 = ((f32[8,80,128]{2,1,0:T(8,128)}), f32[8,80,128]{2,1,0:T(8,128)S(1)}, u32[]{:S(2)}, u32[]{:S(2)}) async-start(f32[8,80,128]{2,1,0:T(8,128)} %shard_map.72), calls=%async_computation.7 | async-start | bytes 655360 | tf_op jit(solution)/shard_map/all_to_all | solution.py:325

commit v3 on v2

--- a/solution.py
+++ b/solution.py
@@ -42,6 +42,10 @@
         out[f] = own
 
 
+def add_kernel(a, b, out):
+    out[...] = (a[...].astype(F32) + b[...].astype(F32)).astype(out.dtype)
+
+
 def core_kernel(at, mid, width, width_other, own, sent):
     half = own.shape[1]
     zh = at[4]
@@ -62,14 +66,9 @@
         sent[...] = low
 
 
-def copies_kernel(a, b, out):
-    total = (a[...].astype(F32) + b[...].astype(F32)).astype(out.dtype)
-    for j in range(out.shape[0]):
-        out[j] = total
-
-
-def gram_kernel(scale, at, blocks, kept, sent, core, acc):
-    _, total, depth = blocks.shape
+def gram_kernel(scale, at, own, left, right, far_a, far_b, kept, sent, core, acc):
+    total, depth = own.shape
+    far = total // 2
     strip = kept.shape[1]
     for j in range(N_X):
         for x in range(N_X):
@@ -77,8 +76,13 @@
                 for c in range(CORES):
                     source = ((x * Z_HI + zh) * CORES + c) * strip
                     place = ((zh * N_X + x) * CORES + c) * strip
-                    core[place : place + strip, j * depth : (j + 1) * depth] = blocks[
-                        j, source : source + strip, :
+                    if j == N_X - 1:
+                        block = far_a if source < far else far_b
+                        source = source % far
+                    else:
+                        block = (own, left, right)[j]
+                    core[place : place + strip, j * depth : (j + 1) * depth] = block[
+                        source : source + strip, :
                     ]
     rows = []
     for zh in range(Z_HI):
@@ -105,13 +109,31 @@
                 sent[tile * Z_HI + zh] = acc[pl.ds(send_at, strip), lanes]
 
 
-def sum_kernel(rows, parts, out):
-    count = parts.shape[0] // rows
-    total = parts[0:rows, :]
-    for j in range(1, count):
-        total = total + parts[j * rows : (j + 1) * rows, :]
-    for j in range(count):
-        out[j * rows : (j + 1) * rows, :] = total
+def put_scaled(x, out, base, rows, step):
+    largest = jnp.max(jnp.max(jnp.abs(x), axis=0, keepdims=True), axis=1, keepdims=True)
+    exponent = jnp.floor(jnp.log2(jnp.maximum(largest, 2.0**-100))) - 14.0
+    scale = jnp.exp2(-exponent)
+    tail = jnp.broadcast_to(exponent, (step - rows, x.shape[1]))
+    for j in range(x.shape[0] // rows):
+        at = base + j * step
+        out[at : at + rows, :] = x[j * rows : (j + 1) * rows, :] * scale
+        out[at + rows : at + step, :] = tail
+
+
+def pack_kernel(rows, step, a, b, out):
+    put_scaled(a[...] + b[...], out, 0, rows, step)
+
+
+def unscaled(parts, j, rows, step):
+    at = j * step
+    return parts[at : at + rows, :] * jnp.exp2(parts[at + rows : at + rows + 1, :])
+
+
+def sum_kernel(rows, step, parts, out):
+    total = unscaled(parts, 0, rows, step)
+    for j in range(1, parts.shape[0] // step):
+        total = total + unscaled(parts, j, rows, step)
+    put_scaled(total, out, 0, rows, step)
 
 
 def put_product(gram, basis, out):
@@ -126,7 +148,9 @@
         out[j] = packed
 
 
-def first_kernel(flat, shards, gram, out, basis):
+def first_kernel(rows, step, pieces, shards, gram, out, flat, basis):
+    for j in range(pieces.shape[0] // step):
+        flat[j * rows : (j + 1) * rows, :] = unscaled(pieces, j, rows, step)
     mine, total = gram.shape
     for t in range(total // LANES):
         gram[:, t * LANES : (t + 1) * LANES] = flat[t * mine : (t + 1) * mine, :]
@@ -224,10 +248,9 @@
     )(*args)
 
 
-def trade(x, axes):
-    count = lax.axis_size(axes)
-    rows = lax.all_to_all(x.reshape(count, 1, -1), axes, 0, 0, tiled=True)
-    return rows.reshape(x.shape)
+def trade(x, count, axes):
+    blocks = lax.all_to_all(x.reshape(count, -1, LANES), axes, 0, 0, tiled=True)
+    return blocks.reshape(-1, LANES).astype(F32)
 
 
 def shift(x, by):
@@ -283,23 +306,25 @@
         (at, mid, width, width_other),
     )
 
-    copies = call(
-        copies_kernel, shape(N_X, total, half, dtype=mid.dtype), [VMEM] * 2, (own, swap(sent, "c"))
-    )
+    core = call(
+        add_kernel, shape(total, half, dtype=mid.dtype), [VMEM] * 2, (own, swap(sent, "c"))
+    )
+
     part = frames_dev // 2
     start = jnp.concatenate([start_basis[:part], start_basis[part:]], axis=1).reshape(1, -1)
     start = jnp.broadcast_to(start[None], (lax.axis_size(FRM),) + start.shape)
-    copies, start = lax.optimization_barrier((copies, start))
-    blocks = lax.all_to_all(copies, "x", 0, 0, tiled=True)
+    core, start = lax.optimization_barrier((core, start))
+    left, right = shift(core, 1), shift(core, -1)
     shards = lax.all_to_all(start, FRM, 0, 0, tiled=True).reshape(-1, LANES)
-    blocks, shards = lax.optimization_barrier((blocks, shards))
+    far_a, far_b = shift(left[: total // 2], 1), shift(right[total // 2 :], -1)
+    far_a, far_b, shards = lax.optimization_barrier((far_a, far_b, shards))
     mine = Z_HI * strip
     tiles = total // LANES
     kept, sent = call(
         lambda *refs: gram_kernel(1.0 / (rank_h * rank_w), *refs),
         [shape(tiles * Z_HI, strip, LANES)] * 2,
-        [SMEM, VMEM],
-        (at, blocks),
+        [SMEM] + [VMEM] * 5,
+        (at, core, left, right, far_a, far_b),
         [
             pltpu.VMEM((total, N_X * half), jnp.bfloat16),
             pltpu.VMEM((total // N_X, 2 * LANES), F32),
@@ -308,18 +333,29 @@
     came = swap(sent, "c")
 
     flat = shape(tiles * mine, LANES)
-    pieces = trade(kept.reshape(flat.shape) + came.reshape(flat.shape), PLANE)
-    rows = flat.shape[0] // lax.axis_size(PLANE)
-    pieces = call(lambda *refs: sum_kernel(rows, *refs), flat, [VMEM], (pieces,))
-    pieces = trade(pieces, PLANE)
+    count = lax.axis_size(PLANE)
+    rows = flat.shape[0] // count
+    step = -(-(rows + 1) // 16) * 16
+    pieces = call(
+        lambda *refs: pack_kernel(rows, step, *refs),
+        shape(count * step, LANES),
+        [VMEM] * 2,
+        (kept.reshape(flat.shape), came.reshape(flat.shape)),
+    )
+    pieces = trade(pieces.astype(jnp.float16), count, PLANE)
+    piece = call(
+        lambda *refs: sum_kernel(rows, step, *refs), shape(step, LANES), [VMEM], (pieces,)
+    )
+    piece = piece.astype(jnp.float16)
+    pieces = trade(jnp.broadcast_to(piece[None], (count,) + piece.shape), count, PLANE)
 
     packed_shape = shape(N_X * CORES, strip, Z_HI * rank_f)
     gram, packed = call(
-        first_kernel,
+        lambda *refs: first_kernel(rows, step, *refs),
         [shape(mine, total), packed_shape],
         [VMEM] * 2,
         (pieces, shards),
-        [pltpu.VMEM((total // Z_HI, Z_HI * rank_f), F32)],
+        [pltpu.VMEM(flat.shape, F32), pltpu.VMEM((total // Z_HI, Z_HI * rank_f), F32)],
     )
     for step in range(ITERS):
         packed = lax.all_to_all(packed, ("x", "c"), 0, 0, tiled=True)

time: 248 us -> 231 us (0.931)
  blocking collectives: 123 us -> 77.7 us
  starting transfers between devices: 66.3 us -> 85.1 us
  waiting for transfers between devices: 27.6 us -> 35.4 us
    all_to_all x4 -> x2, blocking collectives: 98.6 us -> 51.1 us  [trade(): blocks = lax.all_to_all(x.reshape(count, -1, LANES), axes, 0, 0, tiled=True)]
    ppermute x6 -> x10, starting transfers between devices: 21.6 us -> 35.3 us  [shift(): return lax.ppermute(x, 'x', [(i, (i + by) % N_X) for i in range(N_X)])]
    ppermute x6 -> x10, waiting for transfers between devices: 8.6 us -> 16.4 us  [shift(): return lax.ppermute(x, 'x', [(i, (i + by) % N_X) for i in range(N_X)])]
    all_to_all x0 -> x1, starting transfers between devices: none -> 6.86 us  [local(): shards = lax.all_to_all(start, FRM, 0, 0, tiled=True).reshape(-1, LANES)]
    all_to_all x2, blocking collectives: 24 us -> 26.6 us  [local(): packed = lax.all_to_all(packed, ('x', 'c'), 0, 0, tiled=True)]
    pallas_call x15 -> x16, Pallas kernels: 21.9 us -> 22.4 us  [call(): pl.pallas_call(kernel, out_shape=outs, in_specs=ins, out_specs=jax.tree.m...]
  transfers between devices with their start and end apart: 11 -> 16, of which waited for: 9 -> 12; matrix products, arithmetic and copies ran while one was open for 0% -> 0% of each run, Pallas kernels for 1% -> 1%
where the time goes in v3:
time: 231 us; the launch traced here: 230 us
  starting transfers between devices  85.1 us (37%)
  blocking collectives  77.7 us (34%)
  waiting for transfers between devices  35.4 us (15%)
  Pallas kernels  22.4 us (10%)
  local copies, waits for them, and re-layouts  3.98 us (2%)
  matrix products  3.66 us (2%)
    all_to_all x2, blocking collectives, trade(): blocks = lax.all_to_all(x.reshape(count, -1, LANES), axes, 0, 0, tiled=True)  51.1 us
    ppermute x10, starting transfers between devices, shift(): return lax.ppermute(x, 'x', [(i, (i + by) % N_X) for i in range(N_X)])  35.3 us
    all_to_all x2, blocking collectives, local(): packed = lax.all_to_all(packed, ('x', 'c'), 0, 0, tiled=True)  26.6 us
    pallas_call x16, Pallas kernels, call(): pl.pallas_call(kernel, out_shape=outs, in_specs=ins, out_specs=jax.tree.m...  22.4 us
    ppermute x3, starting transfers between devices, swap(): return lax.ppermute(x, axis, [(0, 1), (1, 0)])  20.1 us
    all_to_all x1, starting transfers between devices, local(): lax.all_to_all(mid, PLANE, 0, 0, tiled=True).reshape(Z_HI, total, cols)  18.8 us
    ppermute x10, waiting for transfers between devices, shift(): return lax.ppermute(x, 'x', [(i, (i + by) % N_X) for i in range(N_X)])  16.4 us
    ppermute x3, waiting for transfers between devices, swap(): return lax.ppermute(x, axis, [(0, 1), (1, 0)])  12.2 us
  transfers between devices with their start and end apart: 16, of which 12 were waited for; matrix products, arithmetic and copies ran while one was open for 0% of the time, Pallas kernels for 1%

profile of v3, /device:TPU:1, one launch (start us, length us, event | category | flops | bytes accessed | tf_op | source)
XLA Modules:
  0.0 229.7 jit_solution(2236357613945248011)
XLA Ops:
  1.6 3.7 %convert_bitcast_fusion.mid = bf16[40,256,128]{2,1,0:T(8,128)(2,1)S(1)} fusion(bf16[40,384,128]{2,1,0:T(8,128)(2,1)} %param.4, bf16[384,256]{1,0:T(8,128)(2,1)S(1)} %copy-done), kind=kOutput, calls=%fused_computation | convolution fusion | flops 1007943680 | bytes 6750208 | tf_op jit(solution)/shard_map/fhw,hr->frw/dot_general | solution.py:293
  5.9 3.9 %collective-permute-start = (bf16[20,64,128]{2,1,0:T(8,128)(2,1)S(1)}, bf16[20,64,128]{2,1,0:T(8,128)(2,1)S(1)}, u32[]{:S(2)}, u32[]{:S(2)}) collective-permute-start(bf16[20,64,128]{2,1,0:T(8,128)(2,1)S(1)} %get-tuple-element.17), channel_id=1, source_target_pairs={{0,4},{4,8},{8,12},{12,0},{1,5},{5,9},{9,13},{13,1},{2,6},{6,10},{... | collective-permute-start | bytes 983048 | tf_op jit(solution)/shard_map/ppermute | solution.py:257
  9.9 3.2 %collective-permute-start.3 = (bf16[20,64,128]{2,1,0:T(8,128)(2,1)S(1)}, bf16[20,64,128]{2,1,0:T(8,128)(2,1)S(1)}, u32[]{:S(2)}, u32[]{:S(2)}) collective-permute-start(bf16[20,64,128]{2,1,0:T(8,128)(2,1)S(1)} %get-tuple-element.18), channel_id=1, source_target_pairs={{0,12},{4,0},{8,4},{12,8},{1,13},{5,1},{9,5},{13,9},{2,14},{6,2},{... | collective-permute-start | bytes 983048 | tf_op jit(solution)/shard_map/ppermute | solution.py:257
  13.1 2.5 %collective-permute-done.came = bf16[20,64,128]{2,1,0:T(8,128)(2,1)S(1)} collective-permute-done((bf16[20,64,128]{2,1,0:T(8,128)(2,1)S(1)}, bf16[20,64,128]{2,1,0:T(8,128)(2,1)S(1)}, u32[]{:S(2)}, u32[]{:S(2)}) %collective-permute-start) | collective-permute-done | bytes 327712 | tf_op jit(solution)/shard_map/ppermute | solution.py:257
  16.2 3.8 %collective-permute-start.1 = (bf16[20,64,128]{2,1,0:T(8,128)(2,1)S(1)}, bf16[20,64,128]{2,1,0:T(8,128)(2,1)S(1)}, u32[]{:S(2)}, u32[]{:S(2)}) collective-permute-start(bf16[20,64,128]{2,1,0:T(8,128)(2,1)S(1)} %shard_map.60), channel_id=1, source_target_pairs={{0,4},{4,8},{8,12},{12,0},{1,5},{5,9},{9,13},{13,1},{2,6},{6,10},{... | collective-permute-start | bytes 983048 | tf_op jit(solution)/shard_map/ppermute | solution.py:257
  20.6 4.2 %collective-permute-start.4 = (bf16[20,64,128]{2,1,0:T(8,128)(2,1)S(1)}, bf16[20,64,128]{2,1,0:T(8,128)(2,1)S(1)}, u32[]{:S(2)}, u32[]{:S(2)}) collective-permute-start(bf16[20,64,128]{2,1,0:T(8,128)(2,1)S(1)} %shard_map.63), channel_id=1, source_target_pairs={{0,12},{4,0},{8,4},{12,8},{1,13},{5,1},{9,5},{13,9},{2,14},{6,2},{... | collective-permute-start | bytes 983048 | tf_op jit(solution)/shard_map/ppermute | solution.py:257
  24.8 1.9 collective-permute-done.1.came
  27.3 2.8 %collective-permute-start.2 = (bf16[20,64,128]{2,1,0:T(8,128)(2,1)S(1)}, bf16[20,64,128]{2,1,0:T(8,128)(2,1)S(1)}, u32[]{:S(2)}, u32[]{:S(2)}) collective-permute-start(bf16[20,64,128]{2,1,0:T(8,128)(2,1)S(1)} %shard_map.61), channel_id=1, source_target_pairs={{0,4},{4,8},{8,12},{12,0},{1,5},{5,9},{9,13},{13,1},{2,6},{6,10},{... | collective-permute-start | bytes 983048 | tf_op jit(solution)/shard_map/ppermute | solution.py:257
  30.8 3.7 %collective-permute-start.5 = (bf16[20,64,128]{2,1,0:T(8,128)(2,1)S(1)}, bf16[20,64,128]{2,1,0:T(8,128)(2,1)S(1)}, u32[]{:S(2)}, u32[]{:S(2)}) collective-permute-start(bf16[20,64,128]{2,1,0:T(8,128)(2,1)S(1)} %shard_map.64), channel_id=1, source_target_pairs={{0,12},{4,0},{8,4},{12,8},{1,13},{5,1},{9,5},{13,9},{2,14},{6,2},{... | collective-permute-start | bytes 983048 | tf_op jit(solution)/shard_map/ppermute | solution.py:257
  34.5 2.1 collective-permute-done.2.came
  37.3 2.1 collective-permute-done.5.came
  41.3 18.8 %all-to-all-start = ((bf16[64,40,128]{2,1,0:T(8,128)(2,1)}), bf16[64,40,128]{2,1,0:T(8,128)(2,1)S(1)}, u32[]{:S(2)}, u32[]{:S(2)}) async-start(bf16[64,40,128]{2,1,0:T(8,128)(2,1)} %copy.10), calls=%async_computation | async-start | bytes 1310720 | tf_op jit(solution)/shard_map/all_to_all | solution.py:300
  60.1 6.9 %collective-permute-start.6 = (bf16[128,256]{1,0:T(8,128)(2,1)S(1)}, bf16[128,256]{1,0:T(8,128)(2,1)S(1)}, u32[]{:S(2)}, u32[]{:S(2)}) collective-permute-start(bf16[128,256]{1,0:T(8,128)(2,1)S(1)} %copy-done.1), channel_id=1, source_target_pairs={{0,2},{2,0},{1,3},{3,1},{4,6},{6,4},{5,7},{7,5},{8,10},{10,8},{9,1... | collective-permute-start | bytes 196616 | tf_op jit(solution)/shard_map/ppermute | solution.py:261
  67.1 9.1 %collective-permute-done.6.width_other = bf16[128,256]{1,0:T(8,128)(2,1)S(1)} collective-permute-done((bf16[128,256]{1,0:T(8,128)(2,1)S(1)}, bf16[128,256]{1,0:T(8,128)(2,1)S(1)}, u32[]{:S(2)}, u32[]{:S(2)}) %collective-permute-start.6) | collective-permute-done | bytes 65568 | tf_op jit(solution)/shard_map/ppermute | solution.py:261
  77.7 8.9 %collective-permute-start.7 = (bf16[1280,128]{1,0:T(8,128)(2,1)S(1)}, bf16[1280,128]{1,0:T(8,128)(2,1)S(1)}, u32[]{:S(2)}, u32[]{:S(2)}) collective-permute-start(bf16[1280,128]{1,0:T(8,128)(2,1)S(1)} %get-tuple-element.22), channel_id=1, source_target_pairs={{0,1},{1,0},{2,3},{3,2},{4,5},{5,4},{6,7},{7,6},{8,9},{9,8},{10,11... | collective-permute-start | bytes 983048 | tf_op jit(solution)/shard_map/ppermute | solution.py:261
  88.9 6.9 %all-to-all-start.1 = ((f32[32,1,2560]{2,1,0:T(1,128)}), f32[32,1,2560]{2,1,0:T(1,128)S(1)}, u32[]{:S(2)}, u32[]{:S(2)}) async-start(f32[32,1,2560]{2,1,0:T(1,128)} %broadcast_in_dim.14), calls=%async_computation.1 | async-start | bytes 655360 | tf_op jit(solution)/shard_map/all_to_all | solution.py:318
  95.7 1.9 collective-permute-start.8
  97.7 5.3 %collective-permute-start.9 = (bf16[1280,128]{1,0:T(8,128)(2,1)S(1)}, bf16[1280,128]{1,0:T(8,128)(2,1)S(1)}, u32[]{:S(2)}, u32[]{:S(2)}) collective-permute-start(bf16[1280,128]{1,0:T(8,128)(2,1)S(1)} %shard_map.67.refs_1_), channel_id=1, source_target_pairs={{0,12},{4,0},{8,4},{12,8},{1,13},{5,1},{9,5},{13,9},{2,14},{6,2},{... | collective-permute-start | bytes 983048 | tf_op jit(solution)/shard_map/ppermute | solution.py:257
  103.0 5.5 %collective-permute-done.8.refs_2_ = bf16[1280,128]{1,0:T(8,128)(2,1)S(1)} collective-permute-done((bf16[1280,128]{1,0:T(8,128)(2,1)S(1)}, bf16[1280,128]{1,0:T(8,128)(2,1)S(1)}, u32[]{:S(2)}, u32[]{:S(2)}) %collective-permute-start.8) | collective-permute-done | bytes 327712 | tf_op jit(solution)/shard_map/ppermute | solution.py:257
  108.5 1.9 collective-permute-start.10
  110.5 4.6 %collective-permute-start.11 = (bf16[640,128]{1,0:T(8,128)(2,1)S(1)}, bf16[640,128]{1,0:T(8,128)(2,1)S(1)}, u32[]{:S(2)}, u32[]{:S(2)}) collective-permute-start(bf16[640,128]{1,0:T(8,128)(2,1)S(1)} %slice.17), channel_id=1, source_target_pairs={{0,12},{4,0},{8,4},{12,8},{1,13},{5,1},{9,5},{13,9},{2,14},{6,2},{... | collective-permute-start | bytes 491528 | tf_op jit(solution)/shard_map/ppermute | solution.py:257
  118.8 4.2 %collective-permute-start.12 = (f32[20,80,128]{2,1,0:T(8,128)S(1)}, f32[20,80,128]{2,1,0:T(8,128)S(1)}, u32[]{:S(2)}, u32[]{:S(2)}) collective-permute-start(f32[20,80,128]{2,1,0:T(8,128)S(1)} %get-tuple-element.28), channel_id=1, source_target_pairs={{0,1},{1,0},{2,3},{3,2},{4,5},{5,4},{6,7},{7,6},{8,9},{9,8},{10,11... | collective-permute-start | bytes 2457608 | tf_op jit(solution)/shard_map/ppermute | solution.py:261
  123.1 1.9 collective-permute-done.12
  125.3 27.8 %all_to_all.35 = f16[64,32,128]{2,1,0:T(8,128)(2,1)S(1)} all-to-all(f16[64,32,128]{2,1,0:T(8,128)(2,1)S(1)} %bitcast.38), channel_id=1, replica_groups=mesh['y'=8,'zl'=4,'x'=4,'zh'=2,'c'=2] {'zh','y','zl'}, dimensions={0} | all-to-all | bytes 1048576 | tf_op jit(solution)/shard_map/all_to_all | solution.py:252
  153.5 23.3 %all_to_all.36 = f16[64,32,128]{2,1,0:T(8,128)(2,1)S(1)} all-to-all(f16[64,32,128]{2,1,0:T(8,128)(2,1)S(1)} %broadcast_in_dim.15), channel_id=1, replica_groups=mesh['y'=8,'zl'=4,'x'=4,'zh'=2,'c'=2] {'zh','y','zl'}, dimensions={0} | all-to-all | bytes 1048576 | tf_op jit(solution)/shard_map/all_to_all | solution.py:252
  178.2 16.0 %all_to_all.37 = f32[8,80,128]{2,1,0:T(8,128)S(1)} all-to-all(f32[8,80,128]{2,1,0:T(8,128)S(1)} %get-tuple-element.31), channel_id=1, replica_groups=mesh['y'=8,'zl'=4,'x'=4,'zh'=2,'c'=2] {'x','c'}, dimensions={0} | all-to-all | bytes 655360 | tf_op jit(solution)/shard_map/all_to_all | solution.py:361
  194.1 4.4 %shard_map.72 = f32[8,80,128]{2,1,0:T(8,128)S(1)} custom-call(f32[640,128]{1,0:T(8,128)S(1)} %bitcast.34, f32[160,1280]{1,0:T(8,128)S(1)} %get-tuple-element.30.gram), custom_call_target="tpu_custom_call" | custom-call | tf_op jit(solution)/shard_map/pallas_call | solution.py:241
  198.5 10.6 %all_to_all.38 = f32[8,80,128]{2,1,0:T(8,128)S(1)} all-to-all(f32[8,80,128]{2,1,0:T(8,128)S(1)} %shard_map.72), channel_id=1, replica_groups=mesh['y'=8,'zl'=4,'x'=4,'zh'=2,'c'=2] {'x','c'}, dimensions={0} | all-to-all | bytes 655360 | tf_op jit(solution)/shard_map/all_to_all | solution.py:361
  209.1 5.1 %shard_map.73 = f32[8,80,128]{2,1,0:T(8,128)} custom-call(f32[640,128]{1,0:T(8,128)S(1)} %bitcast.35, f32[160,1280]{1,0:T(8,128)S(1)} %get-tuple-element.30.gram), custom_call_target="tpu_custom_call" | custom-call | tf_op jit(solution)/shard_map/pallas_call | solution.py:241
  214.3 4.1 %all-to-all-start.6 = ((f32[8,80,128]{2,1,0:T(8,128)}), f32[8,80,128]{2,1,0:T(8,128)S(1)}, u32[]{:S(2)}, u32[]{:S(2)}) async-start(f32[8,80,128]{2,1,0:T(8,128)} %shard_map.73), calls=%async_computation.6 | async-start | bytes 655360 | tf_op jit(solution)/shard_map/all_to_all | solution.py:361
  219.1 6.4 %all-to-all-done.6 = f32[8,80,128]{2,1,0:T(8,128)S(1)} async-done(((f32[8,80,128]{2,1,0:T(8,128)}), f32[8,80,128]{2,1,0:T(8,128)S(1)}, u32[]{:S(2)}, u32[]{:S(2)}) %all-to-all-start.6) | async-done | bytes 327712 | tf_op jit(solution)/shard_map/all_to_all | solution.py:361
  225.5 4.2 %shard_map.74 = f32[40,64]{1,0:T(8,128)} custom-call(s32[5]{0:T(128)S(1)} %stack.23.at.refs_0_, f32[640,128]{1,0:T(8,128)S(1)} %bitcast.32), custom_call_target="tpu_custom_call" | custom-call | tf_op jit(solution)/shard_map/pallas_call | solution.py:241
  (42 shorter events, 16.9 us)
Async XLA Ops:
  0.6 0.9 copy-start
  5.9 9.7 %collective-permute-start = (bf16[20,64,128]{2,1,0:T(8,128)(2,1)S(1)}, bf16[20,64,128]{2,1,0:T(8,128)(2,1)S(1)}, u32[]{:S(2)}, u32[]{:S(2)}) collective-permute-start(bf16[20,64,128]{2,1,0:T(8,128)(2,1)S(1)} %get-tuple-element.17), channel_id=1, source_target_pairs={{0,4},{4,8},{8,12},{12,0},{1,5},{5,9},{9,13},{13,1},{2,6},{6,10},{... | collective-permute-start | bytes 983048 | tf_op jit(solution)/shard_map/ppermute | solution.py:257
  9.9 10.1 %collective-permute-start.3 = (bf16[20,64,128]{2,1,0:T(8,128)(2,1)S(1)}, bf16[20,64,128]{2,1,0:T(8,128)(2,1)S(1)}, u32[]{:S(2)}, u32[]{:S(2)}) collective-permute-start(bf16[20,64,128]{2,1,0:T(8,128)(2,1)S(1)} %get-tuple-element.18), channel_id=1, source_target_pairs={{0,12},{4,0},{8,4},{12,8},{1,13},{5,1},{9,5},{13,9},{2,14},{6,2},{... | collective-permute-start | bytes 983048 | tf_op jit(solution)/shard_map/ppermute | solution.py:257
  16.2 10.5 %collective-permute-start.1 = (bf16[20,64,128]{2,1,0:T(8,128)(2,1)S(1)}, bf16[20,64,128]{2,1,0:T(8,128)(2,1)S(1)}, u32[]{:S(2)}, u32[]{:S(2)}) collective-permute-start(bf16[20,64,128]{2,1,0:T(8,128)(2,1)S(1)} %shard_map.60), channel_id=1, source_target_pairs={{0,4},{4,8},{8,12},{12,0},{1,5},{5,9},{9,13},{13,1},{2,6},{6,10},{... | collective-permute-start | bytes 983048 | tf_op jit(solution)/shard_map/ppermute | solution.py:257
  20.6 9.5 %collective-permute-start.4 = (bf16[20,64,128]{2,1,0:T(8,128)(2,1)S(1)}, bf16[20,64,128]{2,1,0:T(8,128)(2,1)S(1)}, u32[]{:S(2)}, u32[]{:S(2)}) collective-permute-start(bf16[20,64,128]{2,1,0:T(8,128)(2,1)S(1)} %shard_map.63), channel_id=1, source_target_pairs={{0,12},{4,0},{8,4},{12,8},{1,13},{5,1},{9,5},{13,9},{2,14},{6,2},{... | collective-permute-start | bytes 983048 | tf_op jit(solution)/shard_map/ppermute | solution.py:257
  27.3 9.3 %collective-permute-start.2 = (bf16[20,64,128]{2,1,0:T(8,128)(2,1)S(1)}, bf16[20,64,128]{2,1,0:T(8,128)(2,1)S(1)}, u32[]{:S(2)}, u32[]{:S(2)}) collective-permute-start(bf16[20,64,128]{2,1,0:T(8,128)(2,1)S(1)} %shard_map.61), channel_id=1, source_target_pairs={{0,4},{4,8},{8,12},{12,0},{1,5},{5,9},{9,13},{13,1},{2,6},{6,10},{... | collective-permute-start | bytes 983048 | tf_op jit(solution)/shard_map/ppermute | solution.py:257
  30.8 8.6 %collective-permute-start.5 = (bf16[20,64,128]{2,1,0:T(8,128)(2,1)S(1)}, bf16[20,64,128]{2,1,0:T(8,128)(2,1)S(1)}, u32[]{:S(2)}, u32[]{:S(2)}) collective-permute-start(bf16[20,64,128]{2,1,0:T(8,128)(2,1)S(1)} %shard_map.64), channel_id=1, source_target_pairs={{0,12},{4,0},{8,4},{12,8},{1,13},{5,1},{9,5},{13,9},{2,14},{6,2},{... | collective-permute-start | bytes 983048 | tf_op jit(solution)/shard_map/ppermute | solution.py:257
  37.2 22.9 %copy-start.1 = (bf16[128,256]{1,0:T(8,128)(2,1)S(1)}, bf16[128,256]{1,0:T(8,128)(2,1)}, u32[]{:S(2)}) copy-start(bf16[128,256]{1,0:T(8,128)(2,1)} %width) | copy-start | bytes 196612
  37.2 49.4 %copy-start.2 = (f32[40,64]{1,0:T(8,128)S(1)}, f32[40,64]{1,0:T(8,128)}, u32[]{:S(2)}) copy-start(f32[40,64]{1,0:T(8,128)} %param.7) | copy-start | bytes 30724
  41.3 35.3 %all-to-all-start = ((bf16[64,40,128]{2,1,0:T(8,128)(2,1)}), bf16[64,40,128]{2,1,0:T(8,128)(2,1)S(1)}, u32[]{:S(2)}, u32[]{:S(2)}) async-start(bf16[64,40,128]{2,1,0:T(8,128)(2,1)} %copy.10), calls=%async_computation | async-start | bytes 1310720 | tf_op jit(solution)/shard_map/all_to_all | solution.py:300
  60.1 16.1 %collective-permute-start.6 = (bf16[128,256]{1,0:T(8,128)(2,1)S(1)}, bf16[128,256]{1,0:T(8,128)(2,1)S(1)}, u32[]{:S(2)}, u32[]{:S(2)}) collective-permute-start(bf16[128,256]{1,0:T(8,128)(2,1)S(1)} %copy-done.1), channel_id=1, source_target_pairs={{0,2},{2,0},{1,3},{3,1},{4,6},{6,4},{5,7},{7,5},{8,10},{10,8},{9,1... | collective-permute-start | bytes 196616 | tf_op jit(solution)/shard_map/ppermute | solution.py:261
  77.7 10.2 %collective-permute-start.7 = (bf16[1280,128]{1,0:T(8,128)(2,1)S(1)}, bf16[1280,128]{1,0:T(8,128)(2,1)S(1)}, u32[]{:S(2)}, u32[]{:S(2)}) collective-permute-start(bf16[1280,128]{1,0:T(8,128)(2,1)S(1)} %get-tuple-element.22), channel_id=1, source_target_pairs={{0,1},{1,0},{2,3},{3,2},{4,5},{5,4},{6,7},{7,6},{8,9},{9,8},{10,11... | collective-permute-start | bytes 983048 | tf_op jit(solution)/shard_map/ppermute | solution.py:261
  88.9 28.4 %all-to-all-start.1 = ((f32[32,1,2560]{2,1,0:T(1,128)}), f32[32,1,2560]{2,1,0:T(1,128)S(1)}, u32[]{:S(2)}, u32[]{:S(2)}) async-start(f32[32,1,2560]{2,1,0:T(1,128)} %broadcast_in_dim.14), calls=%async_computation.1 | async-start | bytes 655360 | tf_op jit(solution)/shard_map/all_to_all | solution.py:318
  95.7 12.8 %collective-permute-start.8 = (bf16[1280,128]{1,0:T(8,128)(2,1)S(1)}, bf16[1280,128]{1,0:T(8,128)(2,1)S(1)}, u32[]{:S(2)}, u32[]{:S(2)}) collective-permute-start(bf16[1280,128]{1,0:T(8,128)(2,1)S(1)} %shard_map.67.refs_1_), channel_id=1, source_target_pairs={{0,4},{4,8},{8,12},{12,0},{1,5},{5,9},{9,13},{13,1},{2,6},{6,10},{... | collective-permute-start | bytes 983048 | tf_op jit(solution)/shard_map/ppermute | solution.py:257
  97.7 12.8 %collective-permute-start.9 = (bf16[1280,128]{1,0:T(8,128)(2,1)S(1)}, bf16[1280,128]{1,0:T(8,128)(2,1)S(1)}, u32[]{:S(2)}, u32[]{:S(2)}) collective-permute-start(bf16[1280,128]{1,0:T(8,128)(2,1)S(1)} %shard_map.67.refs_1_), channel_id=1, source_target_pairs={{0,12},{4,0},{8,4},{12,8},{1,13},{5,1},{9,5},{13,9},{2,14},{6,2},{... | collective-permute-start | bytes 983048 | tf_op jit(solution)/shard_map/ppermute | solution.py:257
  108.5 7.6 %collective-permute-start.10 = (bf16[640,128]{1,0:T(8,128)(2,1)S(1)}, bf16[640,128]{1,0:T(8,128)(2,1)S(1)}, u32[]{:S(2)}, u32[]{:S(2)}) collective-permute-start(bf16[640,128]{1,0:T(8,128)(2,1)S(1)} %slice.16), channel_id=1, source_target_pairs={{0,4},{4,8},{8,12},{12,0},{1,5},{5,9},{9,13},{13,1},{2,6},{6,10},{... | collective-permute-start | bytes 491528 | tf_op jit(solution)/shard_map/ppermute | solution.py:257
  110.5 6.8 %collective-permute-start.11 = (bf16[640,128]{1,0:T(8,128)(2,1)S(1)}, bf16[640,128]{1,0:T(8,128)(2,1)S(1)}, u32[]{:S(2)}, u32[]{:S(2)}) collective-permute-start(bf16[640,128]{1,0:T(8,128)(2,1)S(1)} %slice.17), channel_id=1, source_target_pairs={{0,12},{4,0},{8,4},{12,8},{1,13},{5,1},{9,5},{13,9},{2,14},{6,2},{... | collective-permute-start | bytes 491528 | tf_op jit(solution)/shard_map/ppermute | solution.py:257
  118.8 6.2 %collective-permute-start.12 = (f32[20,80,128]{2,1,0:T(8,128)S(1)}, f32[20,80,128]{2,1,0:T(8,128)S(1)}, u32[]{:S(2)}, u32[]{:S(2)}) collective-permute-start(f32[20,80,128]{2,1,0:T(8,128)S(1)} %get-tuple-element.28), channel_id=1, source_target_pairs={{0,1},{1,0},{2,3},{3,2},{4,5},{5,4},{6,7},{7,6},{8,9},{9,8},{10,11... | collective-permute-start | bytes 2457608 | tf_op jit(solution)/shard_map/ppermute | solution.py:261
  214.3 11.2 %all-to-all-start.6 = ((f32[8,80,128]{2,1,0:T(8,128)}), f32[8,80,128]{2,1,0:T(8,128)S(1)}, u32[]{:S(2)}, u32[]{:S(2)}) async-start(f32[8,80,128]{2,1,0:T(8,128)} %shard_map.73), calls=%async_computation.6 | async-start | bytes 655360 | tf_op jit(solution)/shard_map/all_to_all | solution.py:361

commit v4 on v3

--- a/solution.py
+++ b/solution.py
@@ -42,6 +42,16 @@
         out[f] = own
 
 
+def pass_kernel(at, left, right, out):
+    @pl.when(at[1] == 0)
+    def _():
+        out[...] = left[...]
+
+    @pl.when(at[1] != 0)
+    def _():
+        out[...] = right[...]
+
+
 def add_kernel(a, b, out):
     out[...] = (a[...].astype(F32) + b[...].astype(F32)).astype(out.dtype)
 
@@ -66,21 +76,15 @@
         sent[...] = low
 
 
-def gram_kernel(scale, at, own, left, right, far_a, far_b, kept, sent, core, acc):
+def gram_kernel(scale, at, own, left, right, far, kept, sent, core, acc):
     total, depth = own.shape
-    far = total // 2
     strip = kept.shape[1]
-    for j in range(N_X):
+    for j, block in enumerate((own, left, right, far)):
         for x in range(N_X):
             for zh in range(Z_HI):
                 for c in range(CORES):
                     source = ((x * Z_HI + zh) * CORES + c) * strip
                     place = ((zh * N_X + x) * CORES + c) * strip
-                    if j == N_X - 1:
-                        block = far_a if source < far else far_b
-                        source = source % far
-                    else:
-                        block = (own, left, right)[j]
                     core[place : place + strip, j * depth : (j + 1) * depth] = block[
                         source : source + strip, :
                     ]
@@ -109,31 +113,38 @@
                 sent[tile * Z_HI + zh] = acc[pl.ds(send_at, strip), lanes]
 
 
-def put_scaled(x, out, base, rows, step):
+def scaled(x):
     largest = jnp.max(jnp.max(jnp.abs(x), axis=0, keepdims=True), axis=1, keepdims=True)
     exponent = jnp.floor(jnp.log2(jnp.maximum(largest, 2.0**-100))) - 14.0
-    scale = jnp.exp2(-exponent)
-    tail = jnp.broadcast_to(exponent, (step - rows, x.shape[1]))
+    return x * jnp.exp2(-exponent), jnp.broadcast_to(exponent, (1, x.shape[1]))
+
+
+def put_pieces(x, extra, out, rows, step):
+    x, exponent = scaled(x)
+    extra, extra_exponent = scaled(extra)
+    tail = jnp.concatenate([exponent, extra, extra_exponent], axis=0)
+    end = rows + tail.shape[0]
     for j in range(x.shape[0] // rows):
-        at = base + j * step
-        out[at : at + rows, :] = x[j * rows : (j + 1) * rows, :] * scale
-        out[at + rows : at + step, :] = tail
-
-
-def pack_kernel(rows, step, a, b, out):
-    put_scaled(a[...] + b[...], out, 0, rows, step)
-
-
-def unscaled(parts, j, rows, step):
-    at = j * step
-    return parts[at : at + rows, :] * jnp.exp2(parts[at + rows : at + rows + 1, :])
-
-
-def sum_kernel(rows, step, parts, out):
-    total = unscaled(parts, 0, rows, step)
+        at = j * step
+        out[at : at + rows, :] = x[j * rows : (j + 1) * rows, :]
+        out[at + rows : at + end, :] = tail
+        if end < step:
+            out[at + end : at + step, :] = jnp.zeros((step - end, x.shape[1]), F32)
+
+
+def pack_kernel(rows, step, a, b, extra, out):
+    put_pieces(a[...] + b[...], extra[...], out, rows, step)
+
+
+def unscaled(parts, start, rows):
+    return parts[start : start + rows, :] * jnp.exp2(parts[start + rows : start + rows + 1, :])
+
+
+def sum_kernel(rows, step, parts, extra, out):
+    total = unscaled(parts, 0, rows)
     for j in range(1, parts.shape[0] // step):
-        total = total + unscaled(parts, j, rows, step)
-    put_scaled(total, out, 0, rows, step)
+        total = total + unscaled(parts, j * step, rows)
+    put_pieces(total, extra[...], out, rows, step)
 
 
 def put_product(gram, basis, out):
@@ -143,28 +154,43 @@
     high = jnp.dot(gram[:, half:], basis, precision=HIGHEST, preferred_element_type=F32)
     product = low[:, :rank] + high[:, rank:]
     strip = product.shape[0] // Z_HI
-    packed = jnp.concatenate([product[:strip], product[strip:]], axis=1)
+    packed, exponent = scaled(jnp.concatenate([product[:strip], product[strip:]], axis=1))
+    tail = jnp.broadcast_to(exponent, (out.shape[1] - strip, exponent.shape[1]))
     for j in range(out.shape[0]):
-        out[j] = packed
-
-
-def first_kernel(rows, step, pieces, shards, gram, out, flat, basis):
-    for j in range(pieces.shape[0] // step):
-        flat[j * rows : (j + 1) * rows, :] = unscaled(pieces, j, rows, step)
+        out[j, 0:strip, :] = packed
+        out[j, strip:, :] = tail
+
+
+def take_product(parts, packed):
+    count = packed.shape[0]
+    peers = N_X * CORES
+    strip, step = count // peers, parts.shape[0] // peers
+    for j in range(peers):
+        packed[j * strip : (j + 1) * strip, :] = unscaled(parts, j * step, strip)
+
+
+def first_kernel(rows, step, out_pieces, back_pieces, gram, out, flat, basis):
+    count = back_pieces.shape[0] // step
+    for j in range(count):
+        flat[j * rows : (j + 1) * rows, :] = unscaled(back_pieces, j * step, rows)
     mine, total = gram.shape
     for t in range(total // LANES):
         gram[:, t * LANES : (t + 1) * LANES] = flat[t * mine : (t + 1) * mine, :]
     rank = basis.shape[1] // Z_HI
     strip = total // (N_X * Z_HI * CORES)
-    half = strip // 4
-    for frm in range(total // (2 * half)):
+    share = strip // (4 * Z_HI)
+    for j in range(count):
+        zh, frm = divmod(j, count // Z_HI)
         place, odd = divmod(frm, 2)
         x, side, c = place // (Z_HI * CORES), place // CORES % Z_HI, place % CORES
+        start = (x * CORES + c) * strip + (2 * odd + zh) * (2 * share)
+        block = jnp.concatenate(
+            [unscaled(p, j * step + rows + 1, share // 2) for p in (out_pieces, back_pieces)], axis=0
+        )
         for part in range(2):
-            start = (x * CORES + c) * strip + (2 * odd + part) * half
-            basis[start : start + half, side * rank : (side + 1) * rank] = shards[
-                frm * half : (frm + 1) * half, part * rank : (part + 1) * rank
-            ]
+            basis[start + part * share : start + (part + 1) * share, side * rank : (side + 1) * rank] = (
+                block[:, part * rank : (part + 1) * rank]
+            )
     put_product(gram[...], basis[...], out)
 
 
@@ -223,13 +249,15 @@
     )
 
 
-def step_kernel(packed, gram, out):
+def step_kernel(parts, gram, out, packed):
+    take_product(parts, packed)
     product = packed[...]
     basis = apply_factor(product, factor_of(product))
     put_product(gram[...], basis, out)
 
 
-def last_kernel(at, packed, out):
+def last_kernel(at, parts, out, packed):
+    take_product(parts, packed)
     frames, rank = out.shape
     inverse = factor_of(packed[...])
     rows = packed[pl.ds(pl.multiple_of(at[3], 8), frames), :]
@@ -310,21 +338,17 @@
         add_kernel, shape(total, half, dtype=mid.dtype), [VMEM] * 2, (own, swap(sent, "c"))
     )
 
-    part = frames_dev // 2
-    start = jnp.concatenate([start_basis[:part], start_basis[part:]], axis=1).reshape(1, -1)
-    start = jnp.broadcast_to(start[None], (lax.axis_size(FRM),) + start.shape)
-    core, start = lax.optimization_barrier((core, start))
     left, right = shift(core, 1), shift(core, -1)
-    shards = lax.all_to_all(start, FRM, 0, 0, tiled=True).reshape(-1, LANES)
-    far_a, far_b = shift(left[: total // 2], 1), shift(right[total // 2 :], -1)
-    far_a, far_b, shards = lax.optimization_barrier((far_a, far_b, shards))
+    passed = call(pass_kernel, shape(total, half, dtype=mid.dtype), [SMEM, VMEM, VMEM], (at, left, right))
+    ways = [(x * CORES + c, (x + 1 - 2 * c) % N_X * CORES + c) for x in range(N_X) for c in range(CORES)]
+    far = lax.ppermute(passed, ("x", "c"), ways)
     mine = Z_HI * strip
     tiles = total // LANES
     kept, sent = call(
         lambda *refs: gram_kernel(1.0 / (rank_h * rank_w), *refs),
         [shape(tiles * Z_HI, strip, LANES)] * 2,
-        [SMEM] + [VMEM] * 5,
-        (at, core, left, right, far_a, far_b),
+        [SMEM] + [VMEM] * 4,
+        (at, core, left, right, far),
         [
             pltpu.VMEM((total, N_X * half), jnp.bfloat16),
             pltpu.VMEM((total // N_X, 2 * LANES), F32),
@@ -335,34 +359,44 @@
     flat = shape(tiles * mine, LANES)
     count = lax.axis_size(PLANE)
     rows = flat.shape[0] // count
-    step = -(-(rows + 1) // 16) * 16
-    pieces = call(
+    step = -(-(rows + 2 + frames_dev // (4 * Z_HI)) // 16) * 16
+    share = frames_dev // (2 * Z_HI)
+    start = lax.dynamic_slice_in_dim(start_basis, zh_at * 2 * share, 2 * share, 0)
+    start = jnp.concatenate([start[:share], start[share:]], axis=1)
+    upper, lower = start[: share // 2], start[share // 2 :]
+    out_pieces = call(
         lambda *refs: pack_kernel(rows, step, *refs),
         shape(count * step, LANES),
+        [VMEM] * 3,
+        (kept.reshape(flat.shape), came.reshape(flat.shape), upper),
+    )
+    out_pieces = trade(out_pieces.astype(jnp.float16), count, PLANE)
+    piece = call(
+        lambda *refs: sum_kernel(rows, step, *refs),
+        shape(step, LANES),
         [VMEM] * 2,
-        (kept.reshape(flat.shape), came.reshape(flat.shape)),
-    )
-    pieces = trade(pieces.astype(jnp.float16), count, PLANE)
-    piece = call(
-        lambda *refs: sum_kernel(rows, step, *refs), shape(step, LANES), [VMEM], (pieces,)
+        (out_pieces, lower),
     )
     piece = piece.astype(jnp.float16)
     pieces = trade(jnp.broadcast_to(piece[None], (count,) + piece.shape), count, PLANE)
 
-    packed_shape = shape(N_X * CORES, strip, Z_HI * rank_f)
+    packed_shape = shape(N_X * CORES, strip + 8, Z_HI * rank_f)
+    packed_rows = pltpu.VMEM((total // Z_HI, Z_HI * rank_f), F32)
     gram, packed = call(
         lambda *refs: first_kernel(rows, step, *refs),
         [shape(mine, total), packed_shape],
         [VMEM] * 2,
-        (pieces, shards),
-        [pltpu.VMEM(flat.shape, F32), pltpu.VMEM((total // Z_HI, Z_HI * rank_f), F32)],
+        (out_pieces, pieces),
+        [pltpu.VMEM(flat.shape, F32), packed_rows],
     )
     for step in range(ITERS):
-        packed = lax.all_to_all(packed, ("x", "c"), 0, 0, tiled=True)
-        packed = packed.reshape(total // Z_HI, Z_HI * rank_f)
+        packed = packed.reshape(-1, packed.shape[2]).astype(jnp.float16)
+        packed = trade(packed, N_X * CORES, ("x", "c"))
         if step < ITERS - 1:
-            packed = call(step_kernel, packed_shape, [VMEM] * 2, (packed, gram))
-    factor = call(last_kernel, shape(frames_dev, rank_f), [SMEM, VMEM], (at, packed))
+            packed = call(step_kernel, packed_shape, [VMEM] * 2, (packed, gram), [packed_rows])
+    factor = call(
+        last_kernel, shape(frames_dev, rank_f), [SMEM, VMEM], (at, packed), [packed_rows]
+    )
     strip_rows = lax.dynamic_slice_in_dim(gram, zh_at * strip, strip, 0)
     column = frame_zh * (total // Z_HI) + frame_row
     gram_out = lax.dynamic_slice_in_dim(strip_rows.T, column, frames_dev, 0)

time: 231 us -> 217 us (0.939)
  starting transfers between devices: 85.1 us -> 77.4 us
  blocking collectives: 77.7 us -> 70.5 us
    all_to_all x2 -> x0, blocking collectives: 26.6 us -> none  [local(): packed = lax.all_to_all(packed, ('x', 'c'), 0, 0, tiled=True)]
    all_to_all x2 -> x4, blocking collectives: 51.1 us -> 70.5 us  [trade(): blocks = lax.all_to_all(x.reshape(count, -1, LANES), axes, 0, 0, tiled=True)]
    all_to_all x2 -> x1, starting transfers between devices: 10.9 us -> 4.22 us  [trade(): blocks = lax.all_to_all(x.reshape(count, -1, LANES), axes, 0, 0, tiled=True)]
    ppermute x10 -> x8, starting transfers between devices: 35.3 us -> 28.8 us  [shift(): return lax.ppermute(x, 'x', [(i, (i + by) % N_X) for i in range(N_X)])]
    ppermute x0 -> x1, starting transfers between devices: none -> 5.32 us  [local(): far = lax.ppermute(passed, ('x', 'c'), ways)]
    ppermute x0 -> x1, waiting for transfers between devices: none -> 4 us  [local(): far = lax.ppermute(passed, ('x', 'c'), ways)]
    all_to_all x2 -> x1, waiting for transfers between devices: 6.37 us -> 4.98 us  [trade(): blocks = lax.all_to_all(x.reshape(count, -1, LANES), axes, 0, 0, tiled=True)]
    ppermute x10 -> x8, waiting for transfers between devices: 16.4 us -> 15.3 us  [shift(): return lax.ppermute(x, 'x', [(i, (i + by) % N_X) for i in range(N_X)])]
  transfers between devices with their start and end apart: 16 -> 14, of which waited for: 12 -> 12; matrix products, arithmetic and copies ran while one was open for 0% -> 0% of each run, Pallas kernels for 1% -> 1%
where the time goes in v4:
time: 217 us
  starting transfers between devices  77.4 us (36%)
  blocking collectives  70.5 us (32%)
  waiting for transfers between devices  36.9 us (17%)
  Pallas kernels  22.6 us (10%)
  matrix products  3.66 us (2%)
  local copies, waits for them, and re-layouts  3.07 us (1%)
    all_to_all x4, blocking collectives, trade(): blocks = lax.all_to_all(x.reshape(count, -1, LANES), axes, 0, 0, tiled=True)  70.5 us
    ppermute x8, starting transfers between devices, shift(): return lax.ppermute(x, 'x', [(i, (i + by) % N_X) for i in range(N_X)])  28.8 us
    pallas_call x17, Pallas kernels, call(): pl.pallas_call(kernel, out_shape=outs, in_specs=ins, out_specs=jax.tree.m...  22.6 us
    ppermute x3, starting transfers between devices, swap(): return lax.ppermute(x, axis, [(0, 1), (1, 0)])  20.3 us
    all_to_all x1, starting transfers between devices, local(): lax.all_to_all(mid, PLANE, 0, 0, tiled=True).reshape(Z_HI, total, cols)  18.8 us
    ppermute x8, waiting for transfers between devices, shift(): return lax.ppermute(x, 'x', [(i, (i + by) % N_X) for i in range(N_X)])  15.3 us
    ppermute x3, waiting for transfers between devices, swap(): return lax.ppermute(x, axis, [(0, 1), (1, 0)])  12.2 us
    ppermute x1, starting transfers between devices, local(): far = lax.ppermute(passed, ('x', 'c'), ways)  5.32 us
  transfers between devices with their start and end apart: 14, of which 12 were waited for; matrix products, arithmetic and copies ran while one was open for 0% of the time, Pallas kernels for 1%

profile of v4, /device:TPU:1, one launch (start us, length us, event | category | flops | bytes accessed | tf_op | source)
XLA Modules:
  0.0 216.5 jit_solution(14826374839338226558)
XLA Ops:
  1.6 3.7 %convert_bitcast_fusion.mid = bf16[40,256,128]{2,1,0:T(8,128)(2,1)S(1)} fusion(bf16[40,384,128]{2,1,0:T(8,128)(2,1)} %param.4, bf16[384,256]{1,0:T(8,128)(2,1)S(1)} %copy-done), kind=kOutput, calls=%fused_computation | convolution fusion | flops 1007943680 | bytes 6750208 | tf_op jit(solution)/shard_map/fhw,hr->frw/dot_general | solution.py:321
  5.9 3.9 %collective-permute-start = (bf16[20,64,128]{2,1,0:T(8,128)(2,1)S(1)}, bf16[20,64,128]{2,1,0:T(8,128)(2,1)S(1)}, u32[]{:S(2)}, u32[]{:S(2)}) collective-permute-start(bf16[20,64,128]{2,1,0:T(8,128)(2,1)S(1)} %get-tuple-element.12), channel_id=1, source_target_pairs={{0,4},{4,8},{8,12},{12,0},{1,5},{5,9},{9,13},{13,1},{2,6},{6,10},{... | collective-permute-start | bytes 983048 | tf_op jit(solution)/shard_map/ppermute | solution.py:285
  9.9 3.2 %collective-permute-start.3 = (bf16[20,64,128]{2,1,0:T(8,128)(2,1)S(1)}, bf16[20,64,128]{2,1,0:T(8,128)(2,1)S(1)}, u32[]{:S(2)}, u32[]{:S(2)}) collective-permute-start(bf16[20,64,128]{2,1,0:T(8,128)(2,1)S(1)} %get-tuple-element.13), channel_id=1, source_target_pairs={{0,12},{4,0},{8,4},{12,8},{1,13},{5,1},{9,5},{13,9},{2,14},{6,2},{... | collective-permute-start | bytes 983048 | tf_op jit(solution)/shard_map/ppermute | solution.py:285
  13.1 2.5 %collective-permute-done.came = bf16[20,64,128]{2,1,0:T(8,128)(2,1)S(1)} collective-permute-done((bf16[20,64,128]{2,1,0:T(8,128)(2,1)S(1)}, bf16[20,64,128]{2,1,0:T(8,128)(2,1)S(1)}, u32[]{:S(2)}, u32[]{:S(2)}) %collective-permute-start) | collective-permute-done | bytes 327712 | tf_op jit(solution)/shard_map/ppermute | solution.py:285
  16.2 3.8 %collective-permute-start.1 = (bf16[20,64,128]{2,1,0:T(8,128)(2,1)S(1)}, bf16[20,64,128]{2,1,0:T(8,128)(2,1)S(1)}, u32[]{:S(2)}, u32[]{:S(2)}) collective-permute-start(bf16[20,64,128]{2,1,0:T(8,128)(2,1)S(1)} %shard_map.60), channel_id=1, source_target_pairs={{0,4},{4,8},{8,12},{12,0},{1,5},{5,9},{9,13},{13,1},{2,6},{6,10},{... | collective-permute-start | bytes 983048 | tf_op jit(solution)/shard_map/ppermute | solution.py:285
  20.6 4.2 %collective-permute-start.4 = (bf16[20,64,128]{2,1,0:T(8,128)(2,1)S(1)}, bf16[20,64,128]{2,1,0:T(8,128)(2,1)S(1)}, u32[]{:S(2)}, u32[]{:S(2)}) collective-permute-start(bf16[20,64,128]{2,1,0:T(8,128)(2,1)S(1)} %shard_map.63), channel_id=1, source_target_pairs={{0,12},{4,0},{8,4},{12,8},{1,13},{5,1},{9,5},{13,9},{2,14},{6,2},{... | collective-permute-start | bytes 983048 | tf_op jit(solution)/shard_map/ppermute | solution.py:285
  24.8 1.9 collective-permute-done.1.came
  27.3 2.8 %collective-permute-start.2 = (bf16[20,64,128]{2,1,0:T(8,128)(2,1)S(1)}, bf16[20,64,128]{2,1,0:T(8,128)(2,1)S(1)}, u32[]{:S(2)}, u32[]{:S(2)}) collective-permute-start(bf16[20,64,128]{2,1,0:T(8,128)(2,1)S(1)} %shard_map.61), channel_id=1, source_target_pairs={{0,4},{4,8},{8,12},{12,0},{1,5},{5,9},{9,13},{13,1},{2,6},{6,10},{... | collective-permute-start | bytes 983048 | tf_op jit(solution)/shard_map/ppermute | solution.py:285
  30.8 3.7 %collective-permute-start.5 = (bf16[20,64,128]{2,1,0:T(8,128)(2,1)S(1)}, bf16[20,64,128]{2,1,0:T(8,128)(2,1)S(1)}, u32[]{:S(2)}, u32[]{:S(2)}) collective-permute-start(bf16[20,64,128]{2,1,0:T(8,128)(2,1)S(1)} %shard_map.64), channel_id=1, source_target_pairs={{0,12},{4,0},{8,4},{12,8},{1,13},{5,1},{9,5},{13,9},{2,14},{6,2},{... | collective-permute-start | bytes 983048 | tf_op jit(solution)/shard_map/ppermute | solution.py:285
  34.5 2.1 collective-permute-done.2.came
  37.2 2.1 collective-permute-done.5.came
  41.3 18.8 %all-to-all-start = ((bf16[64,40,128]{2,1,0:T(8,128)(2,1)}), bf16[64,40,128]{2,1,0:T(8,128)(2,1)S(1)}, u32[]{:S(2)}, u32[]{:S(2)}) async-start(bf16[64,40,128]{2,1,0:T(8,128)(2,1)} %copy.10), calls=%async_computation | async-start | bytes 1310720 | tf_op jit(solution)/shard_map/all_to_all | solution.py:328
  60.2 6.9 %collective-permute-start.6 = (bf16[128,256]{1,0:T(8,128)(2,1)S(1)}, bf16[128,256]{1,0:T(8,128)(2,1)S(1)}, u32[]{:S(2)}, u32[]{:S(2)}) collective-permute-start(bf16[128,256]{1,0:T(8,128)(2,1)S(1)} %copy-done.1), channel_id=1, source_target_pairs={{0,2},{2,0},{1,3},{3,1},{4,6},{6,4},{5,7},{7,5},{8,10},{10,8},{9,1... | collective-permute-start | bytes 196616 | tf_op jit(solution)/shard_map/ppermute | solution.py:289
  67.1 9.1 %collective-permute-done.6.width_other = bf16[128,256]{1,0:T(8,128)(2,1)S(1)} collective-permute-done((bf16[128,256]{1,0:T(8,128)(2,1)S(1)}, bf16[128,256]{1,0:T(8,128)(2,1)S(1)}, u32[]{:S(2)}, u32[]{:S(2)}) %collective-permute-start.6) | collective-permute-done | bytes 65568 | tf_op jit(solution)/shard_map/ppermute | solution.py:289
  77.7 8.9 %collective-permute-start.7 = (bf16[1280,128]{1,0:T(8,128)(2,1)S(1)}, bf16[1280,128]{1,0:T(8,128)(2,1)S(1)}, u32[]{:S(2)}, u32[]{:S(2)}) collective-permute-start(bf16[1280,128]{1,0:T(8,128)(2,1)S(1)} %get-tuple-element.17), channel_id=1, source_target_pairs={{0,1},{1,0},{2,3},{3,2},{4,5},{5,4},{6,7},{7,6},{8,9},{9,8},{10,11... | collective-permute-start | bytes 983048 | tf_op jit(solution)/shard_map/ppermute | solution.py:289
  88.0 1.9 collective-permute-start.8
  89.9 5.3 %collective-permute-start.9 = (bf16[1280,128]{1,0:T(8,128)(2,1)S(1)}, bf16[1280,128]{1,0:T(8,128)(2,1)S(1)}, u32[]{:S(2)}, u32[]{:S(2)}) collective-permute-start(bf16[1280,128]{1,0:T(8,128)(2,1)S(1)} %shard_map.67.refs_1_), channel_id=1, source_target_pairs={{0,12},{4,0},{8,4},{12,8},{1,13},{5,1},{9,5},{13,9},{2,14},{6,2},{... | collective-permute-start | bytes 983048 | tf_op jit(solution)/shard_map/ppermute | solution.py:285
  95.2 5.8 %collective-permute-done.8.left.refs_2_ = bf16[1280,128]{1,0:T(8,128)(2,1)S(1)} collective-permute-done((bf16[1280,128]{1,0:T(8,128)(2,1)S(1)}, bf16[1280,128]{1,0:T(8,128)(2,1)S(1)}, u32[]{:S(2)}, u32[]{:S(2)}) %collective-permute-start.8) | collective-permute-done | bytes 327712 | tf_op jit(solution)/shard_map/ppermute | solution.py:285
  102.5 5.3 %collective-permute-start.10 = (bf16[1280,128]{1,0:T(8,128)(2,1)S(1)}, bf16[1280,128]{1,0:T(8,128)(2,1)S(1)}, u32[]{:S(2)}, u32[]{:S(2)}) collective-permute-start(bf16[1280,128]{1,0:T(8,128)(2,1)S(1)} %shard_map.68), channel_id=1, source_target_pairs={{0,4},{1,13},{4,8},{5,1},{8,12},{9,5},{12,0},{13,9},{2,6},{3,15},{... | collective-permute-start | bytes 983048 | tf_op jit(solution)/shard_map/ppermute | solution.py:344
  107.8 4.0 %collective-permute-done.10.refs_4_ = bf16[1280,128]{1,0:T(8,128)(2,1)S(1)} collective-permute-done((bf16[1280,128]{1,0:T(8,128)(2,1)S(1)}, bf16[1280,128]{1,0:T(8,128)(2,1)S(1)}, u32[]{:S(2)}, u32[]{:S(2)}) %collective-permute-start.10) | collective-permute-done | bytes 327712 | tf_op jit(solution)/shard_map/ppermute | solution.py:344
  111.8 1.5 shard_map.69
  113.3 4.4 %collective-permute-start.11 = (f32[20,80,128]{2,1,0:T(8,128)S(1)}, f32[20,80,128]{2,1,0:T(8,128)S(1)}, u32[]{:S(2)}, u32[]{:S(2)}) collective-permute-start(f32[20,80,128]{2,1,0:T(8,128)S(1)} %get-tuple-element.19), channel_id=1, source_target_pairs={{0,1},{1,0},{2,3},{3,2},{4,5},{5,4},{6,7},{7,6},{8,9},{9,8},{10,11... | collective-permute-start | bytes 2457608 | tf_op jit(solution)/shard_map/ppermute | solution.py:289
  117.9 1.8 collective-permute-done.11
  120.1 25.5 %all_to_all.30 = f16[64,32,128]{2,1,0:T(8,128)(2,1)S(1)} all-to-all(f16[64,32,128]{2,1,0:T(8,128)(2,1)S(1)} %bitcast.37), channel_id=1, replica_groups=mesh['y'=8,'zl'=4,'x'=4,'zh'=2,'c'=2] {'zh','y','zl'}, dimensions={0} | all-to-all | bytes 1048576 | tf_op jit(solution)/shard_map/all_to_all | solution.py:280
  146.0 23.3 %all_to_all.31 = f16[64,32,128]{2,1,0:T(8,128)(2,1)S(1)} all-to-all(f16[64,32,128]{2,1,0:T(8,128)(2,1)S(1)} %broadcast_in_dim.2), channel_id=1, replica_groups=mesh['y'=8,'zl'=4,'x'=4,'zh'=2,'c'=2] {'zh','y','zl'}, dimensions={0} | all-to-all | bytes 1048576 | tf_op jit(solution)/shard_map/all_to_all | solution.py:280
  170.9 12.5 %all_to_all.32 = f16[8,88,128]{2,1,0:T(8,128)(2,1)S(1)} all-to-all(f16[8,88,128]{2,1,0:T(8,128)(2,1)S(1)} %convert_element_type.56), channel_id=1, replica_groups=mesh['y'=8,'zl'=4,'x'=4,'zh'=2,'c'=2] {'x','c'}, dimensions={0} | all-to-all | bytes 360448 | tf_op jit(solution)/shard_map/all_to_all | solution.py:280
  183.4 4.5 %shard_map.73 = f32[8,88,128]{2,1,0:T(8,128)S(1)} custom-call(f32[704,128]{1,0:T(8,128)S(1)} %bitcast_convert_fusion.4.parts, f32[160,1280]{1,0:T(8,128)S(1)} %get-tuple-element.20.gram), custom_call_target="tpu_custom_call" | custom-call | tf_op jit(solution)/shard_map/pallas_call | solution.py:269
  188.0 9.1 %all_to_all.33 = f16[8,88,128]{2,1,0:T(8,128)(2,1)S(1)} all-to-all(f16[8,88,128]{2,1,0:T(8,128)(2,1)S(1)} %convert_element_type.59), channel_id=1, replica_groups=mesh['y'=8,'zl'=4,'x'=4,'zh'=2,'c'=2] {'x','c'}, dimensions={0} | all-to-all | bytes 360448 | tf_op jit(solution)/shard_map/all_to_all | solution.py:280
  197.1 4.5 %shard_map.74 = f32[8,88,128]{2,1,0:T(8,128)S(1)} custom-call(f32[704,128]{1,0:T(8,128)S(1)} %bitcast_convert_fusion.3.parts, f32[160,1280]{1,0:T(8,128)S(1)} %get-tuple-element.20.gram), custom_call_target="tpu_custom_call" | custom-call | tf_op jit(solution)/shard_map/pallas_call | solution.py:269
  202.3 4.2 %all-to-all-start.5 = ((f16[8,88,128]{2,1,0:T(8,128)(2,1)}), f16[8,88,128]{2,1,0:T(8,128)(2,1)S(1)}, u32[]{:S(2)}, u32[]{:S(2)}) async-start(f16[8,88,128]{2,1,0:T(8,128)(2,1)} %convert_element_type.62), calls=%async_computation.5 | async-start | bytes 360448 | tf_op jit(solution)/shard_map/all_to_all | solution.py:280
  207.3 5.0 %all-to-all-done.5 = f16[8,88,128]{2,1,0:T(8,128)(2,1)S(1)} async-done(((f16[8,88,128]{2,1,0:T(8,128)(2,1)}), f16[8,88,128]{2,1,0:T(8,128)(2,1)S(1)}, u32[]{:S(2)}, u32[]{:S(2)}) %all-to-all-start.5) | async-done | bytes 180256 | tf_op jit(solution)/shard_map/all_to_all | solution.py:280
  212.3 4.2 %shard_map.75 = f32[40,64]{1,0:T(8,128)} custom-call(s32[5]{0:T(128)S(1)} %stack.23.at.refs_0_, f32[704,128]{1,0:T(8,128)S(1)} %bitcast_convert_fusion.2.parts), custom_call_target="tpu_custom_call" | custom-call | tf_op jit(solution)/shard_map/pallas_call | solution.py:269
  (42 shorter events, 14.8 us)
Async XLA Ops:
  0.6 0.9 copy-start
  5.9 9.7 %collective-permute-start = (bf16[20,64,128]{2,1,0:T(8,128)(2,1)S(1)}, bf16[20,64,128]{2,1,0:T(8,128)(2,1)S(1)}, u32[]{:S(2)}, u32[]{:S(2)}) collective-permute-start(bf16[20,64,128]{2,1,0:T(8,128)(2,1)S(1)} %get-tuple-element.12), channel_id=1, source_target_pairs={{0,4},{4,8},{8,12},{12,0},{1,5},{5,9},{9,13},{13,1},{2,6},{6,10},{... | collective-permute-start | bytes 983048 | tf_op jit(solution)/shard_map/ppermute | solution.py:285
  9.9 10.1 %collective-permute-start.3 = (bf16[20,64,128]{2,1,0:T(8,128)(2,1)S(1)}, bf16[20,64,128]{2,1,0:T(8,128)(2,1)S(1)}, u32[]{:S(2)}, u32[]{:S(2)}) collective-permute-start(bf16[20,64,128]{2,1,0:T(8,128)(2,1)S(1)} %get-tuple-element.13), channel_id=1, source_target_pairs={{0,12},{4,0},{8,4},{12,8},{1,13},{5,1},{9,5},{13,9},{2,14},{6,2},{... | collective-permute-start | bytes 983048 | tf_op jit(solution)/shard_map/ppermute | solution.py:285
  16.2 10.5 %collective-permute-start.1 = (bf16[20,64,128]{2,1,0:T(8,128)(2,1)S(1)}, bf16[20,64,128]{2,1,0:T(8,128)(2,1)S(1)}, u32[]{:S(2)}, u32[]{:S(2)}) collective-permute-start(bf16[20,64,128]{2,1,0:T(8,128)(2,1)S(1)} %shard_map.60), channel_id=1, source_target_pairs={{0,4},{4,8},{8,12},{12,0},{1,5},{5,9},{9,13},{13,1},{2,6},{6,10},{... | collective-permute-start | bytes 983048 | tf_op jit(solution)/shard_map/ppermute | solution.py:285
  20.6 9.5 %collective-permute-start.4 = (bf16[20,64,128]{2,1,0:T(8,128)(2,1)S(1)}, bf16[20,64,128]{2,1,0:T(8,128)(2,1)S(1)}, u32[]{:S(2)}, u32[]{:S(2)}) collective-permute-start(bf16[20,64,128]{2,1,0:T(8,128)(2,1)S(1)} %shard_map.63), channel_id=1, source_target_pairs={{0,12},{4,0},{8,4},{12,8},{1,13},{5,1},{9,5},{13,9},{2,14},{6,2},{... | collective-permute-start | bytes 983048 | tf_op jit(solution)/shard_map/ppermute | solution.py:285
  27.3 9.3 %collective-permute-start.2 = (bf16[20,64,128]{2,1,0:T(8,128)(2,1)S(1)}, bf16[20,64,128]{2,1,0:T(8,128)(2,1)S(1)}, u32[]{:S(2)}, u32[]{:S(2)}) collective-permute-start(bf16[20,64,128]{2,1,0:T(8,128)(2,1)S(1)} %shard_map.61), channel_id=1, source_target_pairs={{0,4},{4,8},{8,12},{12,0},{1,5},{5,9},{9,13},{13,1},{2,6},{6,10},{... | collective-permute-start | bytes 983048 | tf_op jit(solution)/shard_map/ppermute | solution.py:285
  30.8 8.6 %collective-permute-start.5 = (bf16[20,64,128]{2,1,0:T(8,128)(2,1)S(1)}, bf16[20,64,128]{2,1,0:T(8,128)(2,1)S(1)}, u32[]{:S(2)}, u32[]{:S(2)}) collective-permute-start(bf16[20,64,128]{2,1,0:T(8,128)(2,1)S(1)} %shard_map.64), channel_id=1, source_target_pairs={{0,12},{4,0},{8,4},{12,8},{1,13},{5,1},{9,5},{13,9},{2,14},{6,2},{... | collective-permute-start | bytes 983048 | tf_op jit(solution)/shard_map/ppermute | solution.py:285
  37.2 22.9 %copy-start.1 = (bf16[128,256]{1,0:T(8,128)(2,1)S(1)}, bf16[128,256]{1,0:T(8,128)(2,1)}, u32[]{:S(2)}) copy-start(bf16[128,256]{1,0:T(8,128)(2,1)} %width) | copy-start | bytes 196612
  40.0 77.8 %copy-start.2 = (f32[40,64]{1,0:T(8,128)S(1)}, f32[40,64]{1,0:T(8,128)}, u32[]{:S(2)}) copy-start(f32[40,64]{1,0:T(8,128)} %param.7) | copy-start | bytes 30724
  41.3 35.3 %all-to-all-start = ((bf16[64,40,128]{2,1,0:T(8,128)(2,1)}), bf16[64,40,128]{2,1,0:T(8,128)(2,1)S(1)}, u32[]{:S(2)}, u32[]{:S(2)}) async-start(bf16[64,40,128]{2,1,0:T(8,128)(2,1)} %copy.10), calls=%async_computation | async-start | bytes 1310720 | tf_op jit(solution)/shard_map/all_to_all | solution.py:328
  60.2 16.1 %collective-permute-start.6 = (bf16[128,256]{1,0:T(8,128)(2,1)S(1)}, bf16[128,256]{1,0:T(8,128)(2,1)S(1)}, u32[]{:S(2)}, u32[]{:S(2)}) collective-permute-start(bf16[128,256]{1,0:T(8,128)(2,1)S(1)} %copy-done.1), channel_id=1, source_target_pairs={{0,2},{2,0},{1,3},{3,1},{4,6},{6,4},{5,7},{7,5},{8,10},{10,8},{9,1... | collective-permute-start | bytes 196616 | tf_op jit(solution)/shard_map/ppermute | solution.py:289
  77.7 10.2 %collective-permute-start.7 = (bf16[1280,128]{1,0:T(8,128)(2,1)S(1)}, bf16[1280,128]{1,0:T(8,128)(2,1)S(1)}, u32[]{:S(2)}, u32[]{:S(2)}) collective-permute-start(bf16[1280,128]{1,0:T(8,128)(2,1)S(1)} %get-tuple-element.17), channel_id=1, source_target_pairs={{0,1},{1,0},{2,3},{3,2},{4,5},{5,4},{6,7},{7,6},{8,9},{9,8},{10,11... | collective-permute-start | bytes 983048 | tf_op jit(solution)/shard_map/ppermute | solution.py:289
  88.0 13.1 %collective-permute-start.8 = (bf16[1280,128]{1,0:T(8,128)(2,1)S(1)}, bf16[1280,128]{1,0:T(8,128)(2,1)S(1)}, u32[]{:S(2)}, u32[]{:S(2)}) collective-permute-start(bf16[1280,128]{1,0:T(8,128)(2,1)S(1)} %shard_map.67.refs_1_), channel_id=1, source_target_pairs={{0,4},{4,8},{8,12},{12,0},{1,5},{5,9},{9,13},{13,1},{2,6},{6,10},{... | collective-permute-start | bytes 983048 | tf_op jit(solution)/shard_map/ppermute | solution.py:285
  89.9 12.0 %collective-permute-start.9 = (bf16[1280,128]{1,0:T(8,128)(2,1)S(1)}, bf16[1280,128]{1,0:T(8,128)(2,1)S(1)}, u32[]{:S(2)}, u32[]{:S(2)}) collective-permute-start(bf16[1280,128]{1,0:T(8,128)(2,1)S(1)} %shard_map.67.refs_1_), channel_id=1, source_target_pairs={{0,12},{4,0},{8,4},{12,8},{1,13},{5,1},{9,5},{13,9},{2,14},{6,2},{... | collective-permute-start | bytes 983048 | tf_op jit(solution)/shard_map/ppermute | solution.py:285
  102.5 9.3 %collective-permute-start.10 = (bf16[1280,128]{1,0:T(8,128)(2,1)S(1)}, bf16[1280,128]{1,0:T(8,128)(2,1)S(1)}, u32[]{:S(2)}, u32[]{:S(2)}) collective-permute-start(bf16[1280,128]{1,0:T(8,128)(2,1)S(1)} %shard_map.68), channel_id=1, source_target_pairs={{0,4},{1,13},{4,8},{5,1},{8,12},{9,5},{12,0},{13,9},{2,6},{3,15},{... | collective-permute-start | bytes 983048 | tf_op jit(solution)/shard_map/ppermute | solution.py:344
  113.3 6.4 %collective-permute-start.11 = (f32[20,80,128]{2,1,0:T(8,128)S(1)}, f32[20,80,128]{2,1,0:T(8,128)S(1)}, u32[]{:S(2)}, u32[]{:S(2)}) collective-permute-start(f32[20,80,128]{2,1,0:T(8,128)S(1)} %get-tuple-element.19), channel_id=1, source_target_pairs={{0,1},{1,0},{2,3},{3,2},{4,5},{5,4},{6,7},{7,6},{8,9},{9,8},{10,11... | collective-permute-start | bytes 2457608 | tf_op jit(solution)/shard_map/ppermute | solution.py:289
  202.3 10.0 %all-to-all-start.5 = ((f16[8,88,128]{2,1,0:T(8,128)(2,1)}), f16[8,88,128]{2,1,0:T(8,128)(2,1)S(1)}, u32[]{:S(2)}, u32[]{:S(2)}) async-start(f16[8,88,128]{2,1,0:T(8,128)(2,1)} %convert_element_type.62), calls=%async_computation.5 | async-start | bytes 360448 | tf_op jit(solution)/shard_map/all_to_all | solution.py:280

commit v5 on v4

--- a/solution.py
+++ b/solution.py
@@ -15,7 +15,7 @@
 LANES = 128
 FRM = ("y", "zl")
 PLANE = ("zh", "y", "zl")
-PIVOTS = 4
+PIVOTS = 8
 VMEM = pl.BlockSpec(memory_space=pltpu.VMEM)
 SMEM = pl.BlockSpec(memory_space=pltpu.SMEM)
 PARAMS = pltpu.CompilerParams(vmem_limit_bytes=40 << 20)
@@ -42,18 +42,10 @@
         out[f] = own
 
 
-def pass_kernel(at, left, right, out):
-    @pl.when(at[1] == 0)
-    def _():
-        out[...] = left[...]
-
-    @pl.when(at[1] != 0)
-    def _():
-        out[...] = right[...]
-
-
-def add_kernel(a, b, out):
-    out[...] = (a[...].astype(F32) + b[...].astype(F32)).astype(out.dtype)
+def copies_kernel(a, b, out):
+    total = (a[...].astype(F32) + b[...].astype(F32)).astype(out.dtype)
+    for j in range(out.shape[0]):
+        out[j] = total
 
 
 def core_kernel(at, mid, width, width_other, own, sent):
@@ -76,17 +68,17 @@
         sent[...] = low
 
 
-def gram_kernel(scale, at, own, left, right, far, kept, sent, core, acc):
-    total, depth = own.shape
+def gram_kernel(scale, at, blocks, kept, sent, core, acc):
+    _, total, depth = blocks.shape
     strip = kept.shape[1]
-    for j, block in enumerate((own, left, right, far)):
+    for j in range(N_X):
         for x in range(N_X):
             for zh in range(Z_HI):
                 for c in range(CORES):
                     source = ((x * Z_HI + zh) * CORES + c) * strip
                     place = ((zh * N_X + x) * CORES + c) * strip
-                    core[place : place + strip, j * depth : (j + 1) * depth] = block[
-                        source : source + strip, :
+                    core[place : place + strip, j * depth : (j + 1) * depth] = blocks[
+                        j, source : source + strip, :
                     ]
     rows = []
     for zh in range(Z_HI):
@@ -334,21 +326,18 @@
         (at, mid, width, width_other),
     )
 
-    core = call(
-        add_kernel, shape(total, half, dtype=mid.dtype), [VMEM] * 2, (own, swap(sent, "c"))
-    )
-
-    left, right = shift(core, 1), shift(core, -1)
-    passed = call(pass_kernel, shape(total, half, dtype=mid.dtype), [SMEM, VMEM, VMEM], (at, left, right))
-    ways = [(x * CORES + c, (x + 1 - 2 * c) % N_X * CORES + c) for x in range(N_X) for c in range(CORES)]
-    far = lax.ppermute(passed, ("x", "c"), ways)
+
+    copies = call(
+        copies_kernel, shape(N_X, total, half, dtype=mid.dtype), [VMEM] * 2, (own, swap(sent, "c"))
+    )
+    blocks = lax.all_to_all(copies, "x", 0, 0, tiled=True)
     mine = Z_HI * strip
     tiles = total // LANES
     kept, sent = call(
         lambda *refs: gram_kernel(1.0 / (rank_h * rank_w), *refs),
         [shape(tiles * Z_HI, strip, LANES)] * 2,
-        [SMEM] + [VMEM] * 4,
-        (at, core, left, right, far),
+        [SMEM, VMEM],
+        (at, blocks),
         [
             pltpu.VMEM((total, N_X * half), jnp.bfloat16),
             pltpu.VMEM((total // N_X, 2 * LANES), F32),

time: 217 us -> 213 us (0.982)
  blocking collectives: 70.5 us -> 91.3 us
  starting transfers between devices: 77.4 us -> 64.3 us
  waiting for transfers between devices: 36.9 us -> 26.2 us
    all_to_all x0 -> x1, blocking collectives: none -> 21.5 us  [local(): blocks = lax.all_to_all(copies, 'x', 0, 0, tiled=True)]
    ppermute x8 -> x6, starting transfers between devices: 28.8 us -> 21.6 us  [shift(): return lax.ppermute(x, 'x', [(i, (i + by) % N_X) for i in range(N_X)])]
    ppermute x8 -> x6, waiting for transfers between devices: 15.3 us -> 8.62 us  [shift(): return lax.ppermute(x, 'x', [(i, (i + by) % N_X) for i in range(N_X)])]
    ppermute x1 -> x0, starting transfers between devices: 5.32 us -> none  [local(): far = lax.ppermute(passed, ('x', 'c'), ways)]
    ppermute x1 -> x0, waiting for transfers between devices: 4 us -> none  [local(): far = lax.ppermute(passed, ('x', 'c'), ways)]
    pallas_call x17 -> x16, Pallas kernels: 22.6 us -> 21.2 us  [call(): pl.pallas_call(kernel, out_shape=outs, in_specs=ins, out_specs=jax.tree.m...]
  transfers between devices with their start and end apart: 14 -> 11, of which waited for: 12 -> 9; matrix products, arithmetic and copies ran while one was open for 0% -> 0% of each run, Pallas kernels for 1% -> 1%
where the time goes in v5:
time: 213 us; the launch traced here: 212 us
  blocking collectives  91.3 us (43%)
  starting transfers between devices  64.3 us (30%)
  waiting for transfers between devices  26.2 us (12%)
  Pallas kernels  21.2 us (10%)
  matrix products  3.66 us (2%)
  local copies, waits for them, and re-layouts  3.07 us (1%)
    all_to_all x4, blocking collectives, trade(): blocks = lax.all_to_all(x.reshape(count, -1, LANES), axes, 0, 0, tiled=True)  69.8 us
    ppermute x6, starting transfers between devices, shift(): return lax.ppermute(x, 'x', [(i, (i + by) % N_X) for i in range(N_X)])  21.6 us
    all_to_all x1, blocking collectives, local(): blocks = lax.all_to_all(copies, 'x', 0, 0, tiled=True)  21.5 us
    pallas_call x16, Pallas kernels, call(): pl.pallas_call(kernel, out_shape=outs, in_specs=ins, out_specs=jax.tree.m...  21.2 us
    ppermute x3, starting transfers between devices, swap(): return lax.ppermute(x, axis, [(0, 1), (1, 0)])  19.6 us
    all_to_all x1, starting transfers between devices, local(): lax.all_to_all(mid, PLANE, 0, 0, tiled=True).reshape(Z_HI, total, cols)  18.9 us
    ppermute x3, waiting for transfers between devices, swap(): return lax.ppermute(x, axis, [(0, 1), (1, 0)])  12.2 us
    ppermute x6, waiting for transfers between devices, shift(): return lax.ppermute(x, 'x', [(i, (i + by) % N_X) for i in range(N_X)])  8.62 us
  transfers between devices with their start and end apart: 11, of which 9 were waited for; matrix products, arithmetic and copies ran while one was open for 0% of the time, Pallas kernels for 1%

profile of v5, /device:TPU:1, one launch (start us, length us, event | category | flops | bytes accessed | tf_op | source)
XLA Modules:
  0.0 212.0 jit_solution(10275561733879952227)
XLA Ops:
  1.6 3.7 %convert_bitcast_fusion.mid = bf16[40,256,128]{2,1,0:T(8,128)(2,1)S(1)} fusion(bf16[40,384,128]{2,1,0:T(8,128)(2,1)} %param.4, bf16[384,256]{1,0:T(8,128)(2,1)S(1)} %copy-done), kind=kOutput, calls=%fused_computation | convolution fusion | flops 1007943680 | bytes 6750208 | tf_op jit(solution)/shard_map/fhw,hr->frw/dot_general | solution.py:313
  5.9 3.9 %collective-permute-start = (bf16[20,64,128]{2,1,0:T(8,128)(2,1)S(1)}, bf16[20,64,128]{2,1,0:T(8,128)(2,1)S(1)}, u32[]{:S(2)}, u32[]{:S(2)}) collective-permute-start(bf16[20,64,128]{2,1,0:T(8,128)(2,1)S(1)} %get-tuple-element.12), channel_id=1, source_target_pairs={{0,4},{4,8},{8,12},{12,0},{1,5},{5,9},{9,13},{13,1},{2,6},{6,10},{... | collective-permute-start | bytes 983048 | tf_op jit(solution)/shard_map/ppermute | solution.py:277
  9.9 3.2 %collective-permute-start.3 = (bf16[20,64,128]{2,1,0:T(8,128)(2,1)S(1)}, bf16[20,64,128]{2,1,0:T(8,128)(2,1)S(1)}, u32[]{:S(2)}, u32[]{:S(2)}) collective-permute-start(bf16[20,64,128]{2,1,0:T(8,128)(2,1)S(1)} %get-tuple-element.13), channel_id=1, source_target_pairs={{0,12},{4,0},{8,4},{12,8},{1,13},{5,1},{9,5},{13,9},{2,14},{6,2},{... | collective-permute-start | bytes 983048 | tf_op jit(solution)/shard_map/ppermute | solution.py:277
  13.1 2.5 %collective-permute-done.came = bf16[20,64,128]{2,1,0:T(8,128)(2,1)S(1)} collective-permute-done((bf16[20,64,128]{2,1,0:T(8,128)(2,1)S(1)}, bf16[20,64,128]{2,1,0:T(8,128)(2,1)S(1)}, u32[]{:S(2)}, u32[]{:S(2)}) %collective-permute-start) | collective-permute-done | bytes 327712 | tf_op jit(solution)/shard_map/ppermute | solution.py:277
  16.2 3.8 %collective-permute-start.1 = (bf16[20,64,128]{2,1,0:T(8,128)(2,1)S(1)}, bf16[20,64,128]{2,1,0:T(8,128)(2,1)S(1)}, u32[]{:S(2)}, u32[]{:S(2)}) collective-permute-start(bf16[20,64,128]{2,1,0:T(8,128)(2,1)S(1)} %shard_map.60), channel_id=1, source_target_pairs={{0,4},{4,8},{8,12},{12,0},{1,5},{5,9},{9,13},{13,1},{2,6},{6,10},{... | collective-permute-start | bytes 983048 | tf_op jit(solution)/shard_map/ppermute | solution.py:277
  20.6 4.2 %collective-permute-start.4 = (bf16[20,64,128]{2,1,0:T(8,128)(2,1)S(1)}, bf16[20,64,128]{2,1,0:T(8,128)(2,1)S(1)}, u32[]{:S(2)}, u32[]{:S(2)}) collective-permute-start(bf16[20,64,128]{2,1,0:T(8,128)(2,1)S(1)} %shard_map.63), channel_id=1, source_target_pairs={{0,12},{4,0},{8,4},{12,8},{1,13},{5,1},{9,5},{13,9},{2,14},{6,2},{... | collective-permute-start | bytes 983048 | tf_op jit(solution)/shard_map/ppermute | solution.py:277
  24.8 1.9 collective-permute-done.1.came
  27.3 2.8 %collective-permute-start.2 = (bf16[20,64,128]{2,1,0:T(8,128)(2,1)S(1)}, bf16[20,64,128]{2,1,0:T(8,128)(2,1)S(1)}, u32[]{:S(2)}, u32[]{:S(2)}) collective-permute-start(bf16[20,64,128]{2,1,0:T(8,128)(2,1)S(1)} %shard_map.61), channel_id=1, source_target_pairs={{0,4},{4,8},{8,12},{12,0},{1,5},{5,9},{9,13},{13,1},{2,6},{6,10},{... | collective-permute-start | bytes 983048 | tf_op jit(solution)/shard_map/ppermute | solution.py:277
  30.8 3.7 %collective-permute-start.5 = (bf16[20,64,128]{2,1,0:T(8,128)(2,1)S(1)}, bf16[20,64,128]{2,1,0:T(8,128)(2,1)S(1)}, u32[]{:S(2)}, u32[]{:S(2)}) collective-permute-start(bf16[20,64,128]{2,1,0:T(8,128)(2,1)S(1)} %shard_map.64), channel_id=1, source_target_pairs={{0,12},{4,0},{8,4},{12,8},{1,13},{5,1},{9,5},{13,9},{2,14},{6,2},{... | collective-permute-start | bytes 983048 | tf_op jit(solution)/shard_map/ppermute | solution.py:277
  34.5 2.1 %collective-permute-done.2.came = bf16[20,64,128]{2,1,0:T(8,128)(2,1)S(1)} collective-permute-done((bf16[20,64,128]{2,1,0:T(8,128)(2,1)S(1)}, bf16[20,64,128]{2,1,0:T(8,128)(2,1)S(1)}, u32[]{:S(2)}, u32[]{:S(2)}) %collective-permute-start.2) | collective-permute-done | bytes 327712 | tf_op jit(solution)/shard_map/ppermute | solution.py:277
  37.2 2.1 collective-permute-done.5.came
  40.0 1.3 copy.10
  41.3 18.9 %all-to-all-start = ((bf16[64,40,128]{2,1,0:T(8,128)(2,1)}), bf16[64,40,128]{2,1,0:T(8,128)(2,1)S(1)}, u32[]{:S(2)}, u32[]{:S(2)}) async-start(bf16[64,40,128]{2,1,0:T(8,128)(2,1)} %copy.10), calls=%async_computation | async-start | bytes 1310720 | tf_op jit(solution)/shard_map/all_to_all | solution.py:320
  60.3 6.9 %collective-permute-start.6 = (bf16[128,256]{1,0:T(8,128)(2,1)S(1)}, bf16[128,256]{1,0:T(8,128)(2,1)S(1)}, u32[]{:S(2)}, u32[]{:S(2)}) collective-permute-start(bf16[128,256]{1,0:T(8,128)(2,1)S(1)} %copy-done.1), channel_id=1, source_target_pairs={{0,2},{2,0},{1,3},{3,1},{4,6},{6,4},{5,7},{7,5},{8,10},{10,8},{9,1... | collective-permute-start | bytes 196616 | tf_op jit(solution)/shard_map/ppermute | solution.py:281
  67.2 9.1 %collective-permute-done.6.width_other = bf16[128,256]{1,0:T(8,128)(2,1)S(1)} collective-permute-done((bf16[128,256]{1,0:T(8,128)(2,1)S(1)}, bf16[128,256]{1,0:T(8,128)(2,1)S(1)}, u32[]{:S(2)}, u32[]{:S(2)}) %collective-permute-start.6) | collective-permute-done | bytes 65568 | tf_op jit(solution)/shard_map/ppermute | solution.py:281
  76.8 1.1 shard_map.66
  77.9 8.9 %collective-permute-start.7 = (bf16[1280,128]{1,0:T(8,128)(2,1)S(1)}, bf16[1280,128]{1,0:T(8,128)(2,1)S(1)}, u32[]{:S(2)}, u32[]{:S(2)}) collective-permute-start(bf16[1280,128]{1,0:T(8,128)(2,1)S(1)} %get-tuple-element.17), channel_id=1, source_target_pairs={{0,1},{1,0},{2,3},{3,2},{4,5},{5,4},{6,7},{7,6},{8,9},{9,8},{10,11... | collective-permute-start | bytes 983048 | tf_op jit(solution)/shard_map/ppermute | solution.py:281
  86.8 1.2 collective-permute-done.7.b
  88.1 21.5 %all_to_all.35.refs_1_ = bf16[4,1280,128]{2,1,0:T(8,128)(2,1)S(1)} all-to-all(bf16[4,1280,128]{2,1,0:T(8,128)(2,1)S(1)} %shard_map.67), channel_id=1, replica_groups=mesh['y'=8,'zl'=4,'x'=4,'zh'=2,'c'=2] {'x'}, dimensions={0} | all-to-all | bytes 2621440 | tf_op jit(solution)/shard_map/all_to_all | solution.py:333
  109.6 1.5 shard_map.68
  111.1 3.7 %collective-permute-start.8 = (f32[20,80,128]{2,1,0:T(8,128)S(1)}, f32[20,80,128]{2,1,0:T(8,128)S(1)}, u32[]{:S(2)}, u32[]{:S(2)}) collective-permute-start(f32[20,80,128]{2,1,0:T(8,128)S(1)} %get-tuple-element.19), channel_id=1, source_target_pairs={{0,1},{1,0},{2,3},{3,2},{4,5},{5,4},{6,7},{7,6},{8,9},{9,8},{10,11... | collective-permute-start | bytes 2457608 | tf_op jit(solution)/shard_map/ppermute | solution.py:281
  114.9 1.8 collective-permute-done.8
  117.1 25.5 %all_to_all.36 = f16[64,32,128]{2,1,0:T(8,128)(2,1)S(1)} all-to-all(f16[64,32,128]{2,1,0:T(8,128)(2,1)S(1)} %bitcast.37), channel_id=1, replica_groups=mesh['y'=8,'zl'=4,'x'=4,'zh'=2,'c'=2] {'zh','y','zl'}, dimensions={0} | all-to-all | bytes 1048576 | tf_op jit(solution)/shard_map/all_to_all | solution.py:272
  143.1 23.3 %all_to_all.37 = f16[64,32,128]{2,1,0:T(8,128)(2,1)S(1)} all-to-all(f16[64,32,128]{2,1,0:T(8,128)(2,1)S(1)} %broadcast_in_dim.2), channel_id=1, replica_groups=mesh['y'=8,'zl'=4,'x'=4,'zh'=2,'c'=2] {'zh','y','zl'}, dimensions={0} | all-to-all | bytes 1048576 | tf_op jit(solution)/shard_map/all_to_all | solution.py:272
  166.5 1.4 shard_map.71
  167.9 11.8 %all_to_all.38 = f16[8,88,128]{2,1,0:T(8,128)(2,1)S(1)} all-to-all(f16[8,88,128]{2,1,0:T(8,128)(2,1)S(1)} %convert_element_type.56), channel_id=1, replica_groups=mesh['y'=8,'zl'=4,'x'=4,'zh'=2,'c'=2] {'x','c'}, dimensions={0} | all-to-all | bytes 360448 | tf_op jit(solution)/shard_map/all_to_all | solution.py:272
  179.8 4.2 %shard_map.72 = f32[8,88,128]{2,1,0:T(8,128)S(1)} custom-call(f32[704,128]{1,0:T(8,128)S(1)} %bitcast_convert_fusion.4.parts, f32[160,1280]{1,0:T(8,128)S(1)} %get-tuple-element.20.gram), custom_call_target="tpu_custom_call" | custom-call | tf_op jit(solution)/shard_map/pallas_call | solution.py:261
  184.1 9.1 %all_to_all.39 = f16[8,88,128]{2,1,0:T(8,128)(2,1)S(1)} all-to-all(f16[8,88,128]{2,1,0:T(8,128)(2,1)S(1)} %convert_element_type.59), channel_id=1, replica_groups=mesh['y'=8,'zl'=4,'x'=4,'zh'=2,'c'=2] {'x','c'}, dimensions={0} | all-to-all | bytes 360448 | tf_op jit(solution)/shard_map/all_to_all | solution.py:272
  193.2 4.2 %shard_map.73 = f32[8,88,128]{2,1,0:T(8,128)S(1)} custom-call(f32[704,128]{1,0:T(8,128)S(1)} %bitcast_convert_fusion.3.parts, f32[160,1280]{1,0:T(8,128)S(1)} %get-tuple-element.20.gram), custom_call_target="tpu_custom_call" | custom-call | tf_op jit(solution)/shard_map/pallas_call | solution.py:261
  198.1 4.2 %all-to-all-start.6 = ((f16[8,88,128]{2,1,0:T(8,128)(2,1)}), f16[8,88,128]{2,1,0:T(8,128)(2,1)S(1)}, u32[]{:S(2)}, u32[]{:S(2)}) async-start(f16[8,88,128]{2,1,0:T(8,128)(2,1)} %convert_element_type.62), calls=%async_computation.6 | async-start | bytes 360448 | tf_op jit(solution)/shard_map/all_to_all | solution.py:272
  203.1 5.0 %all-to-all-done.6 = f16[8,88,128]{2,1,0:T(8,128)(2,1)S(1)} async-done(((f16[8,88,128]{2,1,0:T(8,128)(2,1)}), f16[8,88,128]{2,1,0:T(8,128)(2,1)S(1)}, u32[]{:S(2)}, u32[]{:S(2)}) %all-to-all-start.6) | async-done | bytes 180256 | tf_op jit(solution)/shard_map/all_to_all | solution.py:272
  208.1 4.0 %shard_map.74 = f32[40,64]{1,0:T(8,128)} custom-call(s32[5]{0:T(128)S(1)} %stack.23.at.refs_0_, f32[704,128]{1,0:T(8,128)S(1)} %bitcast_convert_fusion.2.parts), custom_call_target="tpu_custom_call" | custom-call | tf_op jit(solution)/shard_map/pallas_call | solution.py:261
  (36 shorter events, 8.4 us)
Async XLA Ops:
  0.6 0.9 copy-start
  5.9 9.7 %collective-permute-start = (bf16[20,64,128]{2,1,0:T(8,128)(2,1)S(1)}, bf16[20,64,128]{2,1,0:T(8,128)(2,1)S(1)}, u32[]{:S(2)}, u32[]{:S(2)}) collective-permute-start(bf16[20,64,128]{2,1,0:T(8,128)(2,1)S(1)} %get-tuple-element.12), channel_id=1, source_target_pairs={{0,4},{4,8},{8,12},{12,0},{1,5},{5,9},{9,13},{13,1},{2,6},{6,10},{... | collective-permute-start | bytes 983048 | tf_op jit(solution)/shard_map/ppermute | solution.py:277
  9.9 10.1 %collective-permute-start.3 = (bf16[20,64,128]{2,1,0:T(8,128)(2,1)S(1)}, bf16[20,64,128]{2,1,0:T(8,128)(2,1)S(1)}, u32[]{:S(2)}, u32[]{:S(2)}) collective-permute-start(bf16[20,64,128]{2,1,0:T(8,128)(2,1)S(1)} %get-tuple-element.13), channel_id=1, source_target_pairs={{0,12},{4,0},{8,4},{12,8},{1,13},{5,1},{9,5},{13,9},{2,14},{6,2},{... | collective-permute-start | bytes 983048 | tf_op jit(solution)/shard_map/ppermute | solution.py:277
  16.2 10.5 %collective-permute-start.1 = (bf16[20,64,128]{2,1,0:T(8,128)(2,1)S(1)}, bf16[20,64,128]{2,1,0:T(8,128)(2,1)S(1)}, u32[]{:S(2)}, u32[]{:S(2)}) collective-permute-start(bf16[20,64,128]{2,1,0:T(8,128)(2,1)S(1)} %shard_map.60), channel_id=1, source_target_pairs={{0,4},{4,8},{8,12},{12,0},{1,5},{5,9},{9,13},{13,1},{2,6},{6,10},{... | collective-permute-start | bytes 983048 | tf_op jit(solution)/shard_map/ppermute | solution.py:277
  20.6 9.5 %collective-permute-start.4 = (bf16[20,64,128]{2,1,0:T(8,128)(2,1)S(1)}, bf16[20,64,128]{2,1,0:T(8,128)(2,1)S(1)}, u32[]{:S(2)}, u32[]{:S(2)}) collective-permute-start(bf16[20,64,128]{2,1,0:T(8,128)(2,1)S(1)} %shard_map.63), channel_id=1, source_target_pairs={{0,12},{4,0},{8,4},{12,8},{1,13},{5,1},{9,5},{13,9},{2,14},{6,2},{... | collective-permute-start | bytes 983048 | tf_op jit(solution)/shard_map/ppermute | solution.py:277
  27.3 9.3 %collective-permute-start.2 = (bf16[20,64,128]{2,1,0:T(8,128)(2,1)S(1)}, bf16[20,64,128]{2,1,0:T(8,128)(2,1)S(1)}, u32[]{:S(2)}, u32[]{:S(2)}) collective-permute-start(bf16[20,64,128]{2,1,0:T(8,128)(2,1)S(1)} %shard_map.61), channel_id=1, source_target_pairs={{0,4},{4,8},{8,12},{12,0},{1,5},{5,9},{9,13},{13,1},{2,6},{6,10},{... | collective-permute-start | bytes 983048 | tf_op jit(solution)/shard_map/ppermute | solution.py:277
  30.8 8.6 %collective-permute-start.5 = (bf16[20,64,128]{2,1,0:T(8,128)(2,1)S(1)}, bf16[20,64,128]{2,1,0:T(8,128)(2,1)S(1)}, u32[]{:S(2)}, u32[]{:S(2)}) collective-permute-start(bf16[20,64,128]{2,1,0:T(8,128)(2,1)S(1)} %shard_map.64), channel_id=1, source_target_pairs={{0,12},{4,0},{8,4},{12,8},{1,13},{5,1},{9,5},{13,9},{2,14},{6,2},{... | collective-permute-start | bytes 983048 | tf_op jit(solution)/shard_map/ppermute | solution.py:277
  37.2 23.0 %copy-start.1 = (bf16[128,256]{1,0:T(8,128)(2,1)S(1)}, bf16[128,256]{1,0:T(8,128)(2,1)}, u32[]{:S(2)}) copy-start(bf16[128,256]{1,0:T(8,128)(2,1)} %width) | copy-start | bytes 196612
  41.3 73.5 %copy-start.2 = (f32[40,64]{1,0:T(8,128)S(1)}, f32[40,64]{1,0:T(8,128)}, u32[]{:S(2)}) copy-start(f32[40,64]{1,0:T(8,128)} %param.7) | copy-start | bytes 30724
  41.3 35.4 %all-to-all-start = ((bf16[64,40,128]{2,1,0:T(8,128)(2,1)}), bf16[64,40,128]{2,1,0:T(8,128)(2,1)S(1)}, u32[]{:S(2)}, u32[]{:S(2)}) async-start(bf16[64,40,128]{2,1,0:T(8,128)(2,1)} %copy.10), calls=%async_computation | async-start | bytes 1310720 | tf_op jit(solution)/shard_map/all_to_all | solution.py:320
  60.3 16.1 %collective-permute-start.6 = (bf16[128,256]{1,0:T(8,128)(2,1)S(1)}, bf16[128,256]{1,0:T(8,128)(2,1)S(1)}, u32[]{:S(2)}, u32[]{:S(2)}) collective-permute-start(bf16[128,256]{1,0:T(8,128)(2,1)S(1)} %copy-done.1), channel_id=1, source_target_pairs={{0,2},{2,0},{1,3},{3,1},{4,6},{6,4},{5,7},{7,5},{8,10},{10,8},{9,1... | collective-permute-start | bytes 196616 | tf_op jit(solution)/shard_map/ppermute | solution.py:281
  77.9 10.2 %collective-permute-start.7 = (bf16[1280,128]{1,0:T(8,128)(2,1)S(1)}, bf16[1280,128]{1,0:T(8,128)(2,1)S(1)}, u32[]{:S(2)}, u32[]{:S(2)}) collective-permute-start(bf16[1280,128]{1,0:T(8,128)(2,1)S(1)} %get-tuple-element.17), channel_id=1, source_target_pairs={{0,1},{1,0},{2,3},{3,2},{4,5},{5,4},{6,7},{7,6},{8,9},{9,8},{10,11... | collective-permute-start | bytes 983048 | tf_op jit(solution)/shard_map/ppermute | solution.py:281
  111.1 5.7 %collective-permute-start.8 = (f32[20,80,128]{2,1,0:T(8,128)S(1)}, f32[20,80,128]{2,1,0:T(8,128)S(1)}, u32[]{:S(2)}, u32[]{:S(2)}) collective-permute-start(f32[20,80,128]{2,1,0:T(8,128)S(1)} %get-tuple-element.19), channel_id=1, source_target_pairs={{0,1},{1,0},{2,3},{3,2},{4,5},{5,4},{6,7},{7,6},{8,9},{9,8},{10,11... | collective-permute-start | bytes 2457608 | tf_op jit(solution)/shard_map/ppermute | solution.py:281
  198.1 10.0 %all-to-all-start.6 = ((f16[8,88,128]{2,1,0:T(8,128)(2,1)}), f16[8,88,128]{2,1,0:T(8,128)(2,1)S(1)}, u32[]{:S(2)}, u32[]{:S(2)}) async-start(f16[8,88,128]{2,1,0:T(8,128)(2,1)} %convert_element_type.62), calls=%async_computation.6 | async-start | bytes 360448 | tf_op jit(solution)/shard_map/all_to_all | solution.py:272

commit v6 on v5

--- a/solution.py
+++ b/solution.py
@@ -139,11 +139,29 @@
     put_pieces(total, extra[...], out, rows, step)
 
 
+def halves(x):
+    upper = x.astype(jnp.bfloat16)
+    return upper, (x - upper.astype(F32)).astype(jnp.bfloat16)
+
+
+def split_dot(a, b, dims):
+    a_upper, a_lower = halves(a)
+    b_upper, b_lower = halves(b)
+    both = jnp.concatenate([b_upper, b_lower], axis=1 - dims[1])
+    wide = lax.dot_general(
+        a_upper, both, (((dims[0],), (dims[1],)), ((), ())), preferred_element_type=F32
+    )
+    count = wide.shape[1] // 2
+    return wide[:, :count] + wide[:, count:] + lax.dot_general(
+        a_lower, b_upper, (((dims[0],), (dims[1],)), ((), ())), preferred_element_type=F32
+    )
+
+
 def put_product(gram, basis, out):
     half = basis.shape[0]
     rank = basis.shape[1] // Z_HI
-    low = jnp.dot(gram[:, :half], basis, precision=HIGHEST, preferred_element_type=F32)
-    high = jnp.dot(gram[:, half:], basis, precision=HIGHEST, preferred_element_type=F32)
+    low = split_dot(gram[:, :half], basis, (1, 0))
+    high = split_dot(gram[:, half:], basis, (1, 0))
     product = low[:, :rank] + high[:, rank:]
     strip = product.shape[0] // Z_HI
     packed, exponent = scaled(jnp.concatenate([product[:strip], product[strip:]], axis=1))
@@ -224,10 +242,13 @@
 
 
 def factor_of(packed):
+    parts = jnp.concatenate(halves(packed), axis=1)
     both = lax.dot_general(
-        packed, packed, (((0,), (0,)), ((), ())), precision=HIGHEST, preferred_element_type=F32
-    )
-    rank = both.shape[0] // Z_HI
+        parts, parts, (((0,), (0,)), ((), ())), preferred_element_type=F32
+    )
+    count = packed.shape[1]
+    both = (both[:count, :count] + both[count:, count:]) + (both[:count, count:] + both[count:, :count])
+    rank = count // Z_HI
     inverse = inverse_factor(both[:rank, :rank] + both[rank:, rank:])
     zero = jnp.zeros_like(inverse)
     return jnp.concatenate(
@@ -244,7 +265,7 @@
 def step_kernel(parts, gram, out, packed):
     take_product(parts, packed)
     product = packed[...]
-    basis = apply_factor(product, factor_of(product))
+    basis = split_dot(product, factor_of(product), (1, 1))
     put_product(gram[...], basis, out)
 
 

time: 213 us -> 210 us (0.986)
  Pallas kernels: 21.2 us -> 18.7 us
    pallas_call x16, Pallas kernels: 21.2 us -> 18.7 us  [call(): pl.pallas_call(kernel, out_shape=outs, in_specs=ins, out_specs=jax.tree.m...]
where the time goes in v6:
time: 210 us
  blocking collectives  91.3 us (43%)
  starting transfers between devices  64.3 us (31%)
  waiting for transfers between devices  26.2 us (12%)
  Pallas kernels  18.7 us (9%)
  matrix products  3.66 us (2%)
  local copies, waits for them, and re-layouts  3.07 us (1%)
    all_to_all x4, blocking collectives, trade(): blocks = lax.all_to_all(x.reshape(count, -1, LANES), axes, 0, 0, tiled=True)  69.8 us
    ppermute x6, starting transfers between devices, shift(): return lax.ppermute(x, 'x', [(i, (i + by) % N_X) for i in range(N_X)])  21.6 us
    all_to_all x1, blocking collectives, local(): blocks = lax.all_to_all(copies, 'x', 0, 0, tiled=True)  21.5 us
    ppermute x3, starting transfers between devices, swap(): return lax.ppermute(x, axis, [(0, 1), (1, 0)])  19.6 us
    all_to_all x1, starting transfers between devices, local(): lax.all_to_all(mid, PLANE, 0, 0, tiled=True).reshape(Z_HI, total, cols)  18.9 us
    pallas_call x16, Pallas kernels, call(): pl.pallas_call(kernel, out_shape=outs, in_specs=ins, out_specs=jax.tree.m...  18.7 us
    ppermute x3, waiting for transfers between devices, swap(): return lax.ppermute(x, axis, [(0, 1), (1, 0)])  12.2 us
    ppermute x6, waiting for transfers between devices, shift(): return lax.ppermute(x, 'x', [(i, (i + by) % N_X) for i in range(N_X)])  8.62 us
  transfers between devices with their start and end apart: 11, of which 9 were waited for; matrix products, arithmetic and copies ran while one was open for 0% of the time, Pallas kernels for 1%

profile of v6, /device:TPU:1, one launch (start us, length us, event | category | flops | bytes accessed | tf_op | source)
XLA Modules:
  0.0 209.6 jit_solution(11282921047538303776)
XLA Ops:
  1.6 3.7 %convert_bitcast_fusion.mid = bf16[40,256,128]{2,1,0:T(8,128)(2,1)S(1)} fusion(bf16[40,384,128]{2,1,0:T(8,128)(2,1)} %param.4, bf16[384,256]{1,0:T(8,128)(2,1)S(1)} %copy-done), kind=kOutput, calls=%fused_computation | convolution fusion | flops 1007943680 | bytes 6750208 | tf_op jit(solution)/shard_map/fhw,hr->frw/dot_general | solution.py:334
  5.9 3.9 %collective-permute-start = (bf16[20,64,128]{2,1,0:T(8,128)(2,1)S(1)}, bf16[20,64,128]{2,1,0:T(8,128)(2,1)S(1)}, u32[]{:S(2)}, u32[]{:S(2)}) collective-permute-start(bf16[20,64,128]{2,1,0:T(8,128)(2,1)S(1)} %get-tuple-element.12), channel_id=1, source_target_pairs={{0,4},{4,8},{8,12},{12,0},{1,5},{5,9},{9,13},{13,1},{2,6},{6,10},{... | collective-permute-start | bytes 983048 | tf_op jit(solution)/shard_map/ppermute | solution.py:298
  9.9 3.2 %collective-permute-start.3 = (bf16[20,64,128]{2,1,0:T(8,128)(2,1)S(1)}, bf16[20,64,128]{2,1,0:T(8,128)(2,1)S(1)}, u32[]{:S(2)}, u32[]{:S(2)}) collective-permute-start(bf16[20,64,128]{2,1,0:T(8,128)(2,1)S(1)} %get-tuple-element.13), channel_id=1, source_target_pairs={{0,12},{4,0},{8,4},{12,8},{1,13},{5,1},{9,5},{13,9},{2,14},{6,2},{... | collective-permute-start | bytes 983048 | tf_op jit(solution)/shard_map/ppermute | solution.py:298
  13.1 2.5 %collective-permute-done.came = bf16[20,64,128]{2,1,0:T(8,128)(2,1)S(1)} collective-permute-done((bf16[20,64,128]{2,1,0:T(8,128)(2,1)S(1)}, bf16[20,64,128]{2,1,0:T(8,128)(2,1)S(1)}, u32[]{:S(2)}, u32[]{:S(2)}) %collective-permute-start) | collective-permute-done | bytes 327712 | tf_op jit(solution)/shard_map/ppermute | solution.py:298
  16.2 3.8 %collective-permute-start.1 = (bf16[20,64,128]{2,1,0:T(8,128)(2,1)S(1)}, bf16[20,64,128]{2,1,0:T(8,128)(2,1)S(1)}, u32[]{:S(2)}, u32[]{:S(2)}) collective-permute-start(bf16[20,64,128]{2,1,0:T(8,128)(2,1)S(1)} %shard_map.60), channel_id=1, source_target_pairs={{0,4},{4,8},{8,12},{12,0},{1,5},{5,9},{9,13},{13,1},{2,6},{6,10},{... | collective-permute-start | bytes 983048 | tf_op jit(solution)/shard_map/ppermute | solution.py:298
  20.6 4.2 %collective-permute-start.4 = (bf16[20,64,128]{2,1,0:T(8,128)(2,1)S(1)}, bf16[20,64,128]{2,1,0:T(8,128)(2,1)S(1)}, u32[]{:S(2)}, u32[]{:S(2)}) collective-permute-start(bf16[20,64,128]{2,1,0:T(8,128)(2,1)S(1)} %shard_map.63), channel_id=1, source_target_pairs={{0,12},{4,0},{8,4},{12,8},{1,13},{5,1},{9,5},{13,9},{2,14},{6,2},{... | collective-permute-start | bytes 983048 | tf_op jit(solution)/shard_map/ppermute | solution.py:298
  24.8 1.9 collective-permute-done.1.came
  27.3 2.8 %collective-permute-start.2 = (bf16[20,64,128]{2,1,0:T(8,128)(2,1)S(1)}, bf16[20,64,128]{2,1,0:T(8,128)(2,1)S(1)}, u32[]{:S(2)}, u32[]{:S(2)}) collective-permute-start(bf16[20,64,128]{2,1,0:T(8,128)(2,1)S(1)} %shard_map.61), channel_id=1, source_target_pairs={{0,4},{4,8},{8,12},{12,0},{1,5},{5,9},{9,13},{13,1},{2,6},{6,10},{... | collective-permute-start | bytes 983048 | tf_op jit(solution)/shard_map/ppermute | solution.py:298
  30.8 3.7 %collective-permute-start.5 = (bf16[20,64,128]{2,1,0:T(8,128)(2,1)S(1)}, bf16[20,64,128]{2,1,0:T(8,128)(2,1)S(1)}, u32[]{:S(2)}, u32[]{:S(2)}) collective-permute-start(bf16[20,64,128]{2,1,0:T(8,128)(2,1)S(1)} %shard_map.64), channel_id=1, source_target_pairs={{0,12},{4,0},{8,4},{12,8},{1,13},{5,1},{9,5},{13,9},{2,14},{6,2},{... | collective-permute-start | bytes 983048 | tf_op jit(solution)/shard_map/ppermute | solution.py:298
  34.5 2.1 %collective-permute-done.2.came = bf16[20,64,128]{2,1,0:T(8,128)(2,1)S(1)} collective-permute-done((bf16[20,64,128]{2,1,0:T(8,128)(2,1)S(1)}, bf16[20,64,128]{2,1,0:T(8,128)(2,1)S(1)}, u32[]{:S(2)}, u32[]{:S(2)}) %collective-permute-start.2) | collective-permute-done | bytes 327712 | tf_op jit(solution)/shard_map/ppermute | solution.py:298
  37.2 2.1 collective-permute-done.5.came
  40.0 1.3 copy.10
  41.3 18.9 %all-to-all-start = ((bf16[64,40,128]{2,1,0:T(8,128)(2,1)}), bf16[64,40,128]{2,1,0:T(8,128)(2,1)S(1)}, u32[]{:S(2)}, u32[]{:S(2)}) async-start(bf16[64,40,128]{2,1,0:T(8,128)(2,1)} %copy.10), calls=%async_computation | async-start | bytes 1310720 | tf_op jit(solution)/shard_map/all_to_all | solution.py:341
  60.3 6.9 %collective-permute-start.6 = (bf16[128,256]{1,0:T(8,128)(2,1)S(1)}, bf16[128,256]{1,0:T(8,128)(2,1)S(1)}, u32[]{:S(2)}, u32[]{:S(2)}) collective-permute-start(bf16[128,256]{1,0:T(8,128)(2,1)S(1)} %copy-done.1), channel_id=1, source_target_pairs={{0,2},{2,0},{1,3},{3,1},{4,6},{6,4},{5,7},{7,5},{8,10},{10,8},{9,1... | collective-permute-start | bytes 196616 | tf_op jit(solution)/shard_map/ppermute | solution.py:302
  67.2 9.1 %collective-permute-done.6.width_other = bf16[128,256]{1,0:T(8,128)(2,1)S(1)} collective-permute-done((bf16[128,256]{1,0:T(8,128)(2,1)S(1)}, bf16[128,256]{1,0:T(8,128)(2,1)S(1)}, u32[]{:S(2)}, u32[]{:S(2)}) %collective-permute-start.6) | collective-permute-done | bytes 65568 | tf_op jit(solution)/shard_map/ppermute | solution.py:302
  76.8 1.1 shard_map.66
  77.9 8.9 %collective-permute-start.7 = (bf16[1280,128]{1,0:T(8,128)(2,1)S(1)}, bf16[1280,128]{1,0:T(8,128)(2,1)S(1)}, u32[]{:S(2)}, u32[]{:S(2)}) collective-permute-start(bf16[1280,128]{1,0:T(8,128)(2,1)S(1)} %get-tuple-element.17), channel_id=1, source_target_pairs={{0,1},{1,0},{2,3},{3,2},{4,5},{5,4},{6,7},{7,6},{8,9},{9,8},{10,11... | collective-permute-start | bytes 983048 | tf_op jit(solution)/shard_map/ppermute | solution.py:302
  86.8 1.2 collective-permute-done.7.b
  88.1 21.5 %all_to_all.35.refs_1_ = bf16[4,1280,128]{2,1,0:T(8,128)(2,1)S(1)} all-to-all(bf16[4,1280,128]{2,1,0:T(8,128)(2,1)S(1)} %shard_map.67), channel_id=1, replica_groups=mesh['y'=8,'zl'=4,'x'=4,'zh'=2,'c'=2] {'x'}, dimensions={0} | all-to-all | bytes 2621440 | tf_op jit(solution)/shard_map/all_to_all | solution.py:354
  109.6 1.5 shard_map.68
  111.1 3.7 %collective-permute-start.8 = (f32[20,80,128]{2,1,0:T(8,128)S(1)}, f32[20,80,128]{2,1,0:T(8,128)S(1)}, u32[]{:S(2)}, u32[]{:S(2)}) collective-permute-start(f32[20,80,128]{2,1,0:T(8,128)S(1)} %get-tuple-element.19), channel_id=1, source_target_pairs={{0,1},{1,0},{2,3},{3,2},{4,5},{5,4},{6,7},{7,6},{8,9},{9,8},{10,11... | collective-permute-start | bytes 2457608 | tf_op jit(solution)/shard_map/ppermute | solution.py:302
  114.9 1.8 collective-permute-done.8
  117.1 25.5 %all_to_all.36 = f16[64,32,128]{2,1,0:T(8,128)(2,1)S(1)} all-to-all(f16[64,32,128]{2,1,0:T(8,128)(2,1)S(1)} %bitcast.37), channel_id=1, replica_groups=mesh['y'=8,'zl'=4,'x'=4,'zh'=2,'c'=2] {'zh','y','zl'}, dimensions={0} | all-to-all | bytes 1048576 | tf_op jit(solution)/shard_map/all_to_all | solution.py:293
  143.1 23.3 %all_to_all.37 = f16[64,32,128]{2,1,0:T(8,128)(2,1)S(1)} all-to-all(f16[64,32,128]{2,1,0:T(8,128)(2,1)S(1)} %broadcast_in_dim.2), channel_id=1, replica_groups=mesh['y'=8,'zl'=4,'x'=4,'zh'=2,'c'=2] {'zh','y','zl'}, dimensions={0} | all-to-all | bytes 1048576 | tf_op jit(solution)/shard_map/all_to_all | solution.py:293
  166.5 0.9 shard_map.71
  167.5 11.8 %all_to_all.38 = f16[8,88,128]{2,1,0:T(8,128)(2,1)S(1)} all-to-all(f16[8,88,128]{2,1,0:T(8,128)(2,1)S(1)} %convert_element_type.56), channel_id=1, replica_groups=mesh['y'=8,'zl'=4,'x'=4,'zh'=2,'c'=2] {'x','c'}, dimensions={0} | all-to-all | bytes 360448 | tf_op jit(solution)/shard_map/all_to_all | solution.py:293
  179.4 3.3 %shard_map.72 = f32[8,88,128]{2,1,0:T(8,128)S(1)} custom-call(f32[704,128]{1,0:T(8,128)S(1)} %bitcast_convert_fusion.4.parts, f32[160,1280]{1,0:T(8,128)S(1)} %get-tuple-element.20.gram), custom_call_target="tpu_custom_call" | custom-call | tf_op jit(solution)/shard_map/pallas_call | solution.py:282
  182.7 9.1 %all_to_all.39 = f16[8,88,128]{2,1,0:T(8,128)(2,1)S(1)} all-to-all(f16[8,88,128]{2,1,0:T(8,128)(2,1)S(1)} %convert_element_type.59), channel_id=1, replica_groups=mesh['y'=8,'zl'=4,'x'=4,'zh'=2,'c'=2] {'x','c'}, dimensions={0} | all-to-all | bytes 360448 | tf_op jit(solution)/shard_map/all_to_all | solution.py:293
  191.8 3.3 %shard_map.73 = f32[8,88,128]{2,1,0:T(8,128)S(1)} custom-call(f32[704,128]{1,0:T(8,128)S(1)} %bitcast_convert_fusion.3.parts, f32[160,1280]{1,0:T(8,128)S(1)} %get-tuple-element.20.gram), custom_call_target="tpu_custom_call" | custom-call | tf_op jit(solution)/shard_map/pallas_call | solution.py:282
  195.8 4.2 %all-to-all-start.6 = ((f16[8,88,128]{2,1,0:T(8,128)(2,1)}), f16[8,88,128]{2,1,0:T(8,128)(2,1)S(1)}, u32[]{:S(2)}, u32[]{:S(2)}) async-start(f16[8,88,128]{2,1,0:T(8,128)(2,1)} %convert_element_type.62), calls=%async_computation.6 | async-start | bytes 360448 | tf_op jit(solution)/shard_map/all_to_all | solution.py:293
  200.8 5.0 %all-to-all-done.6 = f16[8,88,128]{2,1,0:T(8,128)(2,1)S(1)} async-done(((f16[8,88,128]{2,1,0:T(8,128)(2,1)}), f16[8,88,128]{2,1,0:T(8,128)(2,1)S(1)}, u32[]{:S(2)}, u32[]{:S(2)}) %all-to-all-start.6) | async-done | bytes 180256 | tf_op jit(solution)/shard_map/all_to_all | solution.py:293
  205.8 3.8 %shard_map.74 = f32[40,64]{1,0:T(8,128)} custom-call(s32[5]{0:T(128)S(1)} %stack.23.at.refs_0_, f32[704,128]{1,0:T(8,128)S(1)} %bitcast_convert_fusion.2.parts), custom_call_target="tpu_custom_call" | custom-call | tf_op jit(solution)/shard_map/pallas_call | solution.py:282
  (36 shorter events, 8.4 us)
Async XLA Ops:
  0.6 0.9 copy-start
  5.9 9.7 %collective-permute-start = (bf16[20,64,128]{2,1,0:T(8,128)(2,1)S(1)}, bf16[20,64,128]{2,1,0:T(8,128)(2,1)S(1)}, u32[]{:S(2)}, u32[]{:S(2)}) collective-permute-start(bf16[20,64,128]{2,1,0:T(8,128)(2,1)S(1)} %get-tuple-element.12), channel_id=1, source_target_pairs={{0,4},{4,8},{8,12},{12,0},{1,5},{5,9},{9,13},{13,1},{2,6},{6,10},{... | collective-permute-start | bytes 983048 | tf_op jit(solution)/shard_map/ppermute | solution.py:298
  9.9 10.1 %collective-permute-start.3 = (bf16[20,64,128]{2,1,0:T(8,128)(2,1)S(1)}, bf16[20,64,128]{2,1,0:T(8,128)(2,1)S(1)}, u32[]{:S(2)}, u32[]{:S(2)}) collective-permute-start(bf16[20,64,128]{2,1,0:T(8,128)(2,1)S(1)} %get-tuple-element.13), channel_id=1, source_target_pairs={{0,12},{4,0},{8,4},{12,8},{1,13},{5,1},{9,5},{13,9},{2,14},{6,2},{... | collective-permute-start | bytes 983048 | tf_op jit(solution)/shard_map/ppermute | solution.py:298
  16.2 10.5 %collective-permute-start.1 = (bf16[20,64,128]{2,1,0:T(8,128)(2,1)S(1)}, bf16[20,64,128]{2,1,0:T(8,128)(2,1)S(1)}, u32[]{:S(2)}, u32[]{:S(2)}) collective-permute-start(bf16[20,64,128]{2,1,0:T(8,128)(2,1)S(1)} %shard_map.60), channel_id=1, source_target_pairs={{0,4},{4,8},{8,12},{12,0},{1,5},{5,9},{9,13},{13,1},{2,6},{6,10},{... | collective-permute-start | bytes 983048 | tf_op jit(solution)/shard_map/ppermute | solution.py:298
  20.6 9.5 %collective-permute-start.4 = (bf16[20,64,128]{2,1,0:T(8,128)(2,1)S(1)}, bf16[20,64,128]{2,1,0:T(8,128)(2,1)S(1)}, u32[]{:S(2)}, u32[]{:S(2)}) collective-permute-start(bf16[20,64,128]{2,1,0:T(8,128)(2,1)S(1)} %shard_map.63), channel_id=1, source_target_pairs={{0,12},{4,0},{8,4},{12,8},{1,13},{5,1},{9,5},{13,9},{2,14},{6,2},{... | collective-permute-start | bytes 983048 | tf_op jit(solution)/shard_map/ppermute | solution.py:298
  27.3 9.3 %collective-permute-start.2 = (bf16[20,64,128]{2,1,0:T(8,128)(2,1)S(1)}, bf16[20,64,128]{2,1,0:T(8,128)(2,1)S(1)}, u32[]{:S(2)}, u32[]{:S(2)}) collective-permute-start(bf16[20,64,128]{2,1,0:T(8,128)(2,1)S(1)} %shard_map.61), channel_id=1, source_target_pairs={{0,4},{4,8},{8,12},{12,0},{1,5},{5,9},{9,13},{13,1},{2,6},{6,10},{... | collective-permute-start | bytes 983048 | tf_op jit(solution)/shard_map/ppermute | solution.py:298
  30.8 8.6 %collective-permute-start.5 = (bf16[20,64,128]{2,1,0:T(8,128)(2,1)S(1)}, bf16[20,64,128]{2,1,0:T(8,128)(2,1)S(1)}, u32[]{:S(2)}, u32[]{:S(2)}) collective-permute-start(bf16[20,64,128]{2,1,0:T(8,128)(2,1)S(1)} %shard_map.64), channel_id=1, source_target_pairs={{0,12},{4,0},{8,4},{12,8},{1,13},{5,1},{9,5},{13,9},{2,14},{6,2},{... | collective-permute-start | bytes 983048 | tf_op jit(solution)/shard_map/ppermute | solution.py:298
  37.2 23.0 %copy-start.1 = (bf16[128,256]{1,0:T(8,128)(2,1)S(1)}, bf16[128,256]{1,0:T(8,128)(2,1)}, u32[]{:S(2)}) copy-start(bf16[128,256]{1,0:T(8,128)(2,1)} %width) | copy-start | bytes 196612
  41.3 73.5 %copy-start.2 = (f32[40,64]{1,0:T(8,128)S(1)}, f32[40,64]{1,0:T(8,128)}, u32[]{:S(2)}) copy-start(f32[40,64]{1,0:T(8,128)} %param.7) | copy-start | bytes 30724
  41.3 35.4 %all-to-all-start = ((bf16[64,40,128]{2,1,0:T(8,128)(2,1)}), bf16[64,40,128]{2,1,0:T(8,128)(2,1)S(1)}, u32[]{:S(2)}, u32[]{:S(2)}) async-start(bf16[64,40,128]{2,1,0:T(8,128)(2,1)} %copy.10), calls=%async_computation | async-start | bytes 1310720 | tf_op jit(solution)/shard_map/all_to_all | solution.py:341
  60.3 16.1 %collective-permute-start.6 = (bf16[128,256]{1,0:T(8,128)(2,1)S(1)}, bf16[128,256]{1,0:T(8,128)(2,1)S(1)}, u32[]{:S(2)}, u32[]{:S(2)}) collective-permute-start(bf16[128,256]{1,0:T(8,128)(2,1)S(1)} %copy-done.1), channel_id=1, source_target_pairs={{0,2},{2,0},{1,3},{3,1},{4,6},{6,4},{5,7},{7,5},{8,10},{10,8},{9,1... | collective-permute-start | bytes 196616 | tf_op jit(solution)/shard_map/ppermute | solution.py:302
  77.9 10.2 %collective-permute-start.7 = (bf16[1280,128]{1,0:T(8,128)(2,1)S(1)}, bf16[1280,128]{1,0:T(8,128)(2,1)S(1)}, u32[]{:S(2)}, u32[]{:S(2)}) collective-permute-start(bf16[1280,128]{1,0:T(8,128)(2,1)S(1)} %get-tuple-element.17), channel_id=1, source_target_pairs={{0,1},{1,0},{2,3},{3,2},{4,5},{5,4},{6,7},{7,6},{8,9},{9,8},{10,11... | collective-permute-start | bytes 983048 | tf_op jit(solution)/shard_map/ppermute | solution.py:302
  111.1 5.7 %collective-permute-start.8 = (f32[20,80,128]{2,1,0:T(8,128)S(1)}, f32[20,80,128]{2,1,0:T(8,128)S(1)}, u32[]{:S(2)}, u32[]{:S(2)}) collective-permute-start(f32[20,80,128]{2,1,0:T(8,128)S(1)} %get-tuple-element.19), channel_id=1, source_target_pairs={{0,1},{1,0},{2,3},{3,2},{4,5},{5,4},{6,7},{7,6},{8,9},{9,8},{10,11... | collective-permute-start | bytes 2457608 | tf_op jit(solution)/shard_map/ppermute | solution.py:302
  195.8 10.0 %all-to-all-start.6 = ((f16[8,88,128]{2,1,0:T(8,128)(2,1)}), f16[8,88,128]{2,1,0:T(8,128)(2,1)S(1)}, u32[]{:S(2)}, u32[]{:S(2)}) async-start(f16[8,88,128]{2,1,0:T(8,128)(2,1)} %convert_element_type.62), calls=%async_computation.6 | async-start | bytes 360448 | tf_op jit(solution)/shard_map/all_to_all | solution.py:293
